TPU v7x, 256 devices: a whole 4x4x8 slice. The times are simulated.
256 devices in a mesh: ta: 4 (over y), gz: 8 (over x, core), xy: 8 (over z).
Axes of the slice: x: 4, y: 4, z: 8, core: 2. Of those that a mesh axis runs over, the one named last changes fastest.
Arguments:
- right_side: float32 [8, 16, 16, 4, 1152], P('ta', 'gz', 'xy'), may hold values from -6 to 6
- link_blocks: bfloat16 [5, 8, 16, 16, 4, 96, 96], P(None, 'ta', 'gz', 'xy'), may hold values from -0.3125 to 0.3125
Outputs:
- solution: float32 [8, 16, 16, 4, 1152], P('ta', 'gz', 'xy')
- residual: float32 [8, 16, 16, 4, 1152], P('ta', 'gz', 'xy')
All inputs are finite; a program needn't handle non-finite values.
Results may differ from a plain program's by a relative error of at most 0.0069.
Values may be sent and summed in bfloat16 or wider, within the bound.
No kernel may reach another device: no remote copies, remote signals or barrier semaphores. Data moves between devices by JAX's collectives and lax.ppermute only.
A program may use at most 64 MiB of HBM per device.

v0:
```python
import functools

import jax
import jax.numpy as jnp
from jax import lax
from jax.experimental import pallas as pl
from jax.experimental.pallas import tpu as pltpu
from jax.sharding import PartitionSpec as P

COMP = 96
RHS = 12
ROWS = 16
ITERS = 4
BASIS = ITERS + 1
mass_term = 6.0
SHIFT = 1.6
EXTENT = (2, 2, 2, 4)
SITES = 32
FACE = 16
GROUPS = 8
ENTRIES = [(i, j) for j in range(BASIS) for i in range(j + 1)]
LANES = len(ENTRIES) * ROWS
FIRST_GROUP = 8
SECOND_GROUP = 32
AXES = ("ta", "gz", "xy")
KEEP_SQUARE = 1e-4
KEEP_VECTOR = 0.1

NT = (((1,), (1,)), ((), ()))
NN = (((1,), (0,)), ((), ()))
TN = (((0,), (0,)), ((), ()))

CELLS = [(t, z, x, y) for t in range(2) for z in range(2) for x in range(2) for y in range(4)]


def place(cell):
    t, z, x, y = cell
    return ((t * 2 + z) * 2 + x) * 4 + y


def moved(cell, direction, by):
    cell = list(cell)
    cell[direction] = (cell[direction] + by) % EXTENT[direction]
    return tuple(cell)


def on_face(cell, direction):
    rest = [c for d, c in enumerate(cell) if d != direction]
    return (rest[0] * 2 + rest[1]) * 4 + rest[2]


def dot(left, right, dims):
    return lax.dot_general(left, right, dims, preferred_element_type=jnp.float32)


def begin_kernel(right_ref, wide_ref, narrow_ref, *firsts):
    wide_ref[...] = jnp.zeros(wide_ref.shape, jnp.float32)
    for group in range(GROUPS):
        row = right_ref[group]
        for source in range(RHS):
            piece = row[:, source * COMP : (source + 1) * COMP]
            for y in range(4):
                wide_ref[group * 4 + y, source : source + 1] = piece[y : y + 1]
    for site in range(SITES):
        narrow_ref[site] = wide_ref[site].astype(jnp.bfloat16)
    send_firsts(narrow_ref, firsts)


def send_firsts(narrow_ref, firsts):
    for direction in range(3):
        for cell in CELLS:
            if cell[direction] == 0:
                firsts[direction][on_face(cell, direction)] = narrow_ref[place(cell)]


def send_products(narrow_ref, links_ref, *products):
    for direction in range(3):
        for cell in CELLS:
            if cell[direction] == 1:
                site = place(cell)
                product = dot(narrow_ref[site], links_ref[(direction + 1) * SITES + site], NN)
                products[direction][on_face(cell, direction)] = product.astype(jnp.bfloat16)


def gram_rows(wides, last):
    return [sum(wides[i][site] * wides[last][site] for site in range(SITES)) for i in range(last + 1)]


def as_rows(wide_ref, row_ref):
    for group in range(GROUPS):
        sites = [wide_ref[group * 4 + y] for y in range(4)]
        pieces = [
            jnp.concatenate([site[source : source + 1] for site in sites], 0) for source in range(RHS)
        ]
        row_ref[group] = jnp.concatenate(pieces, 1)


def inner_kernel(step, narrow_ref, links_ref, *refs):
    wides, (part_ref, gram_ref), row_refs = refs[: step + 1], refs[step + 1 : step + 3], refs[step + 3 :]
    for cell in CELLS:
        site = place(cell)
        total = dot(narrow_ref[site], links_ref[site], NT)
        for direction in range(4):
            block = (direction + 1) * SITES
            if direction == 3 or cell[direction] == 0:
                total -= dot(narrow_ref[place(moved(cell, direction, 1))], links_ref[block + site], NT)
            if direction == 3 or cell[direction] == 1:
                behind = place(moved(cell, direction, -1))
                total -= dot(narrow_ref[behind], links_ref[block + behind], NN)
        if step:
            total -= SHIFT * wides[step - 1][site]
        part_ref[site] = total
    for i, row in enumerate(gram_rows(wides, step)):
        gram_ref[i] = row
    for row_ref in row_refs:
        as_rows(wides[step], row_ref)


def joined(cell, part_ref, links_ref, ahead, behind):
    site = place(cell)
    total = part_ref[site]
    for direction in range(3):
        spot = on_face(cell, direction)
        if cell[direction] == 1:
            total -= dot(ahead[direction][spot], links_ref[(direction + 1) * SITES + site], NT)
        else:
            total -= behind[direction][spot].astype(jnp.float32)
    return total


def outer_kernel(part_ref, links_ref, *refs):
    ahead, behind, (wide_ref, narrow_ref), faces = refs[0:3], refs[3:6], refs[6:8], refs[8:14]
    for cell in CELLS:
        total = joined(cell, part_ref, links_ref, ahead, behind)
        wide_ref[place(cell)] = total
        narrow_ref[place(cell)] = total.astype(jnp.bfloat16)
    send_firsts(narrow_ref, faces[0:3])
    send_products(narrow_ref, links_ref, *faces[3:6])


def last_kernel(part_ref, links_ref, *refs):
    ahead, behind, wides, grams = refs[0:3], refs[3:6], refs[6:10], refs[10:14]
    row_ref, sums_ref, wide_ref = refs[14:17]
    for cell in CELLS:
        wide_ref[place(cell)] = joined(cell, part_ref, links_ref, ahead, behind)
    rows = [gram[i] for gram in grams for i in range(gram.shape[0])]
    rows += gram_rows(tuple(wides) + (wide_ref,), ITERS)
    stacked = jnp.concatenate(rows, 0)
    sums_ref[...] = lax.dot_general(
        jnp.ones((FIRST_GROUP, COMP), jnp.float32), stacked, NT,
        precision=lax.Precision.HIGHEST, preferred_element_type=jnp.float32,
    )
    as_rows(wide_ref, row_ref)


def apply_coefficients(z):
    q = [mass_term * v for v in z] + [jnp.zeros_like(z[0])]
    for k, v in enumerate(z):
        q[k + 1] = q[k + 1] + v
        if k:
            q[k - 1] = q[k - 1] + SHIFT * v
    return q


def combine(left, right):
    terms = [a * b for a, b in zip(left, right)]
    return sum(terms[1:], terms[0])


def finish_kernel(gathered_ref, w0, w1, w2, w3, w4, solution_ref, residual_ref, sound_ref):
    wides = (w0, w1, w2, w3, w4)
    summed = lax.dot_general(
        gathered_ref[...], jnp.ones((SECOND_GROUP, 128), jnp.float32), TN,
        precision=lax.Precision.HIGHEST, preferred_element_type=jnp.float32,
    )
    gram = {}
    for at, (i, j) in enumerate(ENTRIES):
        gram[i, j] = gram[j, i] = summed[at * ROWS : (at + 1) * ROWS]
    size = {key: jnp.abs(value) for key, value in gram.items()}

    def times_gram(v):
        return [combine(v, [gram[i, j] for j in range(len(v))]) for i in range(BASIS)]

    def worst(v, table):
        v = [jnp.abs(a) for a in v]
        return combine(v, [combine(v, [table[i, j] for j in range(len(v))]) for i in range(len(v))])

    zero = jnp.zeros((ROWS, 128), jnp.float32)
    rho = [zero + 1.0] + [zero] * ITERS
    out = [zero] * ITERS
    saved = []
    margin = zero + 1.0
    for step in range(ITERS):
        z = rho[: step + 1]
        q = apply_coefficients(z)
        h = times_gram(q)
        for q_j, h_j, z_j in saved:
            beta = combine(q_j, h)
            q = [a - beta * b for a, b in zip(q, list(q_j) + [zero] * len(q))]
            h = [a - beta * b for a, b in zip(h, h_j)]
            z = [a - beta * b for a, b in zip(z, list(z_j) + [zero] * len(z))]
        square = combine(q, h)
        margin = jnp.minimum(margin, square - KEEP_SQUARE * worst(q, size))
        scale = lax.rsqrt(jnp.maximum(square, 0.0) + 1e-06)
        alpha = combine(rho, h) * scale
        q = [a * scale for a in q]
        h = [a * scale for a in h]
        z = [a * scale for a in z]
        saved.append((q, h, z))
        out = [a + alpha * b for a, b in zip(out, list(z) + [zero] * ITERS)]
        rho = [a - alpha * b for a, b in zip(rho, list(q) + [zero] * BASIS)]
    for v in (rho, out):
        length = combine(v, times_gram(v))
        margin = jnp.minimum(margin, length - KEEP_VECTOR * combine([a * a for a in v], [gram[i, i] for i in range(len(v))]))
    sound_ref[0, 0] = jnp.where(jnp.min(margin) >= 0.0, 1, 0)

    lane = lax.broadcasted_iota(jnp.int32, (ROWS, 128), 1)
    packed = zero
    for at, v in enumerate(out + rho):
        packed = jnp.where(lane == at, v, packed)
    owner = lax.broadcasted_iota(jnp.int32, (ROWS, RHS * COMP), 1)
    low = lax.broadcasted_iota(jnp.int32, (ROWS, RHS * COMP), 0) * COMP
    spread = jnp.where((owner >= low) & (owner < low + COMP), 1.0, 0.0)
    factors = lax.dot_general(
        packed[:, 0:ROWS], spread, TN, precision=lax.Precision.HIGHEST, preferred_element_type=jnp.float32
    )
    for group in range(GROUPS):
        held = [w[group] for w in wides]
        solution_ref[group] = combine([factors[i : i + 1] for i in range(ITERS)], held)
        residual_ref[group] = combine([factors[ITERS + i : ITERS + i + 1] for i in range(BASIS)], held)


def shape(dims, dtype=jnp.float32):
    return jax.ShapeDtypeStruct(dims, dtype)


FACES = [shape((FACE, ROWS, COMP), jnp.bfloat16)] * 3
ROW = shape((GROUPS, 4, RHS * COMP))
WIDE = shape((SITES, ROWS, COMP))
NARROW = shape((SITES, ROWS, COMP), jnp.bfloat16)


def call(kernel, name, out_shape, operands, scratch=()):
    whole = pl.BlockSpec(memory_space=pltpu.VMEM)
    scalar = pl.BlockSpec(memory_space=pltpu.SMEM)
    return pl.pallas_call(
        kernel,
        name=name,
        out_shape=out_shape,
        in_specs=[whole] * len(operands),
        out_specs=[scalar if o.shape == (1, 1) else whole for o in out_shape],
        scratch_shapes=scratch,
        compiler_params=pltpu.CompilerParams(vmem_limit_bytes=24 * 2**20),
    )(*operands)


def shifted(shard, axis, by):
    length = lax.axis_size(axis)
    return lax.ppermute(shard, axis, [(i, (i + by) % length) for i in range(length)])


def stepwise(right_side, link_blocks):
    shaped = (2, 2, 2, 4, RHS, COMP)
    forward_form, adjoint_form = "tzxyab,tzxyrb->tzxyra", "tzxyba,tzxyrb->tzxyra"

    def multiply(blocks, cells, pattern):
        return jnp.einsum(pattern, blocks, cells, preferred_element_type=jnp.float32)

    def inner_product(left, right):
        return lax.psum(jnp.sum(left * right, axis=(0, 1, 2, 3, 5)), AXES)[:, None]

    out, residual = jnp.zeros(shaped, jnp.float32), right_side.reshape(shaped)
    saved = []
    for step in range(ITERS):
        search = residual
        narrow = search.astype(jnp.bfloat16)
        image = mass_term * search + multiply(link_blocks[0], narrow, forward_form)
        for direction in range(4):
            blocks = link_blocks[direction + 1]
            product = multiply(blocks, narrow, adjoint_form)
            if direction == 3:
                ahead, behind = jnp.roll(narrow, -1, 3), jnp.roll(product, 1, 3)
            else:
                axis = AXES[direction]
                first = lax.slice_in_dim(narrow, 0, 1, axis=direction)
                last = lax.slice_in_dim(product, 1, 2, axis=direction)
                rest = lax.slice_in_dim(narrow, 1, 2, axis=direction)
                front = lax.slice_in_dim(product, 0, 1, axis=direction)
                ahead = jnp.concatenate([rest, shifted(first, axis, -1)], direction)
                behind = jnp.concatenate([shifted(last, axis, 1), front], direction)
            image = image - multiply(blocks, ahead, forward_form) - behind
        for q_j, z_j in saved:
            beta = inner_product(q_j, image)
            image = image - q_j * beta
            search = search - z_j * beta
        length = jnp.sqrt(inner_product(image, image) + 1e-06)
        alpha = inner_product(image, residual) / length
        image, search = image / length, search / length
        out = out + search * alpha
        residual = residual - image * alpha
        saved.append((image, search))
    return out.reshape(right_side.shape), residual.reshape(right_side.shape)


def local(right_side, link_blocks):
    links = link_blocks.reshape(5 * SITES, COMP, COMP)
    row = right_side.reshape(GROUPS, 4, RHS * COMP)
    wide, narrow, *firsts = call(begin_kernel, "begin", [WIDE, NARROW] + FACES, (row,))
    products = call(send_products, "products", FACES, (narrow, links))
    wides, grams, rows = [wide], [], [row]
    for step in range(ITERS):
        ahead = [shifted(firsts[d], AXES[d], -1) for d in range(3)]
        behind = [shifted(products[d], AXES[d], 1) for d in range(3)]
        part, gram, *made = call(
            functools.partial(inner_kernel, step), f"inner{step}",
            [WIDE, shape((step + 1, ROWS, COMP))] + [ROW] * (step > 0), (narrow, links, *wides),
        )
        grams.append(gram)
        rows += made
        if step < ITERS - 1:
            wide, narrow, *faces = call(
                outer_kernel, f"outer{step}", [WIDE, NARROW] + FACES * 2, (part, links, *ahead, *behind)
            )
            firsts, products = faces[0:3], faces[3:6]
            wides.append(wide)
        else:
            made, sums = call(
                last_kernel, "last", [ROW, shape((FIRST_GROUP, LANES))],
                (part, links, *ahead, *behind, *wides, *grams),
                [pltpu.VMEM((SITES, ROWS, COMP), jnp.float32)],
            )
            rows.append(made)
    sums = jnp.sum(lax.all_to_all(sums, "gz", 0, 0), 0)
    sums = lax.all_to_all(jnp.broadcast_to(sums, (SECOND_GROUP, LANES)), ("ta", "xy"), 0, 0)
    out, residual, sound = call(
        finish_kernel, "finish", [ROW, ROW, shape((1, 1), jnp.int32)], (sums, *rows)
    )
    return lax.cond(
        sound[0, 0] > 0,
        lambda: (out.reshape(right_side.shape), residual.reshape(right_side.shape)),
        lambda: stepwise(right_side, link_blocks),
    )


def solution(mesh):
    return jax.shard_map(
        local,
        mesh=mesh,
        in_specs=(P("ta", "gz", "xy", None, None), P(None, "ta", "gz", "xy", None, None, None)),
        out_specs=(P("ta", "gz", "xy", None, None), P("ta", "gz", "xy", None, None)),
        check_vma=False,
    )
```

profile of v0, /device:TPU:1, one launch (start us, length us, event | category | flops | bytes accessed | tf_op | source)
XLA Modules:
  0.0 86.0 jit_solution(8183871799397120355)
XLA Ops:
  0.6 1.5 %begin.1 = (f32[32,16,96]{2,1,0:T(8,128)S(1)}, bf16[32,16,96]{2,1,0:T(8,128)(2,1)S(1)}, bf16[16,16,96]{2,1,0:T(8,128)(2,1)S(1)}, bf16[16,16,96]{2,1,0:T(8,128)(2,1)S(1)}, bf16[16,16,96]{2,1,0:T(8,128)(2,1)S(1)}) custom-call(f32[8,4,1152]{2,1,0:T(4,128)} %bitcast.125), custom_call_target="tpu_custom_call" | custom-call | tf_op jit(solution)/shard_map/begin/pallas_call | solution.py:246
  2.2 3.6 %collective-permute-start.24 = (bf16[16,16,96]{2,1,0:T(8,128)(2,1)S(1)}, bf16[16,16,96]{2,1,0:T(8,128)(2,1)S(1)}, u32[]{:S(2)}, u32[]{:S(2)}) collective-permute-start(bf16[16,16,96]{2,1,0:T(8,128)(2,1)S(1)} %get-tuple-element.65), channel_id=1, source_target_pairs={{0,192},{64,0},{128,64},{192,128},{1,193},{65,1},{129,65},{193,129... | collective-permute-start | bytes 147464 | tf_op jit(solution)/shard_map/ppermute | solution.py:259
  6.8 5.6 %collective-permute-start.26 = (bf16[16,16,96]{2,1,0:T(8,128)(2,1)S(1)}, bf16[16,16,96]{2,1,0:T(8,128)(2,1)S(1)}, u32[]{:S(2)}, u32[]{:S(2)}) collective-permute-start(bf16[16,16,96]{2,1,0:T(8,128)(2,1)S(1)} %get-tuple-element.67), channel_id=1, source_target_pairs={{0,7},{1,0},{2,1},{3,2},{4,3},{5,4},{6,5},{7,6},{8,15},{9,8},{10,9... | collective-permute-start | bytes 147464 | tf_op jit(solution)/shard_map/ppermute | solution.py:259
  12.3 2.5 %products.1 = (bf16[16,16,96]{2,1,0:T(8,128)(2,1)S(1)}, bf16[16,16,96]{2,1,0:T(8,128)(2,1)S(1)}, bf16[16,16,96]{2,1,0:T(8,128)(2,1)S(1)}) custom-call(bf16[32,16,96]{2,1,0:T(8,128)(2,1)S(1)} %get-tuple-element.62.narrow_ref, bf16[160,96,96]{2,1,0:T(8,128)(2,1)} %bitcast.116), custom_call_target="tpu_custom_call" | custom-call | tf_op jit(solution)/shard_map/products/pallas_call | solution.py:246
  14.9 1.4 %collective-permute-start.28 = (bf16[16,16,96]{2,1,0:T(8,128)(2,1)S(1)}, bf16[16,16,96]{2,1,0:T(8,128)(2,1)S(1)}, u32[]{:S(2)}, u32[]{:S(2)}) collective-permute-start(bf16[16,16,96]{2,1,0:T(8,128)(2,1)S(1)} %get-tuple-element.69), channel_id=1, source_target_pairs={{0,8},{8,16},{16,24},{24,32},{32,40},{40,48},{48,56},{56,0},{1,9},... | collective-permute-start | bytes 147464 | tf_op jit(solution)/shard_map/ppermute | solution.py:259
  16.3 2.1 %inner0.1 = (f32[32,16,96]{2,1,0:T(8,128)S(1)}, f32[1,16,96]{2,1,0:T(8,128)S(1)}) custom-call(bf16[32,16,96]{2,1,0:T(8,128)(2,1)S(1)} %get-tuple-element.62.narrow_ref, bf16[160,96,96]{2,1,0:T(8,128)(2,1)S(1)} %bitcast.117, f32[32,16,96]{2,1,0:T(8,128)S(1)} %get-tuple-element.63.refs_0_.refs_6_), custom_call_target="tpu_custom_call" | custom-call | tf_op jit(solution)/shard_map/inner0/pallas_call | solution.py:246
  19.3 1.7 %collective-permute-done.29.refs_5_ = bf16[16,16,96]{2,1,0:T(8,128)(2,1)S(1)} collective-permute-done((bf16[16,16,96]{2,1,0:T(8,128)(2,1)S(1)}, bf16[16,16,96]{2,1,0:T(8,128)(2,1)S(1)}, u32[]{:S(2)}, u32[]{:S(2)}) %collective-permute-start.29) | collective-permute-done | bytes 49184 | tf_op jit(solution)/shard_map/ppermute | solution.py:259
  21.0 1.1 %outer0.1 = (f32[32,16,96]{2,1,0:T(8,128)S(1)}, bf16[32,16,96]{2,1,0:T(8,128)(2,1)S(1)}, bf16[16,16,96]{2,1,0:T(8,128)(2,1)S(1)}, bf16[16,16,96]{2,1,0:T(8,128)(...) custom-call(f32[32,16,96]{2,1,0:T(8,128)S(1)} %get-tuple-element.64., ...), custom_call_target="tpu_custom_call" | custom-call | tf_op jit(solution)/shard_map/outer0/pallas_call | solution.py:246
  22.0 3.0 %collective-permute-start.30 = (bf16[16,16,96]{2,1,0:T(8,128)(2,1)S(1)}, bf16[16,16,96]{2,1,0:T(8,128)(2,1)S(1)}, u32[]{:S(2)}, u32[]{:S(2)}) collective-permute-start(bf16[16,16,96]{2,1,0:T(8,128)(2,1)S(1)} %get-tuple-element.74), channel_id=1, source_target_pairs={{0,192},{64,0},{128,64},{192,128},{1,193},{65,1},{129,65},{193,129... | collective-permute-start | bytes 147464 | tf_op jit(solution)/shard_map/ppermute | solution.py:259
  25.0 2.0 %collective-permute-start.31 = (bf16[16,16,96]{2,1,0:T(8,128)(2,1)S(1)}, bf16[16,16,96]{2,1,0:T(8,128)(2,1)S(1)}, u32[]{:S(2)}, u32[]{:S(2)}) collective-permute-start(bf16[16,16,96]{2,1,0:T(8,128)(2,1)S(1)} %get-tuple-element.75), channel_id=1, source_target_pairs={{0,56},{8,0},{16,8},{24,16},{32,24},{40,32},{48,40},{56,48},{1,57}... | collective-permute-start | bytes 147464 | tf_op jit(solution)/shard_map/ppermute | solution.py:259
  27.3 1.2 %collective-permute-start.35 = (bf16[16,16,96]{2,1,0:T(8,128)(2,1)S(1)}, bf16[16,16,96]{2,1,0:T(8,128)(2,1)S(1)}, u32[]{:S(2)}, u32[]{:S(2)}) collective-permute-start(bf16[16,16,96]{2,1,0:T(8,128)(2,1)S(1)} %get-tuple-element.79), channel_id=1, source_target_pairs={{0,1},{1,2},{2,3},{3,4},{4,5},{5,6},{6,7},{7,0},{8,9},{9,10},{10,1... | collective-permute-start | bytes 147464 | tf_op jit(solution)/shard_map/ppermute | solution.py:259
  28.5 2.1 %inner1.1 = (f32[32,16,96]{2,1,0:T(8,128)S(1)}, f32[2,16,96]{2,1,0:T(8,128)S(1)}, f32[8,4,1152]{2,1,0:T(4,128)S(1)}) custom-call(bf16[32,16,96]{2,1,0:T(8,128)(2,1)S(1)} %get-tuple-element.71.narrow_ref, bf16[160,96,96]{2,1,0:T(8,128)(2,1)S(1)} %bitcast.119, f32[32,16,96]{2,1,0:T(8,128)S(1)} %get-tuple-element.63.refs_0_.refs_6_, ...), custom_call_target="tpu_custom_call" | custom-call | tf_op jit(solution)/shard_map/inner1/pallas_call | solution.py:246
  32.7 3.0 %collective-permute-start.36 = (bf16[16,16,96]{2,1,0:T(8,128)(2,1)S(1)}, bf16[16,16,96]{2,1,0:T(8,128)(2,1)S(1)}, u32[]{:S(2)}, u32[]{:S(2)}) collective-permute-start(bf16[16,16,96]{2,1,0:T(8,128)(2,1)S(1)} %get-tuple-element.83), channel_id=1, source_target_pairs={{0,192},{64,0},{128,64},{192,128},{1,193},{65,1},{129,65},{193,129... | collective-permute-start | bytes 147464 | tf_op jit(solution)/shard_map/ppermute | solution.py:259
  35.7 3.5 %collective-permute-start.37 = (bf16[16,16,96]{2,1,0:T(8,128)(2,1)S(1)}, bf16[16,16,96]{2,1,0:T(8,128)(2,1)S(1)}, u32[]{:S(2)}, u32[]{:S(2)}) collective-permute-start(bf16[16,16,96]{2,1,0:T(8,128)(2,1)S(1)} %get-tuple-element.84), channel_id=1, source_target_pairs={{0,56},{8,0},{16,8},{24,16},{32,24},{40,32},{48,40},{56,48},{1,57}... | collective-permute-start | bytes 147464 | tf_op jit(solution)/shard_map/ppermute | solution.py:259
  39.2 1.5 %collective-permute-start.41 = (bf16[16,16,96]{2,1,0:T(8,128)(2,1)S(1)}, bf16[16,16,96]{2,1,0:T(8,128)(2,1)S(1)}, u32[]{:S(2)}, u32[]{:S(2)}) collective-permute-start(bf16[16,16,96]{2,1,0:T(8,128)(2,1)S(1)} %get-tuple-element.88), channel_id=1, source_target_pairs={{0,1},{1,2},{2,3},{3,4},{4,5},{5,6},{6,7},{7,0},{8,9},{9,10},{10,1... | collective-permute-start | bytes 147464 | tf_op jit(solution)/shard_map/ppermute | solution.py:259
  40.8 2.1 %inner2.1 = (f32[32,16,96]{2,1,0:T(8,128)S(1)}, f32[3,16,96]{2,1,0:T(8,128)S(1)}, f32[8,4,1152]{2,1,0:T(4,128)S(1)}) custom-call(bf16[32,16,96]{2,1,0:T(8,128)(2,1)S(1)} %get-tuple-element.80.narrow_ref, bf16[160,96,96]{2,1,0:T(8,128)(2,1)S(1)} %bitcast.121, f32[32,16,96]{2,1,0:T(8,128)S(1)} %get-tuple-element.63.refs_0_.refs_6_, ...), custom_call_target="tpu_custom_call" | custom-call | tf_op jit(solution)/shard_map/inner2/pallas_call | solution.py:246
  44.7 2.7 %collective-permute-start.42 = (bf16[16,16,96]{2,1,0:T(8,128)(2,1)S(1)}, bf16[16,16,96]{2,1,0:T(8,128)(2,1)S(1)}, u32[]{:S(2)}, u32[]{:S(2)}) collective-permute-start(bf16[16,16,96]{2,1,0:T(8,128)(2,1)S(1)} %get-tuple-element.92), channel_id=1, source_target_pairs={{0,192},{64,0},{128,64},{192,128},{1,193},{65,1},{129,65},{193,129... | collective-permute-start | bytes 147464 | tf_op jit(solution)/shard_map/ppermute | solution.py:259
  47.4 4.1 %collective-permute-start.43 = (bf16[16,16,96]{2,1,0:T(8,128)(2,1)S(1)}, bf16[16,16,96]{2,1,0:T(8,128)(2,1)S(1)}, u32[]{:S(2)}, u32[]{:S(2)}) collective-permute-start(bf16[16,16,96]{2,1,0:T(8,128)(2,1)S(1)} %get-tuple-element.93), channel_id=1, source_target_pairs={{0,56},{8,0},{16,8},{24,16},{32,24},{40,32},{48,40},{56,48},{1,57}... | collective-permute-start | bytes 147464 | tf_op jit(solution)/shard_map/ppermute | solution.py:259
  51.5 1.5 %collective-permute-start.47 = (bf16[16,16,96]{2,1,0:T(8,128)(2,1)S(1)}, bf16[16,16,96]{2,1,0:T(8,128)(2,1)S(1)}, u32[]{:S(2)}, u32[]{:S(2)}) collective-permute-start(bf16[16,16,96]{2,1,0:T(8,128)(2,1)S(1)} %get-tuple-element.97), channel_id=1, source_target_pairs={{0,1},{1,2},{2,3},{3,4},{4,5},{5,6},{6,7},{7,0},{8,9},{9,10},{10,1... | collective-permute-start | bytes 147464 | tf_op jit(solution)/shard_map/ppermute | solution.py:259
  53.0 2.2 %inner3.1 = (f32[32,16,96]{2,1,0:T(8,128)S(1)}, f32[4,16,96]{2,1,0:T(8,128)S(1)}, f32[8,4,1152]{2,1,0:T(4,128)S(1)}) custom-call(bf16[32,16,96]{2,1,0:T(8,128)(2,1)S(1)} %get-tuple-element.89.narrow_ref, bf16[160,96,96]{2,1,0:T(8,128)(2,1)S(1)} %bitcast.123, f32[32,16,96]{2,1,0:T(8,128)S(1)} %get-tuple-element.63.refs_0_.refs_6_, ...), custom_call_target="tpu_custom_call" | custom-call | tf_op jit(solution)/shard_map/inner3/pallas_call | solution.py:246
  56.9 10.9 %all_to_all.17 = f32[8,1,240]{2,1,0:T(1,128)S(1)} all-to-all(f32[8,1,240]{2,1,0:T(1,128)S(1)} %copy.8), channel_id=1, replica_groups=mesh['ta'=4,'gz'=8,'xy'=8] {'gz'}, dimensions={0} | all-to-all | bytes 15360 | tf_op jit(solution)/shard_map/all_to_all | solution.py:333
  68.5 6.0 %all-to-all-start.1 = ((f32[32,1,240]{2,1,0:T(1,128)}), f32[32,1,240]{2,1,0:T(1,128)S(1)}, u32[]{:S(2)}, u32[]{:S(2)}) async-start(f32[32,1,240]{2,1,0:T(1,128)} %broadcast_in_dim.2), calls=%async_computation.1 | async-start | bytes 65536 | tf_op jit(solution)/shard_map/all_to_all | solution.py:334
  74.5 8.8 %all-to-all-done.1 = f32[32,1,240]{2,1,0:T(1,128)S(1)} async-done(((f32[32,1,240]{2,1,0:T(1,128)}), f32[32,1,240]{2,1,0:T(1,128)S(1)}, u32[]{:S(2)}, u32[]{:S(2)}) %all-to-all-start.1) | async-done | bytes 30752 | tf_op jit(solution)/shard_map/all_to_all | solution.py:334
  83.2 1.7 %finish.1 = (f32[8,4,1152]{2,1,0:T(4,128)}, f32[8,4,1152]{2,1,0:T(4,128)}, s32[1,1]{1,0:T(1,128)}) custom-call(f32[32,240]{1,0:T(8,128)S(1)} %bitcast.114, f32[8,4,1152]{2,1,0:T(4,128)S(1)} %bitcast.126, f32[8,4,1152]{2,1,0:T(4,128)S(1)} %get-tuple-element.103.w1, f32[8,4,1152]{2,1,0:T(4,128)S(1)} %get-tuple-element.104.w2, ...), custom_call_target="tpu_custom_call" | custom-call | tf_op jit(solution)/shard_map/finish/pallas_call | solution.py:246
  (47 shorter events, 8.6 us)
Async XLA Ops:
  2.2 14.2 %collective-permute-start.24 = (bf16[16,16,96]{2,1,0:T(8,128)(2,1)S(1)}, bf16[16,16,96]{2,1,0:T(8,128)(2,1)S(1)}, u32[]{:S(2)}, u32[]{:S(2)}) collective-permute-start(bf16[16,16,96]{2,1,0:T(8,128)(2,1)S(1)} %get-tuple-element.65), channel_id=1, source_target_pairs={{0,192},{64,0},{128,64},{192,128},{1,193},{65,1},{129,65},{193,129... | collective-permute-start | bytes 147464 | tf_op jit(solution)/shard_map/ppermute | solution.py:259
  5.8 12.7 %collective-permute-start.25 = (bf16[16,16,96]{2,1,0:T(8,128)(2,1)S(1)}, bf16[16,16,96]{2,1,0:T(8,128)(2,1)S(1)}, u32[]{:S(2)}, u32[]{:S(2)}) collective-permute-start(bf16[16,16,96]{2,1,0:T(8,128)(2,1)S(1)} %get-tuple-element.66), channel_id=1, source_target_pairs={{0,56},{8,0},{16,8},{24,16},{32,24},{40,32},{48,40},{56,48},{1,57}... | collective-permute-start | bytes 147464 | tf_op jit(solution)/shard_map/ppermute | solution.py:259
  6.8 11.7 %collective-permute-start.26 = (bf16[16,16,96]{2,1,0:T(8,128)(2,1)S(1)}, bf16[16,16,96]{2,1,0:T(8,128)(2,1)S(1)}, u32[]{:S(2)}, u32[]{:S(2)}) collective-permute-start(bf16[16,16,96]{2,1,0:T(8,128)(2,1)S(1)} %get-tuple-element.67), channel_id=1, source_target_pairs={{0,7},{1,0},{2,1},{3,2},{4,3},{5,4},{6,5},{7,6},{8,15},{9,8},{10,9... | collective-permute-start | bytes 147464 | tf_op jit(solution)/shard_map/ppermute | solution.py:259
  14.9 4.4 %collective-permute-start.27 = (bf16[16,16,96]{2,1,0:T(8,128)(2,1)S(1)}, bf16[16,16,96]{2,1,0:T(8,128)(2,1)S(1)}, u32[]{:S(2)}, u32[]{:S(2)}) collective-permute-start(bf16[16,16,96]{2,1,0:T(8,128)(2,1)S(1)} %get-tuple-element.68), channel_id=1, source_target_pairs={{0,64},{64,128},{128,192},{192,0},{1,65},{65,129},{129,193},{193,1... | collective-permute-start | bytes 147464 | tf_op jit(solution)/shard_map/ppermute | solution.py:259
  14.9 4.3 %collective-permute-start.28 = (bf16[16,16,96]{2,1,0:T(8,128)(2,1)S(1)}, bf16[16,16,96]{2,1,0:T(8,128)(2,1)S(1)}, u32[]{:S(2)}, u32[]{:S(2)}) collective-permute-start(bf16[16,16,96]{2,1,0:T(8,128)(2,1)S(1)} %get-tuple-element.69), channel_id=1, source_target_pairs={{0,8},{8,16},{16,24},{24,32},{32,40},{40,48},{48,56},{56,0},{1,9},... | collective-permute-start | bytes 147464 | tf_op jit(solution)/shard_map/ppermute | solution.py:259
  16.3 4.6 %collective-permute-start.29 = (bf16[16,16,96]{2,1,0:T(8,128)(2,1)S(1)}, bf16[16,16,96]{2,1,0:T(8,128)(2,1)S(1)}, u32[]{:S(2)}, u32[]{:S(2)}) collective-permute-start(bf16[16,16,96]{2,1,0:T(8,128)(2,1)S(1)} %get-tuple-element.70), channel_id=1, source_target_pairs={{0,1},{1,2},{2,3},{3,4},{4,5},{5,6},{6,7},{7,0},{8,9},{9,10},{10,1... | collective-permute-start | bytes 147464 | tf_op jit(solution)/shard_map/ppermute | solution.py:259
  22.0 5.3 %collective-permute-start.30 = (bf16[16,16,96]{2,1,0:T(8,128)(2,1)S(1)}, bf16[16,16,96]{2,1,0:T(8,128)(2,1)S(1)}, u32[]{:S(2)}, u32[]{:S(2)}) collective-permute-start(bf16[16,16,96]{2,1,0:T(8,128)(2,1)S(1)} %get-tuple-element.74), channel_id=1, source_target_pairs={{0,192},{64,0},{128,64},{192,128},{1,193},{65,1},{129,65},{193,129... | collective-permute-start | bytes 147464 | tf_op jit(solution)/shard_map/ppermute | solution.py:259
  25.0 5.7 %collective-permute-start.31 = (bf16[16,16,96]{2,1,0:T(8,128)(2,1)S(1)}, bf16[16,16,96]{2,1,0:T(8,128)(2,1)S(1)}, u32[]{:S(2)}, u32[]{:S(2)}) collective-permute-start(bf16[16,16,96]{2,1,0:T(8,128)(2,1)S(1)} %get-tuple-element.75), channel_id=1, source_target_pairs={{0,56},{8,0},{16,8},{24,16},{32,24},{40,32},{48,40},{56,48},{1,57}... | collective-permute-start | bytes 147464 | tf_op jit(solution)/shard_map/ppermute | solution.py:259
  27.1 4.3 %collective-permute-start.33 = (bf16[16,16,96]{2,1,0:T(8,128)(2,1)S(1)}, bf16[16,16,96]{2,1,0:T(8,128)(2,1)S(1)}, u32[]{:S(2)}, u32[]{:S(2)}) collective-permute-start(bf16[16,16,96]{2,1,0:T(8,128)(2,1)S(1)} %get-tuple-element.77), channel_id=1, source_target_pairs={{0,64},{64,128},{128,192},{192,0},{1,65},{65,129},{129,193},{193,1... | collective-permute-start | bytes 147464 | tf_op jit(solution)/shard_map/ppermute | solution.py:259
  27.1 4.3 %collective-permute-start.34 = (bf16[16,16,96]{2,1,0:T(8,128)(2,1)S(1)}, bf16[16,16,96]{2,1,0:T(8,128)(2,1)S(1)}, u32[]{:S(2)}, u32[]{:S(2)}) collective-permute-start(bf16[16,16,96]{2,1,0:T(8,128)(2,1)S(1)} %get-tuple-element.78), channel_id=1, source_target_pairs={{0,8},{8,16},{16,24},{24,32},{32,40},{40,48},{48,56},{56,0},{1,9},... | collective-permute-start | bytes 147464 | tf_op jit(solution)/shard_map/ppermute | solution.py:259
  27.3 4.3 %collective-permute-start.35 = (bf16[16,16,96]{2,1,0:T(8,128)(2,1)S(1)}, bf16[16,16,96]{2,1,0:T(8,128)(2,1)S(1)}, u32[]{:S(2)}, u32[]{:S(2)}) collective-permute-start(bf16[16,16,96]{2,1,0:T(8,128)(2,1)S(1)} %get-tuple-element.79), channel_id=1, source_target_pairs={{0,1},{1,2},{2,3},{3,4},{4,5},{5,6},{6,7},{7,0},{8,9},{9,10},{10,1... | collective-permute-start | bytes 147464 | tf_op jit(solution)/shard_map/ppermute | solution.py:259
  32.7 6.5 %collective-permute-start.36 = (bf16[16,16,96]{2,1,0:T(8,128)(2,1)S(1)}, bf16[16,16,96]{2,1,0:T(8,128)(2,1)S(1)}, u32[]{:S(2)}, u32[]{:S(2)}) collective-permute-start(bf16[16,16,96]{2,1,0:T(8,128)(2,1)S(1)} %get-tuple-element.83), channel_id=1, source_target_pairs={{0,192},{64,0},{128,64},{192,128},{1,193},{65,1},{129,65},{193,129... | collective-permute-start | bytes 147464 | tf_op jit(solution)/shard_map/ppermute | solution.py:259
  35.7 7.2 %collective-permute-start.37 = (bf16[16,16,96]{2,1,0:T(8,128)(2,1)S(1)}, bf16[16,16,96]{2,1,0:T(8,128)(2,1)S(1)}, u32[]{:S(2)}, u32[]{:S(2)}) collective-permute-start(bf16[16,16,96]{2,1,0:T(8,128)(2,1)S(1)} %get-tuple-element.84), channel_id=1, source_target_pairs={{0,56},{8,0},{16,8},{24,16},{32,24},{40,32},{48,40},{56,48},{1,57}... | collective-permute-start | bytes 147464 | tf_op jit(solution)/shard_map/ppermute | solution.py:259
  39.2 3.7 %collective-permute-start.38 = (bf16[16,16,96]{2,1,0:T(8,128)(2,1)S(1)}, bf16[16,16,96]{2,1,0:T(8,128)(2,1)S(1)}, u32[]{:S(2)}, u32[]{:S(2)}) collective-permute-start(bf16[16,16,96]{2,1,0:T(8,128)(2,1)S(1)} %get-tuple-element.85), channel_id=1, source_target_pairs={{0,7},{1,0},{2,1},{3,2},{4,3},{5,4},{6,5},{7,6},{8,15},{9,8},{10,9... | collective-permute-start | bytes 147464 | tf_op jit(solution)/shard_map/ppermute | solution.py:259
  39.2 4.3 %collective-permute-start.39 = (bf16[16,16,96]{2,1,0:T(8,128)(2,1)S(1)}, bf16[16,16,96]{2,1,0:T(8,128)(2,1)S(1)}, u32[]{:S(2)}, u32[]{:S(2)}) collective-permute-start(bf16[16,16,96]{2,1,0:T(8,128)(2,1)S(1)} %get-tuple-element.86), channel_id=1, source_target_pairs={{0,64},{64,128},{128,192},{192,0},{1,65},{65,129},{129,193},{193,1... | collective-permute-start | bytes 147464 | tf_op jit(solution)/shard_map/ppermute | solution.py:259
  39.2 4.3 %collective-permute-start.40 = (bf16[16,16,96]{2,1,0:T(8,128)(2,1)S(1)}, bf16[16,16,96]{2,1,0:T(8,128)(2,1)S(1)}, u32[]{:S(2)}, u32[]{:S(2)}) collective-permute-start(bf16[16,16,96]{2,1,0:T(8,128)(2,1)S(1)} %get-tuple-element.87), channel_id=1, source_target_pairs={{0,8},{8,16},{16,24},{24,32},{32,40},{40,48},{48,56},{56,0},{1,9},... | collective-permute-start | bytes 147464 | tf_op jit(solution)/shard_map/ppermute | solution.py:259
  39.2 4.4 %collective-permute-start.41 = (bf16[16,16,96]{2,1,0:T(8,128)(2,1)S(1)}, bf16[16,16,96]{2,1,0:T(8,128)(2,1)S(1)}, u32[]{:S(2)}, u32[]{:S(2)}) collective-permute-start(bf16[16,16,96]{2,1,0:T(8,128)(2,1)S(1)} %get-tuple-element.88), channel_id=1, source_target_pairs={{0,1},{1,2},{2,3},{3,4},{4,5},{5,6},{6,7},{7,0},{8,9},{9,10},{10,1... | collective-permute-start | bytes 147464 | tf_op jit(solution)/shard_map/ppermute | solution.py:259
  44.7 6.7 %collective-permute-start.42 = (bf16[16,16,96]{2,1,0:T(8,128)(2,1)S(1)}, bf16[16,16,96]{2,1,0:T(8,128)(2,1)S(1)}, u32[]{:S(2)}, u32[]{:S(2)}) collective-permute-start(bf16[16,16,96]{2,1,0:T(8,128)(2,1)S(1)} %get-tuple-element.92), channel_id=1, source_target_pairs={{0,192},{64,0},{128,64},{192,128},{1,193},{65,1},{129,65},{193,129... | collective-permute-start | bytes 147464 | tf_op jit(solution)/shard_map/ppermute | solution.py:259
  47.4 7.8 %collective-permute-start.43 = (bf16[16,16,96]{2,1,0:T(8,128)(2,1)S(1)}, bf16[16,16,96]{2,1,0:T(8,128)(2,1)S(1)}, u32[]{:S(2)}, u32[]{:S(2)}) collective-permute-start(bf16[16,16,96]{2,1,0:T(8,128)(2,1)S(1)} %get-tuple-element.93), channel_id=1, source_target_pairs={{0,56},{8,0},{16,8},{24,16},{32,24},{40,32},{48,40},{56,48},{1,57}... | collective-permute-start | bytes 147464 | tf_op jit(solution)/shard_map/ppermute | solution.py:259
  51.4 3.7 %collective-permute-start.44 = (bf16[16,16,96]{2,1,0:T(8,128)(2,1)S(1)}, bf16[16,16,96]{2,1,0:T(8,128)(2,1)S(1)}, u32[]{:S(2)}, u32[]{:S(2)}) collective-permute-start(bf16[16,16,96]{2,1,0:T(8,128)(2,1)S(1)} %get-tuple-element.94), channel_id=1, source_target_pairs={{0,7},{1,0},{2,1},{3,2},{4,3},{5,4},{6,5},{7,6},{8,15},{9,8},{10,9... | collective-permute-start | bytes 147464 | tf_op jit(solution)/shard_map/ppermute | solution.py:259
  51.4 4.3 %collective-permute-start.45 = (bf16[16,16,96]{2,1,0:T(8,128)(2,1)S(1)}, bf16[16,16,96]{2,1,0:T(8,128)(2,1)S(1)}, u32[]{:S(2)}, u32[]{:S(2)}) collective-permute-start(bf16[16,16,96]{2,1,0:T(8,128)(2,1)S(1)} %get-tuple-element.95), channel_id=1, source_target_pairs={{0,64},{64,128},{128,192},{192,0},{1,65},{65,129},{129,193},{193,1... | collective-permute-start | bytes 147464 | tf_op jit(solution)/shard_map/ppermute | solution.py:259
  51.4 4.3 %collective-permute-start.46 = (bf16[16,16,96]{2,1,0:T(8,128)(2,1)S(1)}, bf16[16,16,96]{2,1,0:T(8,128)(2,1)S(1)}, u32[]{:S(2)}, u32[]{:S(2)}) collective-permute-start(bf16[16,16,96]{2,1,0:T(8,128)(2,1)S(1)} %get-tuple-element.96), channel_id=1, source_target_pairs={{0,8},{8,16},{16,24},{24,32},{32,40},{40,48},{48,56},{56,0},{1,9},... | collective-permute-start | bytes 147464 | tf_op jit(solution)/shard_map/ppermute | solution.py:259
  51.5 4.4 %collective-permute-start.47 = (bf16[16,16,96]{2,1,0:T(8,128)(2,1)S(1)}, bf16[16,16,96]{2,1,0:T(8,128)(2,1)S(1)}, u32[]{:S(2)}, u32[]{:S(2)}) collective-permute-start(bf16[16,16,96]{2,1,0:T(8,128)(2,1)S(1)} %get-tuple-element.97), channel_id=1, source_target_pairs={{0,1},{1,2},{2,3},{3,4},{4,5},{5,6},{6,7},{7,0},{8,9},{9,10},{10,1... | collective-permute-start | bytes 147464 | tf_op jit(solution)/shard_map/ppermute | solution.py:259
  68.5 14.7 %all-to-all-start.1 = ((f32[32,1,240]{2,1,0:T(1,128)}), f32[32,1,240]{2,1,0:T(1,128)S(1)}, u32[]{:S(2)}, u32[]{:S(2)}) async-start(f32[32,1,240]{2,1,0:T(1,128)} %broadcast_in_dim.2), calls=%async_computation.1 | async-start | bytes 65536 | tf_op jit(solution)/shard_map/all_to_all | solution.py:334
  (3 other events, 47.5 us)
where the time goes:
time: 86.2 us; the launch traced here: 86 us
  starting transfers between devices  40.4 us (47%)
  Pallas kernels  18.5 us (21%)
  waiting for transfers between devices  13.6 us (16%)
  blocking collectives  10.9 us (13%)
  between operations  1.65 us (2%)
    ppermute x24, starting transfers between devices, shifted(): lax.ppermute(shard, axis, [(i, (i + by) % length) for i in range(length)])  34.4 us
    pallas_call x11, Pallas kernels, call(): pl.pallas_call(kernel, name=name, out_shape=out_shape, in_specs=[whole] *...  18.5 us
    all_to_all x1, blocking collectives, local(): sums = jnp.sum(lax.all_to_all(sums, 'gz', 0, 0), 0)  10.9 us
    all_to_all x1, waiting for transfers between devices, local(): lax.all_to_all(jnp.broadcast_to(sums, (SECOND_GROUP, LANES)), ('ta', 'xy'...  8.77 us
    all_to_all x1, starting transfers between devices, local(): lax.all_to_all(jnp.broadcast_to(sums, (SECOND_GROUP, LANES)), ('ta', 'xy'...  5.97 us
    ppermute x24, waiting for transfers between devices, shifted(): lax.ppermute(shard, axis, [(i, (i + by) % length) for i in range(length)])  4.81 us
  transfers between devices with their start and end apart: 25, of which 9 were waited for; matrix products, arithmetic and copies ran while one was open for 0% of the time, Pallas kernels for 13%

commit v1 on v0

--- a/solution.py
+++ b/solution.py
@@ -23,8 +23,16 @@
 FIRST_GROUP = 8
 SECOND_GROUP = 32
 AXES = ("ta", "gz", "xy")
+ORDER = (0, 2, 1)
 KEEP_SQUARE = 1e-4
 KEEP_VECTOR = 0.1
+
+LAST_SLICES = [(SITES + 16, 16)]
+LAST_SLICES += [(2 * SITES + t * 16 + 8, 8) for t in range(2)]
+LAST_SLICES += [(3 * SITES + t * 16 + z * 8 + 4, 4) for t in range(2) for z in range(2)]
+OTHER_SLICES = [(0, SITES + 16)]
+OTHER_SLICES += [(2 * SITES + t * 16, 8) for t in range(2)]
+OTHER_SLICES += [(3 * SITES + t * 16 + z * 8, 4) for t in range(2) for z in range(2)] + [(4 * SITES, SITES)]
 
 NT = (((1,), (1,)), ((), ()))
 NN = (((1,), (0,)), ((), ()))
@@ -53,10 +61,19 @@
     return lax.dot_general(left, right, dims, preferred_element_type=jnp.float32)
 
 
-def begin_kernel(right_ref, wide_ref, narrow_ref, *firsts):
-    wide_ref[...] = jnp.zeros(wide_ref.shape, jnp.float32)
+def begin_kernel(right_ref, links_ref, wide_ref, narrow_ref, *refs):
+    firsts, products, held_ref, row_ref, sems = refs[0:3], refs[3:6], refs[6], refs[7], refs[8]
+    copies = [pltpu.make_async_copy(right_ref, row_ref, sems.at[0])]
+    for start, count in LAST_SLICES + OTHER_SLICES:
+        here = pl.ds(start, count)
+        copies.append(pltpu.make_async_copy(links_ref.at[here], held_ref.at[here], sems.at[len(copies)]))
+    for copy in copies:
+        copy.start()
+    for site in range(SITES):
+        wide_ref[site] = jnp.zeros((ROWS, COMP), jnp.float32)
+    copies[0].wait()
     for group in range(GROUPS):
-        row = right_ref[group]
+        row = row_ref[group]
         for source in range(RHS):
             piece = row[:, source * COMP : (source + 1) * COMP]
             for y in range(4):
@@ -64,6 +81,11 @@
     for site in range(SITES):
         narrow_ref[site] = wide_ref[site].astype(jnp.bfloat16)
     send_firsts(narrow_ref, firsts)
+    for copy in copies[1 : len(LAST_SLICES) + 1]:
+        copy.wait()
+    send_products(narrow_ref, held_ref, products)
+    for copy in copies[len(LAST_SLICES) + 1 :]:
+        copy.wait()
 
 
 def send_firsts(narrow_ref, firsts):
@@ -73,26 +95,27 @@
                 firsts[direction][on_face(cell, direction)] = narrow_ref[place(cell)]
 
 
-def send_products(narrow_ref, links_ref, *products):
+def send_products(narrow_ref, links_ref, products):
     for direction in range(3):
         for cell in CELLS:
             if cell[direction] == 1:
                 site = place(cell)
+                spot = on_face(cell, direction)
                 product = dot(narrow_ref[site], links_ref[(direction + 1) * SITES + site], NN)
-                products[direction][on_face(cell, direction)] = product.astype(jnp.bfloat16)
+                products[direction][spot] = product.astype(jnp.bfloat16)
 
 
 def gram_rows(wides, last):
     return [sum(wides[i][site] * wides[last][site] for site in range(SITES)) for i in range(last + 1)]
 
 
-def as_rows(wide_ref, row_ref):
+def as_rows(wide_ref, row_ref, at=0):
     for group in range(GROUPS):
         sites = [wide_ref[group * 4 + y] for y in range(4)]
         pieces = [
             jnp.concatenate([site[source : source + 1] for site in sites], 0) for source in range(RHS)
         ]
-        row_ref[group] = jnp.concatenate(pieces, 1)
+        row_ref[at + group] = jnp.concatenate(pieces, 1)
 
 
 def inner_kernel(step, narrow_ref, links_ref, *refs):
@@ -116,41 +139,53 @@
         as_rows(wides[step], row_ref)
 
 
-def joined(cell, part_ref, links_ref, ahead, behind):
-    site = place(cell)
-    total = part_ref[site]
-    for direction in range(3):
-        spot = on_face(cell, direction)
-        if cell[direction] == 1:
-            total -= dot(ahead[direction][spot], links_ref[(direction + 1) * SITES + site], NT)
-        else:
-            total -= behind[direction][spot].astype(jnp.float32)
+def middle_kernel(part_ref, links_ref, behind_ref, *refs):
+    ahead, next_ref = refs[0:3], refs[3]
+    for cell in CELLS:
+        site = place(cell)
+        total = part_ref[site]
+        for direction in range(3):
+            if cell[direction] == 1:
+                link = links_ref[(direction + 1) * SITES + site]
+                total -= dot(ahead[direction][on_face(cell, direction)], link, NT)
+        if cell[0] == 0:
+            total -= behind_ref[on_face(cell, 0)].astype(jnp.float32)
+        next_ref[site] = total
+
+
+def joined(cell, part_ref, behind):
+    total = part_ref[place(cell)]
+    for direction in (1, 2):
+        if cell[direction] == 0:
+            total -= behind[direction - 1][on_face(cell, direction)].astype(jnp.float32)
     return total
 
 
 def outer_kernel(part_ref, links_ref, *refs):
-    ahead, behind, (wide_ref, narrow_ref), faces = refs[0:3], refs[3:6], refs[6:8], refs[8:14]
+    behind, (wide_ref, narrow_ref), faces = refs[0:2], refs[2:4], refs[4:10]
     for cell in CELLS:
-        total = joined(cell, part_ref, links_ref, ahead, behind)
+        total = joined(cell, part_ref, behind)
         wide_ref[place(cell)] = total
         narrow_ref[place(cell)] = total.astype(jnp.bfloat16)
     send_firsts(narrow_ref, faces[0:3])
-    send_products(narrow_ref, links_ref, *faces[3:6])
-
-
-def last_kernel(part_ref, links_ref, *refs):
-    ahead, behind, wides, grams = refs[0:3], refs[3:6], refs[6:10], refs[10:14]
-    row_ref, sums_ref, wide_ref = refs[14:17]
+    send_products(narrow_ref, links_ref, faces[3:6])
+
+
+def last_kernel(part_ref, *refs):
+    behind, wides, grams = refs[0:2], refs[2:6], refs[6:10]
+    rows_in, out_ref, wide_ref = refs[10:14], refs[14], refs[15]
     for cell in CELLS:
-        wide_ref[place(cell)] = joined(cell, part_ref, links_ref, ahead, behind)
+        wide_ref[place(cell)] = joined(cell, part_ref, behind)
     rows = [gram[i] for gram in grams for i in range(gram.shape[0])]
     rows += gram_rows(tuple(wides) + (wide_ref,), ITERS)
     stacked = jnp.concatenate(rows, 0)
-    sums_ref[...] = lax.dot_general(
-        jnp.ones((FIRST_GROUP, COMP), jnp.float32), stacked, NT,
+    out_ref[BASIS * GROUPS, 0:1, 0:LANES] = lax.dot_general(
+        jnp.ones((8, COMP), jnp.float32), stacked, NT,
         precision=lax.Precision.HIGHEST, preferred_element_type=jnp.float32,
-    )
-    as_rows(wide_ref, row_ref)
+    )[0:1]
+    for j, row_ref in enumerate(rows_in):
+        out_ref[j * GROUPS : (j + 1) * GROUPS] = row_ref[...]
+    as_rows(wide_ref, out_ref, ITERS * GROUPS)
 
 
 def apply_coefficients(z):
@@ -167,8 +202,7 @@
     return sum(terms[1:], terms[0])
 
 
-def finish_kernel(gathered_ref, w0, w1, w2, w3, w4, solution_ref, residual_ref, sound_ref):
-    wides = (w0, w1, w2, w3, w4)
+def finish_kernel(gathered_ref, held_ref, solution_ref, residual_ref, sound_ref):
     summed = lax.dot_general(
         gathered_ref[...], jnp.ones((SECOND_GROUP, 128), jnp.float32), TN,
         precision=lax.Precision.HIGHEST, preferred_element_type=jnp.float32,
@@ -225,7 +259,7 @@
         packed[:, 0:ROWS], spread, TN, precision=lax.Precision.HIGHEST, preferred_element_type=jnp.float32
     )
     for group in range(GROUPS):
-        held = [w[group] for w in wides]
+        held = [held_ref[j * GROUPS + group] for j in range(BASIS)]
         solution_ref[group] = combine([factors[i : i + 1] for i in range(ITERS)], held)
         residual_ref[group] = combine([factors[ITERS + i : ITERS + i + 1] for i in range(BASIS)], held)
 
@@ -235,19 +269,20 @@
 
 
 FACES = [shape((FACE, ROWS, COMP), jnp.bfloat16)] * 3
+LINKS = shape((5 * SITES, COMP, COMP), jnp.bfloat16)
 ROW = shape((GROUPS, 4, RHS * COMP))
 WIDE = shape((SITES, ROWS, COMP))
 NARROW = shape((SITES, ROWS, COMP), jnp.bfloat16)
 
 
-def call(kernel, name, out_shape, operands, scratch=()):
+def call(kernel, name, out_shape, operands, scratch=(), apart=()):
     whole = pl.BlockSpec(memory_space=pltpu.VMEM)
     scalar = pl.BlockSpec(memory_space=pltpu.SMEM)
     return pl.pallas_call(
         kernel,
         name=name,
         out_shape=out_shape,
-        in_specs=[whole] * len(operands),
+        in_specs=[pl.BlockSpec(memory_space=pl.ANY) if i in apart else whole for i in range(len(operands))],
         out_specs=[scalar if o.shape == (1, 1) else whole for o in out_shape],
         scratch_shapes=scratch,
         compiler_params=pltpu.CompilerParams(vmem_limit_bytes=24 * 2**20),
@@ -305,35 +340,45 @@
 def local(right_side, link_blocks):
     links = link_blocks.reshape(5 * SITES, COMP, COMP)
     row = right_side.reshape(GROUPS, 4, RHS * COMP)
-    wide, narrow, *firsts = call(begin_kernel, "begin", [WIDE, NARROW] + FACES, (row,))
-    products = call(send_products, "products", FACES, (narrow, links))
+    wide, narrow, *faces, links = call(
+        begin_kernel, "begin", [WIDE, NARROW] + FACES * 2 + [LINKS], (row, links),
+        [pltpu.VMEM((GROUPS, 4, RHS * COMP), jnp.float32),
+         pltpu.SemaphoreType.DMA((len(LAST_SLICES + OTHER_SLICES) + 1,))],
+        apart=(0, 1),
+    )
+    firsts, products = faces[0:3], faces[3:6]
     wides, grams, rows = [wide], [], [row]
     for step in range(ITERS):
-        ahead = [shifted(firsts[d], AXES[d], -1) for d in range(3)]
-        behind = [shifted(products[d], AXES[d], 1) for d in range(3)]
+        ahead, behind = [None] * 3, [None] * 3
+        for d in ORDER:
+            ahead[d] = shifted(firsts[d], AXES[d], -1)
+            behind[d] = shifted(products[d], AXES[d], 1)
         part, gram, *made = call(
             functools.partial(inner_kernel, step), f"inner{step}",
             [WIDE, shape((step + 1, ROWS, COMP))] + [ROW] * (step > 0), (narrow, links, *wides),
         )
         grams.append(gram)
         rows += made
+        (part,) = call(middle_kernel, f"middle{step}", [WIDE], (part, links, behind[0], *ahead))
         if step < ITERS - 1:
             wide, narrow, *faces = call(
-                outer_kernel, f"outer{step}", [WIDE, NARROW] + FACES * 2, (part, links, *ahead, *behind)
+                outer_kernel, f"outer{step}", [WIDE, NARROW] + FACES * 2, (part, links, *behind[1:])
             )
             firsts, products = faces[0:3], faces[3:6]
             wides.append(wide)
         else:
-            made, sums = call(
-                last_kernel, "last", [ROW, shape((FIRST_GROUP, LANES))],
-                (part, links, *ahead, *behind, *wides, *grams),
+            (held,) = call(
+                last_kernel, "last", [shape((BASIS * GROUPS + 1, 4, RHS * COMP))],
+                (part, *behind[1:], *wides, *grams, *rows),
                 [pltpu.VMEM((SITES, ROWS, COMP), jnp.float32)],
             )
-            rows.append(made)
-    sums = jnp.sum(lax.all_to_all(sums, "gz", 0, 0), 0)
-    sums = lax.all_to_all(jnp.broadcast_to(sums, (SECOND_GROUP, LANES)), ("ta", "xy"), 0, 0)
+    sums = held[BASIS * GROUPS, 0, 0:LANES]
+    for axes, members in (("gz", 8), (("ta", "xy"), 32)):
+        sums = lax.all_to_all(jnp.broadcast_to(sums, (members, LANES)), axes, 0, 0)
+        if members == 8:
+            sums = jnp.sum(sums, 0)
     out, residual, sound = call(
-        finish_kernel, "finish", [ROW, ROW, shape((1, 1), jnp.int32)], (sums, *rows)
+        finish_kernel, "finish", [ROW, ROW, shape((1, 1), jnp.int32)], (sums, held)
     )
     return lax.cond(
         sound[0, 0] > 0,

time: 86.2 us -> 81.4 us (0.944)
  starting transfers between devices: 40.4 us -> 38.5 us
  waiting for transfers between devices: 13.6 us -> 12 us
  Pallas kernels: 18.5 us -> 17.2 us
    all_to_all x1, starting transfers between devices: 5.97 us -> 4.1 us  [local(): sums = lax.all_to_all(jnp.broadcast_to(sums, (members, LANES)), axes, 0, 0)]
    ppermute x24, waiting for transfers between devices: 4.81 us -> 3.28 us  [shifted(): lax.ppermute(shard, axis, [(i, (i + by) % length) for i in range(length)])]
    pallas_call x11 -> x14, Pallas kernels: 18.5 us -> 17.2 us  [call(): pl.pallas_call(kernel, name=name, out_shape=out_shape, in_specs=[pl.Block...]
  transfers between devices with their start and end apart: 25 -> 25, of which waited for: 9 -> 5; matrix products, arithmetic and copies ran while one was open for 0% -> 0% of each run, Pallas kernels for 13% -> 14%
where the time goes in v1:
time: 81.4 us; the launch traced here: 81.2 us
  starting transfers between devices  38.5 us (47%)
  Pallas kernels  17.2 us (21%)
  waiting for transfers between devices  12 us (15%)
  blocking collectives  11 us (14%)
  between operations  1.57 us (2%)
    ppermute x24, starting transfers between devices, shifted(): lax.ppermute(shard, axis, [(i, (i + by) % length) for i in range(length)])  34.4 us
    pallas_call x14, Pallas kernels, call(): pl.pallas_call(kernel, name=name, out_shape=out_shape, in_specs=[pl.Block...  17.2 us
    all_to_all x1, blocking collectives, local(): sums = lax.all_to_all(jnp.broadcast_to(sums, (members, LANES)), axes, 0, 0)  11 us
    all_to_all x1, waiting for transfers between devices, local(): sums = lax.all_to_all(jnp.broadcast_to(sums, (members, LANES)), axes, 0, 0)  8.77 us
    all_to_all x1, starting transfers between devices, local(): sums = lax.all_to_all(jnp.broadcast_to(sums, (members, LANES)), axes, 0, 0)  4.1 us
    ppermute x24, waiting for transfers between devices, shifted(): lax.ppermute(shard, axis, [(i, (i + by) % length) for i in range(length)])  3.28 us
  transfers between devices with their start and end apart: 25, of which 5 were waited for; matrix products, arithmetic and copies ran while one was open for 0% of the time, Pallas kernels for 14%

profile of v1, /device:TPU:1, one launch (start us, length us, event | category | flops | bytes accessed | tf_op | source)
XLA Modules:
  0.0 81.2 jit_solution(8151659283460819147)
XLA Ops:
  0.6 2.3 %begin.1 = (f32[32,16,96]{2,1,0:T(8,128)S(1)}, bf16[32,16,96]{2,1,0:T(8,128)(2,1)S(1)}, bf16[16,16,96]{2,1,0:T(8,128)(2,1)S(1)}, bf16[16,16,96]{2,1,0:T(8,128)(2...) custom-call(f32[8,4,1152]{2,1,0:T(4,128)} %bitcast.116, ...), custom_call_target="tpu_custom_call" | custom-call | tf_op jit(solution)/shard_map/begin/pallas_call | solution.py:281
  2.9 2.2 %collective-permute-start.24 = (bf16[16,16,96]{2,1,0:T(8,128)(2,1)S(1)}, bf16[16,16,96]{2,1,0:T(8,128)(2,1)S(1)}, u32[]{:S(2)}, u32[]{:S(2)}) collective-permute-start(bf16[16,16,96]{2,1,0:T(8,128)(2,1)S(1)} %get-tuple-element.65), channel_id=1, source_target_pairs={{0,64},{64,128},{128,192},{192,0},{1,65},{65,129},{129,193},{193,1... | collective-permute-start | bytes 147464 | tf_op jit(solution)/shard_map/ppermute | solution.py:294
  5.2 1.5 %collective-permute-start.25 = (bf16[16,16,96]{2,1,0:T(8,128)(2,1)S(1)}, bf16[16,16,96]{2,1,0:T(8,128)(2,1)S(1)}, u32[]{:S(2)}, u32[]{:S(2)}) collective-permute-start(bf16[16,16,96]{2,1,0:T(8,128)(2,1)S(1)} %get-tuple-element.66), channel_id=1, source_target_pairs={{0,192},{64,0},{128,64},{192,128},{1,193},{65,1},{129,65},{193,129... | collective-permute-start | bytes 147464 | tf_op jit(solution)/shard_map/ppermute | solution.py:294
  6.7 2.8 %collective-permute-start.26 = (bf16[16,16,96]{2,1,0:T(8,128)(2,1)S(1)}, bf16[16,16,96]{2,1,0:T(8,128)(2,1)S(1)}, u32[]{:S(2)}, u32[]{:S(2)}) collective-permute-start(bf16[16,16,96]{2,1,0:T(8,128)(2,1)S(1)} %get-tuple-element.67), channel_id=1, source_target_pairs={{0,56},{8,0},{16,8},{24,16},{32,24},{40,32},{48,40},{56,48},{1,57}... | collective-permute-start | bytes 147464 | tf_op jit(solution)/shard_map/ppermute | solution.py:294
  9.5 3.8 %collective-permute-start.27 = (bf16[16,16,96]{2,1,0:T(8,128)(2,1)S(1)}, bf16[16,16,96]{2,1,0:T(8,128)(2,1)S(1)}, u32[]{:S(2)}, u32[]{:S(2)}) collective-permute-start(bf16[16,16,96]{2,1,0:T(8,128)(2,1)S(1)} %get-tuple-element.68), channel_id=1, source_target_pairs={{0,7},{1,0},{2,1},{3,2},{4,3},{5,4},{6,5},{7,6},{8,15},{9,8},{10,9... | collective-permute-start | bytes 147464 | tf_op jit(solution)/shard_map/ppermute | solution.py:294
  13.3 1.4 %collective-permute-start.28 = (bf16[16,16,96]{2,1,0:T(8,128)(2,1)S(1)}, bf16[16,16,96]{2,1,0:T(8,128)(2,1)S(1)}, u32[]{:S(2)}, u32[]{:S(2)}) collective-permute-start(bf16[16,16,96]{2,1,0:T(8,128)(2,1)S(1)} %get-tuple-element.69), channel_id=1, source_target_pairs={{0,8},{8,16},{16,24},{24,32},{32,40},{40,48},{48,56},{56,0},{1,9},... | collective-permute-start | bytes 147464 | tf_op jit(solution)/shard_map/ppermute | solution.py:294
  14.7 2.1 %inner0.1 = (f32[32,16,96]{2,1,0:T(8,128)S(1)}, f32[1,16,96]{2,1,0:T(8,128)S(1)}) custom-call(bf16[32,16,96]{2,1,0:T(8,128)(2,1)S(1)} %get-tuple-element.61.narrow_ref, bf16[160,96,96]{2,1,0:T(8,128)(2,1)S(1)} %get-tuple-element.62.links_ref, f32[32,16,96]{2,1,0:T(8,128)S(1)} %get-tuple-element.63.refs_0_.refs_2_), custom_call_target="tpu_custom_call" | custom-call | tf_op jit(solution)/shard_map/inner0/pallas_call | solution.py:281
  17.6 1.7 %collective-permute-done.29.refs_1_ = bf16[16,16,96]{2,1,0:T(8,128)(2,1)S(1)} collective-permute-done((bf16[16,16,96]{2,1,0:T(8,128)(2,1)S(1)}, bf16[16,16,96]{2,1,0:T(8,128)(2,1)S(1)}, u32[]{:S(2)}, u32[]{:S(2)}) %collective-permute-start.29) | collective-permute-done | bytes 49184 | tf_op jit(solution)/shard_map/ppermute | solution.py:294
  20.0 2.6 %collective-permute-start.31 = (bf16[16,16,96]{2,1,0:T(8,128)(2,1)S(1)}, bf16[16,16,96]{2,1,0:T(8,128)(2,1)S(1)}, u32[]{:S(2)}, u32[]{:S(2)}) collective-permute-start(bf16[16,16,96]{2,1,0:T(8,128)(2,1)S(1)} %get-tuple-element.75), channel_id=1, source_target_pairs={{0,192},{64,0},{128,64},{192,128},{1,193},{65,1},{129,65},{193,129... | collective-permute-start | bytes 147464 | tf_op jit(solution)/shard_map/ppermute | solution.py:294
  22.6 2.1 %collective-permute-start.32 = (bf16[16,16,96]{2,1,0:T(8,128)(2,1)S(1)}, bf16[16,16,96]{2,1,0:T(8,128)(2,1)S(1)}, u32[]{:S(2)}, u32[]{:S(2)}) collective-permute-start(bf16[16,16,96]{2,1,0:T(8,128)(2,1)S(1)} %get-tuple-element.76), channel_id=1, source_target_pairs={{0,56},{8,0},{16,8},{24,16},{32,24},{40,32},{48,40},{56,48},{1,57}... | collective-permute-start | bytes 147464 | tf_op jit(solution)/shard_map/ppermute | solution.py:294
  25.6 0.8 collective-permute-start.35
  26.3 2.1 %inner1.1 = (f32[32,16,96]{2,1,0:T(8,128)S(1)}, f32[2,16,96]{2,1,0:T(8,128)S(1)}, f32[8,4,1152]{2,1,0:T(4,128)S(1)}) custom-call(bf16[32,16,96]{2,1,0:T(8,128)(2,1)S(1)} %get-tuple-element.71.narrow_ref, bf16[160,96,96]{2,1,0:T(8,128)(2,1)S(1)} %get-tuple-element.62.links_ref, f32[32,16,96]{2,1,0:T(8,128)S(1)} %get-tuple-element.63.refs_0_.refs_2_, ...), custom_call_target="tpu_custom_call" | custom-call | tf_op jit(solution)/shard_map/inner1/pallas_call | solution.py:281
  30.4 2.7 %collective-permute-start.37 = (bf16[16,16,96]{2,1,0:T(8,128)(2,1)S(1)}, bf16[16,16,96]{2,1,0:T(8,128)(2,1)S(1)}, u32[]{:S(2)}, u32[]{:S(2)}) collective-permute-start(bf16[16,16,96]{2,1,0:T(8,128)(2,1)S(1)} %get-tuple-element.84), channel_id=1, source_target_pairs={{0,192},{64,0},{128,64},{192,128},{1,193},{65,1},{129,65},{193,129... | collective-permute-start | bytes 147464 | tf_op jit(solution)/shard_map/ppermute | solution.py:294
  33.1 3.6 %collective-permute-start.38 = (bf16[16,16,96]{2,1,0:T(8,128)(2,1)S(1)}, bf16[16,16,96]{2,1,0:T(8,128)(2,1)S(1)}, u32[]{:S(2)}, u32[]{:S(2)}) collective-permute-start(bf16[16,16,96]{2,1,0:T(8,128)(2,1)S(1)} %get-tuple-element.85), channel_id=1, source_target_pairs={{0,56},{8,0},{16,8},{24,16},{32,24},{40,32},{48,40},{56,48},{1,57}... | collective-permute-start | bytes 147464 | tf_op jit(solution)/shard_map/ppermute | solution.py:294
  37.2 1.0 %collective-permute-start.41 = (bf16[16,16,96]{2,1,0:T(8,128)(2,1)S(1)}, bf16[16,16,96]{2,1,0:T(8,128)(2,1)S(1)}, u32[]{:S(2)}, u32[]{:S(2)}) collective-permute-start(bf16[16,16,96]{2,1,0:T(8,128)(2,1)S(1)} %get-tuple-element.88), channel_id=1, source_target_pairs={{0,1},{1,2},{2,3},{3,4},{4,5},{5,6},{6,7},{7,0},{8,9},{9,10},{10,1... | collective-permute-start | bytes 147464 | tf_op jit(solution)/shard_map/ppermute | solution.py:294
  38.2 2.1 %inner2.1 = (f32[32,16,96]{2,1,0:T(8,128)S(1)}, f32[3,16,96]{2,1,0:T(8,128)S(1)}, f32[8,4,1152]{2,1,0:T(4,128)S(1)}) custom-call(bf16[32,16,96]{2,1,0:T(8,128)(2,1)S(1)} %get-tuple-element.80.narrow_ref, bf16[160,96,96]{2,1,0:T(8,128)(2,1)S(1)} %get-tuple-element.62.links_ref, f32[32,16,96]{2,1,0:T(8,128)S(1)} %get-tuple-element.63.refs_0_.refs_2_, ...), custom_call_target="tpu_custom_call" | custom-call | tf_op jit(solution)/shard_map/inner2/pallas_call | solution.py:281
  42.0 2.7 %collective-permute-start.43 = (bf16[16,16,96]{2,1,0:T(8,128)(2,1)S(1)}, bf16[16,16,96]{2,1,0:T(8,128)(2,1)S(1)}, u32[]{:S(2)}, u32[]{:S(2)}) collective-permute-start(bf16[16,16,96]{2,1,0:T(8,128)(2,1)S(1)} %get-tuple-element.93), channel_id=1, source_target_pairs={{0,192},{64,0},{128,64},{192,128},{1,193},{65,1},{129,65},{193,129... | collective-permute-start | bytes 147464 | tf_op jit(solution)/shard_map/ppermute | solution.py:294
  44.7 4.0 %collective-permute-start.44 = (bf16[16,16,96]{2,1,0:T(8,128)(2,1)S(1)}, bf16[16,16,96]{2,1,0:T(8,128)(2,1)S(1)}, u32[]{:S(2)}, u32[]{:S(2)}) collective-permute-start(bf16[16,16,96]{2,1,0:T(8,128)(2,1)S(1)} %get-tuple-element.94), channel_id=1, source_target_pairs={{0,56},{8,0},{16,8},{24,16},{32,24},{40,32},{48,40},{56,48},{1,57}... | collective-permute-start | bytes 147464 | tf_op jit(solution)/shard_map/ppermute | solution.py:294
  49.2 1.0 %collective-permute-start.47 = (bf16[16,16,96]{2,1,0:T(8,128)(2,1)S(1)}, bf16[16,16,96]{2,1,0:T(8,128)(2,1)S(1)}, u32[]{:S(2)}, u32[]{:S(2)}) collective-permute-start(bf16[16,16,96]{2,1,0:T(8,128)(2,1)S(1)} %get-tuple-element.97), channel_id=1, source_target_pairs={{0,1},{1,2},{2,3},{3,4},{4,5},{5,6},{6,7},{7,0},{8,9},{9,10},{10,1... | collective-permute-start | bytes 147464 | tf_op jit(solution)/shard_map/ppermute | solution.py:294
  50.2 2.2 %inner3.1 = (f32[32,16,96]{2,1,0:T(8,128)S(1)}, f32[4,16,96]{2,1,0:T(8,128)S(1)}, f32[8,4,1152]{2,1,0:T(4,128)S(1)}) custom-call(bf16[32,16,96]{2,1,0:T(8,128)(2,1)S(1)} %get-tuple-element.89.narrow_ref, bf16[160,96,96]{2,1,0:T(8,128)(2,1)S(1)} %get-tuple-element.62.links_ref, f32[32,16,96]{2,1,0:T(8,128)S(1)} %get-tuple-element.63.refs_0_.refs_2_, ...), custom_call_target="tpu_custom_call" | custom-call | tf_op jit(solution)/shard_map/inner3/pallas_call | solution.py:281
  54.0 11.0 %all_to_all.14 = f32[8,1,240]{2,1,0:T(1,128)S(1)} all-to-all(f32[8,1,240]{2,1,0:T(1,128)S(1)} %broadcast_in_dim.4), channel_id=1, replica_groups=mesh['ta'=4,'gz'=8,'xy'=8] {'gz'}, dimensions={0} | all-to-all | bytes 15360 | tf_op jit(solution)/shard_map/all_to_all | solution.py:377
  65.6 4.1 %all-to-all-start.1 = ((f32[32,1,240]{2,1,0:T(1,128)}), f32[32,1,240]{2,1,0:T(1,128)S(1)}, u32[]{:S(2)}, u32[]{:S(2)}) async-start(f32[32,1,240]{2,1,0:T(1,128)} %broadcast_in_dim.5), calls=%async_computation.1 | async-start | bytes 65536 | tf_op jit(solution)/shard_map/all_to_all | solution.py:377
  69.7 8.8 %all-to-all-done.1 = f32[32,1,240]{2,1,0:T(1,128)S(1)} async-done(((f32[32,1,240]{2,1,0:T(1,128)}), f32[32,1,240]{2,1,0:T(1,128)S(1)}, u32[]{:S(2)}, u32[]{:S(2)}) %all-to-all-start.1) | async-done | bytes 30752 | tf_op jit(solution)/shard_map/all_to_all | solution.py:377
  78.5 1.7 %finish.1 = (f32[8,4,1152]{2,1,0:T(4,128)}, f32[8,4,1152]{2,1,0:T(4,128)}, s32[1,1]{1,0:T(1,128)}) custom-call(f32[32,240]{1,0:T(8,128)S(1)} %bitcast.114, f32[41,4,1152]{2,1,0:T(4,128)S(1)} %last.1.held_ref), custom_call_target="tpu_custom_call" | custom-call | tf_op jit(solution)/shard_map/finish/pallas_call | solution.py:281
  (49 shorter events, 9.3 us)
Async XLA Ops:
  2.9 11.8 %collective-permute-start.24 = (bf16[16,16,96]{2,1,0:T(8,128)(2,1)S(1)}, bf16[16,16,96]{2,1,0:T(8,128)(2,1)S(1)}, u32[]{:S(2)}, u32[]{:S(2)}) collective-permute-start(bf16[16,16,96]{2,1,0:T(8,128)(2,1)S(1)} %get-tuple-element.65), channel_id=1, source_target_pairs={{0,64},{64,128},{128,192},{192,0},{1,65},{65,129},{129,193},{193,1... | collective-permute-start | bytes 147464 | tf_op jit(solution)/shard_map/ppermute | solution.py:294
  5.2 11.7 %collective-permute-start.25 = (bf16[16,16,96]{2,1,0:T(8,128)(2,1)S(1)}, bf16[16,16,96]{2,1,0:T(8,128)(2,1)S(1)}, u32[]{:S(2)}, u32[]{:S(2)}) collective-permute-start(bf16[16,16,96]{2,1,0:T(8,128)(2,1)S(1)} %get-tuple-element.66), channel_id=1, source_target_pairs={{0,192},{64,0},{128,64},{192,128},{1,193},{65,1},{129,65},{193,129... | collective-permute-start | bytes 147464 | tf_op jit(solution)/shard_map/ppermute | solution.py:294
  6.7 10.2 %collective-permute-start.26 = (bf16[16,16,96]{2,1,0:T(8,128)(2,1)S(1)}, bf16[16,16,96]{2,1,0:T(8,128)(2,1)S(1)}, u32[]{:S(2)}, u32[]{:S(2)}) collective-permute-start(bf16[16,16,96]{2,1,0:T(8,128)(2,1)S(1)} %get-tuple-element.67), channel_id=1, source_target_pairs={{0,56},{8,0},{16,8},{24,16},{32,24},{40,32},{48,40},{56,48},{1,57}... | collective-permute-start | bytes 147464 | tf_op jit(solution)/shard_map/ppermute | solution.py:294
  9.5 7.4 %collective-permute-start.27 = (bf16[16,16,96]{2,1,0:T(8,128)(2,1)S(1)}, bf16[16,16,96]{2,1,0:T(8,128)(2,1)S(1)}, u32[]{:S(2)}, u32[]{:S(2)}) collective-permute-start(bf16[16,16,96]{2,1,0:T(8,128)(2,1)S(1)} %get-tuple-element.68), channel_id=1, source_target_pairs={{0,7},{1,0},{2,1},{3,2},{4,3},{5,4},{6,5},{7,6},{8,15},{9,8},{10,9... | collective-permute-start | bytes 147464 | tf_op jit(solution)/shard_map/ppermute | solution.py:294
  13.3 4.3 %collective-permute-start.28 = (bf16[16,16,96]{2,1,0:T(8,128)(2,1)S(1)}, bf16[16,16,96]{2,1,0:T(8,128)(2,1)S(1)}, u32[]{:S(2)}, u32[]{:S(2)}) collective-permute-start(bf16[16,16,96]{2,1,0:T(8,128)(2,1)S(1)} %get-tuple-element.69), channel_id=1, source_target_pairs={{0,8},{8,16},{16,24},{24,32},{32,40},{40,48},{48,56},{56,0},{1,9},... | collective-permute-start | bytes 147464 | tf_op jit(solution)/shard_map/ppermute | solution.py:294
  14.7 4.6 %collective-permute-start.29 = (bf16[16,16,96]{2,1,0:T(8,128)(2,1)S(1)}, bf16[16,16,96]{2,1,0:T(8,128)(2,1)S(1)}, u32[]{:S(2)}, u32[]{:S(2)}) collective-permute-start(bf16[16,16,96]{2,1,0:T(8,128)(2,1)S(1)} %get-tuple-element.70), channel_id=1, source_target_pairs={{0,1},{1,2},{2,3},{3,4},{4,5},{5,6},{6,7},{7,0},{8,9},{9,10},{10,1... | collective-permute-start | bytes 147464 | tf_op jit(solution)/shard_map/ppermute | solution.py:294
  19.8 5.8 %collective-permute-start.30 = (bf16[16,16,96]{2,1,0:T(8,128)(2,1)S(1)}, bf16[16,16,96]{2,1,0:T(8,128)(2,1)S(1)}, u32[]{:S(2)}, u32[]{:S(2)}) collective-permute-start(bf16[16,16,96]{2,1,0:T(8,128)(2,1)S(1)} %get-tuple-element.74), channel_id=1, source_target_pairs={{0,64},{64,128},{128,192},{192,0},{1,65},{65,129},{129,193},{193,1... | collective-permute-start | bytes 147464 | tf_op jit(solution)/shard_map/ppermute | solution.py:294
  20.0 8.5 %collective-permute-start.31 = (bf16[16,16,96]{2,1,0:T(8,128)(2,1)S(1)}, bf16[16,16,96]{2,1,0:T(8,128)(2,1)S(1)}, u32[]{:S(2)}, u32[]{:S(2)}) collective-permute-start(bf16[16,16,96]{2,1,0:T(8,128)(2,1)S(1)} %get-tuple-element.75), channel_id=1, source_target_pairs={{0,192},{64,0},{128,64},{192,128},{1,193},{65,1},{129,65},{193,129... | collective-permute-start | bytes 147464 | tf_op jit(solution)/shard_map/ppermute | solution.py:294
  22.6 5.9 %collective-permute-start.32 = (bf16[16,16,96]{2,1,0:T(8,128)(2,1)S(1)}, bf16[16,16,96]{2,1,0:T(8,128)(2,1)S(1)}, u32[]{:S(2)}, u32[]{:S(2)}) collective-permute-start(bf16[16,16,96]{2,1,0:T(8,128)(2,1)S(1)} %get-tuple-element.76), channel_id=1, source_target_pairs={{0,56},{8,0},{16,8},{24,16},{32,24},{40,32},{48,40},{56,48},{1,57}... | collective-permute-start | bytes 147464 | tf_op jit(solution)/shard_map/ppermute | solution.py:294
  24.7 3.8 %collective-permute-start.33 = (bf16[16,16,96]{2,1,0:T(8,128)(2,1)S(1)}, bf16[16,16,96]{2,1,0:T(8,128)(2,1)S(1)}, u32[]{:S(2)}, u32[]{:S(2)}) collective-permute-start(bf16[16,16,96]{2,1,0:T(8,128)(2,1)S(1)} %get-tuple-element.77), channel_id=1, source_target_pairs={{0,7},{1,0},{2,1},{3,2},{4,3},{5,4},{6,5},{7,6},{8,15},{9,8},{10,9... | collective-permute-start | bytes 147464 | tf_op jit(solution)/shard_map/ppermute | solution.py:294
  25.1 4.1 %collective-permute-start.34 = (bf16[16,16,96]{2,1,0:T(8,128)(2,1)S(1)}, bf16[16,16,96]{2,1,0:T(8,128)(2,1)S(1)}, u32[]{:S(2)}, u32[]{:S(2)}) collective-permute-start(bf16[16,16,96]{2,1,0:T(8,128)(2,1)S(1)} %get-tuple-element.78), channel_id=1, source_target_pairs={{0,8},{8,16},{16,24},{24,32},{32,40},{40,48},{48,56},{56,0},{1,9},... | collective-permute-start | bytes 147464 | tf_op jit(solution)/shard_map/ppermute | solution.py:294
  25.6 4.3 %collective-permute-start.35 = (bf16[16,16,96]{2,1,0:T(8,128)(2,1)S(1)}, bf16[16,16,96]{2,1,0:T(8,128)(2,1)S(1)}, u32[]{:S(2)}, u32[]{:S(2)}) collective-permute-start(bf16[16,16,96]{2,1,0:T(8,128)(2,1)S(1)} %get-tuple-element.79), channel_id=1, source_target_pairs={{0,1},{1,2},{2,3},{3,4},{4,5},{5,6},{6,7},{7,0},{8,9},{9,10},{10,1... | collective-permute-start | bytes 147464 | tf_op jit(solution)/shard_map/ppermute | solution.py:294
  30.3 6.8 %collective-permute-start.36 = (bf16[16,16,96]{2,1,0:T(8,128)(2,1)S(1)}, bf16[16,16,96]{2,1,0:T(8,128)(2,1)S(1)}, u32[]{:S(2)}, u32[]{:S(2)}) collective-permute-start(bf16[16,16,96]{2,1,0:T(8,128)(2,1)S(1)} %get-tuple-element.83), channel_id=1, source_target_pairs={{0,64},{64,128},{128,192},{192,0},{1,65},{65,129},{129,193},{193,1... | collective-permute-start | bytes 147464 | tf_op jit(solution)/shard_map/ppermute | solution.py:294
  30.4 9.9 %collective-permute-start.37 = (bf16[16,16,96]{2,1,0:T(8,128)(2,1)S(1)}, bf16[16,16,96]{2,1,0:T(8,128)(2,1)S(1)}, u32[]{:S(2)}, u32[]{:S(2)}) collective-permute-start(bf16[16,16,96]{2,1,0:T(8,128)(2,1)S(1)} %get-tuple-element.84), channel_id=1, source_target_pairs={{0,192},{64,0},{128,64},{192,128},{1,193},{65,1},{129,65},{193,129... | collective-permute-start | bytes 147464 | tf_op jit(solution)/shard_map/ppermute | solution.py:294
  33.1 7.2 %collective-permute-start.38 = (bf16[16,16,96]{2,1,0:T(8,128)(2,1)S(1)}, bf16[16,16,96]{2,1,0:T(8,128)(2,1)S(1)}, u32[]{:S(2)}, u32[]{:S(2)}) collective-permute-start(bf16[16,16,96]{2,1,0:T(8,128)(2,1)S(1)} %get-tuple-element.85), channel_id=1, source_target_pairs={{0,56},{8,0},{16,8},{24,16},{32,24},{40,32},{48,40},{56,48},{1,57}... | collective-permute-start | bytes 147464 | tf_op jit(solution)/shard_map/ppermute | solution.py:294
  37.2 3.9 %collective-permute-start.40 = (bf16[16,16,96]{2,1,0:T(8,128)(2,1)S(1)}, bf16[16,16,96]{2,1,0:T(8,128)(2,1)S(1)}, u32[]{:S(2)}, u32[]{:S(2)}) collective-permute-start(bf16[16,16,96]{2,1,0:T(8,128)(2,1)S(1)} %get-tuple-element.87), channel_id=1, source_target_pairs={{0,8},{8,16},{16,24},{24,32},{32,40},{40,48},{48,56},{56,0},{1,9},... | collective-permute-start | bytes 147464 | tf_op jit(solution)/shard_map/ppermute | solution.py:294
  37.2 4.3 %collective-permute-start.41 = (bf16[16,16,96]{2,1,0:T(8,128)(2,1)S(1)}, bf16[16,16,96]{2,1,0:T(8,128)(2,1)S(1)}, u32[]{:S(2)}, u32[]{:S(2)}) collective-permute-start(bf16[16,16,96]{2,1,0:T(8,128)(2,1)S(1)} %get-tuple-element.88), channel_id=1, source_target_pairs={{0,1},{1,2},{2,3},{3,4},{4,5},{5,6},{6,7},{7,0},{8,9},{9,10},{10,1... | collective-permute-start | bytes 147464 | tf_op jit(solution)/shard_map/ppermute | solution.py:294
  42.0 7.3 %collective-permute-start.42 = (bf16[16,16,96]{2,1,0:T(8,128)(2,1)S(1)}, bf16[16,16,96]{2,1,0:T(8,128)(2,1)S(1)}, u32[]{:S(2)}, u32[]{:S(2)}) collective-permute-start(bf16[16,16,96]{2,1,0:T(8,128)(2,1)S(1)} %get-tuple-element.92), channel_id=1, source_target_pairs={{0,64},{64,128},{128,192},{192,0},{1,65},{65,129},{129,193},{193,1... | collective-permute-start | bytes 147464 | tf_op jit(solution)/shard_map/ppermute | solution.py:294
  42.0 10.4 %collective-permute-start.43 = (bf16[16,16,96]{2,1,0:T(8,128)(2,1)S(1)}, bf16[16,16,96]{2,1,0:T(8,128)(2,1)S(1)}, u32[]{:S(2)}, u32[]{:S(2)}) collective-permute-start(bf16[16,16,96]{2,1,0:T(8,128)(2,1)S(1)} %get-tuple-element.93), channel_id=1, source_target_pairs={{0,192},{64,0},{128,64},{192,128},{1,193},{65,1},{129,65},{193,129... | collective-permute-start | bytes 147464 | tf_op jit(solution)/shard_map/ppermute | solution.py:294
  44.7 7.7 %collective-permute-start.44 = (bf16[16,16,96]{2,1,0:T(8,128)(2,1)S(1)}, bf16[16,16,96]{2,1,0:T(8,128)(2,1)S(1)}, u32[]{:S(2)}, u32[]{:S(2)}) collective-permute-start(bf16[16,16,96]{2,1,0:T(8,128)(2,1)S(1)} %get-tuple-element.94), channel_id=1, source_target_pairs={{0,56},{8,0},{16,8},{24,16},{32,24},{40,32},{48,40},{56,48},{1,57}... | collective-permute-start | bytes 147464 | tf_op jit(solution)/shard_map/ppermute | solution.py:294
  48.8 3.7 %collective-permute-start.45 = (bf16[16,16,96]{2,1,0:T(8,128)(2,1)S(1)}, bf16[16,16,96]{2,1,0:T(8,128)(2,1)S(1)}, u32[]{:S(2)}, u32[]{:S(2)}) collective-permute-start(bf16[16,16,96]{2,1,0:T(8,128)(2,1)S(1)} %get-tuple-element.95), channel_id=1, source_target_pairs={{0,7},{1,0},{2,1},{3,2},{4,3},{5,4},{6,5},{7,6},{8,15},{9,8},{10,9... | collective-permute-start | bytes 147464 | tf_op jit(solution)/shard_map/ppermute | solution.py:294
  49.2 3.9 %collective-permute-start.46 = (bf16[16,16,96]{2,1,0:T(8,128)(2,1)S(1)}, bf16[16,16,96]{2,1,0:T(8,128)(2,1)S(1)}, u32[]{:S(2)}, u32[]{:S(2)}) collective-permute-start(bf16[16,16,96]{2,1,0:T(8,128)(2,1)S(1)} %get-tuple-element.96), channel_id=1, source_target_pairs={{0,8},{8,16},{16,24},{24,32},{32,40},{40,48},{48,56},{56,0},{1,9},... | collective-permute-start | bytes 147464 | tf_op jit(solution)/shard_map/ppermute | solution.py:294
  49.2 4.3 %collective-permute-start.47 = (bf16[16,16,96]{2,1,0:T(8,128)(2,1)S(1)}, bf16[16,16,96]{2,1,0:T(8,128)(2,1)S(1)}, u32[]{:S(2)}, u32[]{:S(2)}) collective-permute-start(bf16[16,16,96]{2,1,0:T(8,128)(2,1)S(1)} %get-tuple-element.97), channel_id=1, source_target_pairs={{0,1},{1,2},{2,3},{3,4},{4,5},{5,6},{6,7},{7,0},{8,9},{9,10},{10,1... | collective-permute-start | bytes 147464 | tf_op jit(solution)/shard_map/ppermute | solution.py:294
  65.6 12.9 %all-to-all-start.1 = ((f32[32,1,240]{2,1,0:T(1,128)}), f32[32,1,240]{2,1,0:T(1,128)S(1)}, u32[]{:S(2)}, u32[]{:S(2)}) async-start(f32[32,1,240]{2,1,0:T(1,128)} %broadcast_in_dim.5), calls=%async_computation.1 | async-start | bytes 65536 | tf_op jit(solution)/shard_map/all_to_all | solution.py:377
  (2 other events, 7.0 us)

commit v2 on v1

--- a/solution.py
+++ b/solution.py
@@ -17,6 +17,7 @@
 EXTENT = (2, 2, 2, 4)
 SITES = 32
 FACE = 16
+BLOCKS = 12
 GROUPS = 8
 ENTRIES = [(i, j) for j in range(BASIS) for i in range(j + 1)]
 LANES = len(ENTRIES) * ROWS
@@ -80,7 +81,7 @@
                 wide_ref[group * 4 + y, source : source + 1] = piece[y : y + 1]
     for site in range(SITES):
         narrow_ref[site] = wide_ref[site].astype(jnp.bfloat16)
-    send_firsts(narrow_ref, firsts)
+    send_firsts(wide_ref, firsts)
     for copy in copies[1 : len(LAST_SLICES) + 1]:
         copy.wait()
     send_products(narrow_ref, held_ref, products)
@@ -88,21 +89,20 @@
         copy.wait()
 
 
-def send_firsts(narrow_ref, firsts):
+def in_face_order(direction, side):
+    return [c for c in CELLS if c[direction] == side]
+
+
+def send_firsts(wide_ref, firsts):
     for direction in range(3):
-        for cell in CELLS:
-            if cell[direction] == 0:
-                firsts[direction][on_face(cell, direction)] = narrow_ref[place(cell)]
+        packed(firsts[direction], [wide_ref[place(c)] for c in in_face_order(direction, 0)])
 
 
 def send_products(narrow_ref, links_ref, products):
     for direction in range(3):
-        for cell in CELLS:
-            if cell[direction] == 1:
-                site = place(cell)
-                spot = on_face(cell, direction)
-                product = dot(narrow_ref[site], links_ref[(direction + 1) * SITES + site], NN)
-                products[direction][spot] = product.astype(jnp.bfloat16)
+        sites = [place(c) for c in in_face_order(direction, 1)]
+        block = (direction + 1) * SITES
+        packed(products[direction], [dot(narrow_ref[s], links_ref[block + s], NN) for s in sites])
 
 
 def gram_rows(wides, last):
@@ -122,14 +122,16 @@
     wides, (part_ref, gram_ref), row_refs = refs[: step + 1], refs[step + 1 : step + 3], refs[step + 3 :]
     for cell in CELLS:
         site = place(cell)
-        total = dot(narrow_ref[site], links_ref[site], NT)
+        turned = dot(links_ref[site], narrow_ref[site], NT)
         for direction in range(4):
-            block = (direction + 1) * SITES
             if direction == 3 or cell[direction] == 0:
-                total -= dot(narrow_ref[place(moved(cell, direction, 1))], links_ref[block + site], NT)
+                ahead = narrow_ref[place(moved(cell, direction, 1))]
+                turned -= dot(links_ref[(direction + 1) * SITES + site], ahead, NT)
+        total = turned.T
+        for direction in range(4):
             if direction == 3 or cell[direction] == 1:
                 behind = place(moved(cell, direction, -1))
-                total -= dot(narrow_ref[behind], links_ref[block + behind], NN)
+                total -= dot(narrow_ref[behind], links_ref[(direction + 1) * SITES + behind], NN)
         if step:
             total -= SHIFT * wides[step - 1][site]
         part_ref[site] = total
@@ -140,39 +142,63 @@
 
 
 def middle_kernel(part_ref, links_ref, behind_ref, *refs):
-    ahead, next_ref = refs[0:3], refs[3]
+    ahead = [[v.astype(jnp.bfloat16) for v in unpacked(ref)] for ref in refs[0:3]]
+    behind, next_ref = unpacked(behind_ref), refs[3]
     for cell in CELLS:
         site = place(cell)
-        total = part_ref[site]
+        total, turned = part_ref[site], None
         for direction in range(3):
             if cell[direction] == 1:
                 link = links_ref[(direction + 1) * SITES + site]
-                total -= dot(ahead[direction][on_face(cell, direction)], link, NT)
+                term = dot(link, ahead[direction][on_face(cell, direction)], NT)
+                turned = term if turned is None else turned + term
+        if turned is not None:
+            total -= turned.T
         if cell[0] == 0:
-            total -= behind_ref[on_face(cell, 0)].astype(jnp.float32)
+            total -= behind[on_face(cell, 0)]
         next_ref[site] = total
 
 
 def joined(cell, part_ref, behind):
     total = part_ref[place(cell)]
-    for direction in (1, 2):
+    for direction, faces in zip((1, 2), behind):
         if cell[direction] == 0:
-            total -= behind[direction - 1][on_face(cell, direction)].astype(jnp.float32)
+            total -= faces[on_face(cell, direction)]
     return total
 
 
+def packed(ref, values):
+    for at in range(0, FACE, 4):
+        rest = values[at + 3]
+        for j in range(3):
+            block = jnp.concatenate([values[at + j][0:RHS], rest[4 * j : 4 * j + 4]], 0)
+            ref[at // 4 * 3 + j] = block.astype(jnp.bfloat16)
+
+
+def unpacked(ref):
+    values = []
+    for at in range(0, BLOCKS, 3):
+        blocks = [ref[at + j].astype(jnp.float32) for j in range(3)]
+        rest = jnp.concatenate([block[RHS:ROWS] for block in blocks] + [jnp.zeros((4, COMP), jnp.float32)], 0)
+        clear = jnp.zeros((ROWS - RHS, COMP), jnp.float32)
+        values += [jnp.concatenate([block[0:RHS], clear], 0) for block in blocks] + [rest]
+    return values
+
+
 def outer_kernel(part_ref, links_ref, *refs):
-    behind, (wide_ref, narrow_ref), faces = refs[0:2], refs[2:4], refs[4:10]
+    (wide_ref, narrow_ref), faces = refs[2:4], refs[4:10]
+    behind = [unpacked(ref) for ref in refs[0:2]]
     for cell in CELLS:
         total = joined(cell, part_ref, behind)
         wide_ref[place(cell)] = total
         narrow_ref[place(cell)] = total.astype(jnp.bfloat16)
-    send_firsts(narrow_ref, faces[0:3])
+    send_firsts(wide_ref, faces[0:3])
     send_products(narrow_ref, links_ref, faces[3:6])
 
 
 def last_kernel(part_ref, *refs):
-    behind, wides, grams = refs[0:2], refs[2:6], refs[6:10]
+    wides, grams = refs[2:6], refs[6:10]
+    behind = [unpacked(ref) for ref in refs[0:2]]
     rows_in, out_ref, wide_ref = refs[10:14], refs[14], refs[15]
     for cell in CELLS:
         wide_ref[place(cell)] = joined(cell, part_ref, behind)
@@ -202,7 +228,7 @@
     return sum(terms[1:], terms[0])
 
 
-def finish_kernel(gathered_ref, held_ref, solution_ref, residual_ref, sound_ref):
+def finish_kernel(gathered_ref, held_ref, solution_ref, residual_ref, unsound_ref):
     summed = lax.dot_general(
         gathered_ref[...], jnp.ones((SECOND_GROUP, 128), jnp.float32), TN,
         precision=lax.Precision.HIGHEST, preferred_element_type=jnp.float32,
@@ -246,7 +272,7 @@
     for v in (rho, out):
         length = combine(v, times_gram(v))
         margin = jnp.minimum(margin, length - KEEP_VECTOR * combine([a * a for a in v], [gram[i, i] for i in range(len(v))]))
-    sound_ref[0, 0] = jnp.where(jnp.min(margin) >= 0.0, 1, 0)
+    unsound_ref[0, 0] = jnp.where(jnp.min(margin) >= 0.0, 0, 1)
 
     lane = lax.broadcasted_iota(jnp.int32, (ROWS, 128), 1)
     packed = zero
@@ -268,7 +294,7 @@
     return jax.ShapeDtypeStruct(dims, dtype)
 
 
-FACES = [shape((FACE, ROWS, COMP), jnp.bfloat16)] * 3
+FACES = [shape((BLOCKS, ROWS, COMP), jnp.bfloat16)] * 3
 LINKS = shape((5 * SITES, COMP, COMP), jnp.bfloat16)
 ROW = shape((GROUPS, 4, RHS * COMP))
 WIDE = shape((SITES, ROWS, COMP))
@@ -377,13 +403,13 @@
         sums = lax.all_to_all(jnp.broadcast_to(sums, (members, LANES)), axes, 0, 0)
         if members == 8:
             sums = jnp.sum(sums, 0)
-    out, residual, sound = call(
+    out, residual, unsound = call(
         finish_kernel, "finish", [ROW, ROW, shape((1, 1), jnp.int32)], (sums, held)
     )
     return lax.cond(
-        sound[0, 0] > 0,
+        unsound[0, 0] > 0,
+        lambda: stepwise(right_side, link_blocks),
         lambda: (out.reshape(right_side.shape), residual.reshape(right_side.shape)),
-        lambda: stepwise(right_side, link_blocks),
     )
 
 

time: 81.4 us -> 78.6 us (0.966)
  Pallas kernels: 17.2 us -> 13.1 us
  waiting for transfers between devices: 12 us -> 13.9 us
    pallas_call x14, Pallas kernels: 17.2 us -> 13.1 us  [call(): pl.pallas_call(kernel, name=name, out_shape=out_shape, in_specs=[pl.Block...]
    ppermute x24, waiting for transfers between devices: 3.28 us -> 5.21 us  [shifted(): lax.ppermute(shard, axis, [(i, (i + by) % length) for i in range(length)])]
  transfers between devices with their start and end apart: 25 -> 25, of which waited for: 5 -> 8; matrix products, arithmetic and copies ran while one was open for 0% -> 0% of each run, Pallas kernels for 14% -> 9%
where the time goes in v2:
time: 78.6 us; the launch traced here: 78.4 us
  starting transfers between devices  37.9 us (48%)
  waiting for transfers between devices  13.9 us (18%)
  Pallas kernels  13.1 us (17%)
  blocking collectives  11 us (14%)
  between operations  1.5 us (2%)
    ppermute x24, starting transfers between devices, shifted(): lax.ppermute(shard, axis, [(i, (i + by) % length) for i in range(length)])  34 us
    pallas_call x14, Pallas kernels, call(): pl.pallas_call(kernel, name=name, out_shape=out_shape, in_specs=[pl.Block...  13.1 us
    all_to_all x1, blocking collectives, local(): sums = lax.all_to_all(jnp.broadcast_to(sums, (members, LANES)), axes, 0, 0)  11 us
    all_to_all x1, waiting for transfers between devices, local(): sums = lax.all_to_all(jnp.broadcast_to(sums, (members, LANES)), axes, 0, 0)  8.7 us
    ppermute x24, waiting for transfers between devices, shifted(): lax.ppermute(shard, axis, [(i, (i + by) % length) for i in range(length)])  5.21 us
    all_to_all x1, starting transfers between devices, local(): sums = lax.all_to_all(jnp.broadcast_to(sums, (members, LANES)), axes, 0, 0)  3.85 us
  transfers between devices with their start and end apart: 25, of which 8 were waited for; matrix products, arithmetic and copies ran while one was open for 0% of the time, Pallas kernels for 9%

profile of v2, /device:TPU:1, one launch (start us, length us, event | category | flops | bytes accessed | tf_op | source)
XLA Modules:
  0.0 78.4 jit_solution(17670596680988115197)
XLA Ops:
  0.6 2.3 %begin.1 = (f32[32,16,96]{2,1,0:T(8,128)S(1)}, bf16[32,16,96]{2,1,0:T(8,128)(2,1)S(1)}, bf16[12,16,96]{2,1,0:T(8,128)(2,1)S(1)}, bf16[12,16,96]{2,1,0:T(8,128)(2...) custom-call(f32[8,4,1152]{2,1,0:T(4,128)} %bitcast.116, ...), custom_call_target="tpu_custom_call" | custom-call | tf_op jit(solution)/shard_map/begin/pallas_call | solution.py:307
  2.9 2.2 %collective-permute-start.24 = (bf16[12,16,96]{2,1,0:T(8,128)(2,1)S(1)}, bf16[12,16,96]{2,1,0:T(8,128)(2,1)S(1)}, u32[]{:S(2)}, u32[]{:S(2)}) collective-permute-start(bf16[12,16,96]{2,1,0:T(8,128)(2,1)S(1)} %get-tuple-element.65), channel_id=1, source_target_pairs={{0,64},{64,128},{128,192},{192,0},{1,65},{65,129},{129,193},{193,1... | collective-permute-start | bytes 110600 | tf_op jit(solution)/shard_map/ppermute | solution.py:320
  5.2 1.5 %collective-permute-start.25 = (bf16[12,16,96]{2,1,0:T(8,128)(2,1)S(1)}, bf16[12,16,96]{2,1,0:T(8,128)(2,1)S(1)}, u32[]{:S(2)}, u32[]{:S(2)}) collective-permute-start(bf16[12,16,96]{2,1,0:T(8,128)(2,1)S(1)} %get-tuple-element.66), channel_id=1, source_target_pairs={{0,192},{64,0},{128,64},{192,128},{1,193},{65,1},{129,65},{193,129... | collective-permute-start | bytes 110600 | tf_op jit(solution)/shard_map/ppermute | solution.py:320
  6.7 2.8 %collective-permute-start.26 = (bf16[12,16,96]{2,1,0:T(8,128)(2,1)S(1)}, bf16[12,16,96]{2,1,0:T(8,128)(2,1)S(1)}, u32[]{:S(2)}, u32[]{:S(2)}) collective-permute-start(bf16[12,16,96]{2,1,0:T(8,128)(2,1)S(1)} %get-tuple-element.67), channel_id=1, source_target_pairs={{0,56},{8,0},{16,8},{24,16},{32,24},{40,32},{48,40},{56,48},{1,57}... | collective-permute-start | bytes 110600 | tf_op jit(solution)/shard_map/ppermute | solution.py:320
  9.5 3.8 %collective-permute-start.27 = (bf16[12,16,96]{2,1,0:T(8,128)(2,1)S(1)}, bf16[12,16,96]{2,1,0:T(8,128)(2,1)S(1)}, u32[]{:S(2)}, u32[]{:S(2)}) collective-permute-start(bf16[12,16,96]{2,1,0:T(8,128)(2,1)S(1)} %get-tuple-element.68), channel_id=1, source_target_pairs={{0,7},{1,0},{2,1},{3,2},{4,3},{5,4},{6,5},{7,6},{8,15},{9,8},{10,9... | collective-permute-start | bytes 110600 | tf_op jit(solution)/shard_map/ppermute | solution.py:320
  13.3 1.4 %collective-permute-start.28 = (bf16[12,16,96]{2,1,0:T(8,128)(2,1)S(1)}, bf16[12,16,96]{2,1,0:T(8,128)(2,1)S(1)}, u32[]{:S(2)}, u32[]{:S(2)}) collective-permute-start(bf16[12,16,96]{2,1,0:T(8,128)(2,1)S(1)} %get-tuple-element.69), channel_id=1, source_target_pairs={{0,8},{8,16},{16,24},{24,32},{32,40},{40,48},{48,56},{56,0},{1,9},... | collective-permute-start | bytes 110600 | tf_op jit(solution)/shard_map/ppermute | solution.py:320
  14.7 1.3 %inner0.1 = (f32[32,16,96]{2,1,0:T(8,128)S(1)}, f32[1,16,96]{2,1,0:T(8,128)S(1)}) custom-call(bf16[32,16,96]{2,1,0:T(8,128)(2,1)S(1)} %get-tuple-element.61.narrow_ref, bf16[160,96,96]{2,1,0:T(8,128)(2,1)S(1)} %get-tuple-element.62.links_ref, f32[32,16,96]{2,1,0:T(8,128)S(1)} %get-tuple-element.63.refs_0_.refs_2_), custom_call_target="tpu_custom_call" | custom-call | tf_op jit(solution)/shard_map/inner0/pallas_call | solution.py:307
  16.6 2.3 %collective-permute-done.29.refs_1_ = bf16[12,16,96]{2,1,0:T(8,128)(2,1)S(1)} collective-permute-done((bf16[12,16,96]{2,1,0:T(8,128)(2,1)S(1)}, bf16[12,16,96]{2,1,0:T(8,128)(2,1)S(1)}, u32[]{:S(2)}, u32[]{:S(2)}) %collective-permute-start.29) | collective-permute-done | bytes 36896 | tf_op jit(solution)/shard_map/ppermute | solution.py:320
  19.8 2.3 %collective-permute-start.31 = (bf16[12,16,96]{2,1,0:T(8,128)(2,1)S(1)}, bf16[12,16,96]{2,1,0:T(8,128)(2,1)S(1)}, u32[]{:S(2)}, u32[]{:S(2)}) collective-permute-start(bf16[12,16,96]{2,1,0:T(8,128)(2,1)S(1)} %get-tuple-element.75), channel_id=1, source_target_pairs={{0,192},{64,0},{128,64},{192,128},{1,193},{65,1},{129,65},{193,129... | collective-permute-start | bytes 110600 | tf_op jit(solution)/shard_map/ppermute | solution.py:320
  22.1 2.4 %collective-permute-start.32 = (bf16[12,16,96]{2,1,0:T(8,128)(2,1)S(1)}, bf16[12,16,96]{2,1,0:T(8,128)(2,1)S(1)}, u32[]{:S(2)}, u32[]{:S(2)}) collective-permute-start(bf16[12,16,96]{2,1,0:T(8,128)(2,1)S(1)} %get-tuple-element.76), channel_id=1, source_target_pairs={{0,56},{8,0},{16,8},{24,16},{32,24},{40,32},{48,40},{56,48},{1,57}... | collective-permute-start | bytes 110600 | tf_op jit(solution)/shard_map/ppermute | solution.py:320
  24.8 1.2 %collective-permute-start.35 = (bf16[12,16,96]{2,1,0:T(8,128)(2,1)S(1)}, bf16[12,16,96]{2,1,0:T(8,128)(2,1)S(1)}, u32[]{:S(2)}, u32[]{:S(2)}) collective-permute-start(bf16[12,16,96]{2,1,0:T(8,128)(2,1)S(1)} %get-tuple-element.79), channel_id=1, source_target_pairs={{0,1},{1,2},{2,3},{3,4},{4,5},{5,6},{6,7},{7,0},{8,9},{9,10},{10,1... | collective-permute-start | bytes 110600 | tf_op jit(solution)/shard_map/ppermute | solution.py:320
  26.0 1.3 %inner1.1 = (f32[32,16,96]{2,1,0:T(8,128)S(1)}, f32[2,16,96]{2,1,0:T(8,128)S(1)}, f32[8,4,1152]{2,1,0:T(4,128)S(1)}) custom-call(bf16[32,16,96]{2,1,0:T(8,128)(2,1)S(1)} %get-tuple-element.71.narrow_ref, bf16[160,96,96]{2,1,0:T(8,128)(2,1)S(1)} %get-tuple-element.62.links_ref, f32[32,16,96]{2,1,0:T(8,128)S(1)} %get-tuple-element.63.refs_0_.refs_2_, ...), custom_call_target="tpu_custom_call" | custom-call | tf_op jit(solution)/shard_map/inner1/pallas_call | solution.py:307
  29.5 2.7 %collective-permute-start.37 = (bf16[12,16,96]{2,1,0:T(8,128)(2,1)S(1)}, bf16[12,16,96]{2,1,0:T(8,128)(2,1)S(1)}, u32[]{:S(2)}, u32[]{:S(2)}) collective-permute-start(bf16[12,16,96]{2,1,0:T(8,128)(2,1)S(1)} %get-tuple-element.84), channel_id=1, source_target_pairs={{0,192},{64,0},{128,64},{192,128},{1,193},{65,1},{129,65},{193,129... | collective-permute-start | bytes 110600 | tf_op jit(solution)/shard_map/ppermute | solution.py:320
  32.1 3.5 %collective-permute-start.38 = (bf16[12,16,96]{2,1,0:T(8,128)(2,1)S(1)}, bf16[12,16,96]{2,1,0:T(8,128)(2,1)S(1)}, u32[]{:S(2)}, u32[]{:S(2)}) collective-permute-start(bf16[12,16,96]{2,1,0:T(8,128)(2,1)S(1)} %get-tuple-element.85), channel_id=1, source_target_pairs={{0,56},{8,0},{16,8},{24,16},{32,24},{40,32},{48,40},{56,48},{1,57}... | collective-permute-start | bytes 110600 | tf_op jit(solution)/shard_map/ppermute | solution.py:320
  35.8 1.4 %collective-permute-start.41 = (bf16[12,16,96]{2,1,0:T(8,128)(2,1)S(1)}, bf16[12,16,96]{2,1,0:T(8,128)(2,1)S(1)}, u32[]{:S(2)}, u32[]{:S(2)}) collective-permute-start(bf16[12,16,96]{2,1,0:T(8,128)(2,1)S(1)} %get-tuple-element.88), channel_id=1, source_target_pairs={{0,1},{1,2},{2,3},{3,4},{4,5},{5,6},{6,7},{7,0},{8,9},{9,10},{10,1... | collective-permute-start | bytes 110600 | tf_op jit(solution)/shard_map/ppermute | solution.py:320
  37.1 1.3 %inner2.1 = (f32[32,16,96]{2,1,0:T(8,128)S(1)}, f32[3,16,96]{2,1,0:T(8,128)S(1)}, f32[8,4,1152]{2,1,0:T(4,128)S(1)}) custom-call(bf16[32,16,96]{2,1,0:T(8,128)(2,1)S(1)} %get-tuple-element.80.narrow_ref, bf16[160,96,96]{2,1,0:T(8,128)(2,1)S(1)} %get-tuple-element.62.links_ref, f32[32,16,96]{2,1,0:T(8,128)S(1)} %get-tuple-element.63.refs_0_.refs_2_, ...), custom_call_target="tpu_custom_call" | custom-call | tf_op jit(solution)/shard_map/inner2/pallas_call | solution.py:307
  40.5 2.7 %collective-permute-start.43 = (bf16[12,16,96]{2,1,0:T(8,128)(2,1)S(1)}, bf16[12,16,96]{2,1,0:T(8,128)(2,1)S(1)}, u32[]{:S(2)}, u32[]{:S(2)}) collective-permute-start(bf16[12,16,96]{2,1,0:T(8,128)(2,1)S(1)} %get-tuple-element.93), channel_id=1, source_target_pairs={{0,192},{64,0},{128,64},{192,128},{1,193},{65,1},{129,65},{193,129... | collective-permute-start | bytes 110600 | tf_op jit(solution)/shard_map/ppermute | solution.py:320
  43.1 3.6 %collective-permute-start.44 = (bf16[12,16,96]{2,1,0:T(8,128)(2,1)S(1)}, bf16[12,16,96]{2,1,0:T(8,128)(2,1)S(1)}, u32[]{:S(2)}, u32[]{:S(2)}) collective-permute-start(bf16[12,16,96]{2,1,0:T(8,128)(2,1)S(1)} %get-tuple-element.94), channel_id=1, source_target_pairs={{0,56},{8,0},{16,8},{24,16},{32,24},{40,32},{48,40},{56,48},{1,57}... | collective-permute-start | bytes 110600 | tf_op jit(solution)/shard_map/ppermute | solution.py:320
  46.8 1.5 %collective-permute-start.47 = (bf16[12,16,96]{2,1,0:T(8,128)(2,1)S(1)}, bf16[12,16,96]{2,1,0:T(8,128)(2,1)S(1)}, u32[]{:S(2)}, u32[]{:S(2)}) collective-permute-start(bf16[12,16,96]{2,1,0:T(8,128)(2,1)S(1)} %get-tuple-element.97), channel_id=1, source_target_pairs={{0,1},{1,2},{2,3},{3,4},{4,5},{5,6},{6,7},{7,0},{8,9},{9,10},{10,1... | collective-permute-start | bytes 110600 | tf_op jit(solution)/shard_map/ppermute | solution.py:320
  48.3 1.3 %inner3.1 = (f32[32,16,96]{2,1,0:T(8,128)S(1)}, f32[4,16,96]{2,1,0:T(8,128)S(1)}, f32[8,4,1152]{2,1,0:T(4,128)S(1)}) custom-call(bf16[32,16,96]{2,1,0:T(8,128)(2,1)S(1)} %get-tuple-element.89.narrow_ref, bf16[160,96,96]{2,1,0:T(8,128)(2,1)S(1)} %get-tuple-element.62.links_ref, f32[32,16,96]{2,1,0:T(8,128)S(1)} %get-tuple-element.63.refs_0_.refs_2_, ...), custom_call_target="tpu_custom_call" | custom-call | tf_op jit(solution)/shard_map/inner3/pallas_call | solution.py:307
  51.5 11.0 %all_to_all.14 = f32[8,1,240]{2,1,0:T(1,128)S(1)} all-to-all(f32[8,1,240]{2,1,0:T(1,128)S(1)} %broadcast_in_dim.4), channel_id=1, replica_groups=mesh['ta'=4,'gz'=8,'xy'=8] {'gz'}, dimensions={0} | all-to-all | bytes 15360 | tf_op jit(solution)/shard_map/all_to_all | solution.py:403
  63.2 3.9 %all-to-all-start.1 = ((f32[32,1,240]{2,1,0:T(1,128)}), f32[32,1,240]{2,1,0:T(1,128)S(1)}, u32[]{:S(2)}, u32[]{:S(2)}) async-start(f32[32,1,240]{2,1,0:T(1,128)} %broadcast_in_dim.5), calls=%async_computation.1 | async-start | bytes 65536 | tf_op jit(solution)/shard_map/all_to_all | solution.py:403
  67.0 8.7 %all-to-all-done.1 = f32[32,1,240]{2,1,0:T(1,128)S(1)} async-done(((f32[32,1,240]{2,1,0:T(1,128)}), f32[32,1,240]{2,1,0:T(1,128)S(1)}, u32[]{:S(2)}, u32[]{:S(2)}) %all-to-all-start.1) | async-done | bytes 30752 | tf_op jit(solution)/shard_map/all_to_all | solution.py:403
  75.7 1.7 %finish.1 = (f32[8,4,1152]{2,1,0:T(4,128)}, f32[8,4,1152]{2,1,0:T(4,128)}, s32[1,1]{1,0:T(1,128)}) custom-call(f32[32,240]{1,0:T(8,128)S(1)} %bitcast.114, f32[41,4,1152]{2,1,0:T(4,128)S(1)} %last.1.held_ref), custom_call_target="tpu_custom_call" | custom-call | tf_op jit(solution)/shard_map/finish/pallas_call | solution.py:307
  (49 shorter events, 8.7 us)
Async XLA Ops:
  2.9 11.8 %collective-permute-start.24 = (bf16[12,16,96]{2,1,0:T(8,128)(2,1)S(1)}, bf16[12,16,96]{2,1,0:T(8,128)(2,1)S(1)}, u32[]{:S(2)}, u32[]{:S(2)}) collective-permute-start(bf16[12,16,96]{2,1,0:T(8,128)(2,1)S(1)} %get-tuple-element.65), channel_id=1, source_target_pairs={{0,64},{64,128},{128,192},{192,0},{1,65},{65,129},{129,193},{193,1... | collective-permute-start | bytes 110600 | tf_op jit(solution)/shard_map/ppermute | solution.py:320
  5.2 10.9 %collective-permute-start.25 = (bf16[12,16,96]{2,1,0:T(8,128)(2,1)S(1)}, bf16[12,16,96]{2,1,0:T(8,128)(2,1)S(1)}, u32[]{:S(2)}, u32[]{:S(2)}) collective-permute-start(bf16[12,16,96]{2,1,0:T(8,128)(2,1)S(1)} %get-tuple-element.66), channel_id=1, source_target_pairs={{0,192},{64,0},{128,64},{192,128},{1,193},{65,1},{129,65},{193,129... | collective-permute-start | bytes 110600 | tf_op jit(solution)/shard_map/ppermute | solution.py:320
  6.7 9.4 %collective-permute-start.26 = (bf16[12,16,96]{2,1,0:T(8,128)(2,1)S(1)}, bf16[12,16,96]{2,1,0:T(8,128)(2,1)S(1)}, u32[]{:S(2)}, u32[]{:S(2)}) collective-permute-start(bf16[12,16,96]{2,1,0:T(8,128)(2,1)S(1)} %get-tuple-element.67), channel_id=1, source_target_pairs={{0,56},{8,0},{16,8},{24,16},{32,24},{40,32},{48,40},{56,48},{1,57}... | collective-permute-start | bytes 110600 | tf_op jit(solution)/shard_map/ppermute | solution.py:320
  9.5 6.5 %collective-permute-start.27 = (bf16[12,16,96]{2,1,0:T(8,128)(2,1)S(1)}, bf16[12,16,96]{2,1,0:T(8,128)(2,1)S(1)}, u32[]{:S(2)}, u32[]{:S(2)}) collective-permute-start(bf16[12,16,96]{2,1,0:T(8,128)(2,1)S(1)} %get-tuple-element.68), channel_id=1, source_target_pairs={{0,7},{1,0},{2,1},{3,2},{4,3},{5,4},{6,5},{7,6},{8,15},{9,8},{10,9... | collective-permute-start | bytes 110600 | tf_op jit(solution)/shard_map/ppermute | solution.py:320
  13.3 3.2 %collective-permute-start.28 = (bf16[12,16,96]{2,1,0:T(8,128)(2,1)S(1)}, bf16[12,16,96]{2,1,0:T(8,128)(2,1)S(1)}, u32[]{:S(2)}, u32[]{:S(2)}) collective-permute-start(bf16[12,16,96]{2,1,0:T(8,128)(2,1)S(1)} %get-tuple-element.69), channel_id=1, source_target_pairs={{0,8},{8,16},{16,24},{24,32},{32,40},{40,48},{48,56},{56,0},{1,9},... | collective-permute-start | bytes 110600 | tf_op jit(solution)/shard_map/ppermute | solution.py:320
  14.7 4.2 %collective-permute-start.29 = (bf16[12,16,96]{2,1,0:T(8,128)(2,1)S(1)}, bf16[12,16,96]{2,1,0:T(8,128)(2,1)S(1)}, u32[]{:S(2)}, u32[]{:S(2)}) collective-permute-start(bf16[12,16,96]{2,1,0:T(8,128)(2,1)S(1)} %get-tuple-element.70), channel_id=1, source_target_pairs={{0,1},{1,2},{2,3},{3,4},{4,5},{5,6},{6,7},{7,0},{8,9},{9,10},{10,1... | collective-permute-start | bytes 110600 | tf_op jit(solution)/shard_map/ppermute | solution.py:320
  19.3 5.4 %collective-permute-start.30 = (bf16[12,16,96]{2,1,0:T(8,128)(2,1)S(1)}, bf16[12,16,96]{2,1,0:T(8,128)(2,1)S(1)}, u32[]{:S(2)}, u32[]{:S(2)}) collective-permute-start(bf16[12,16,96]{2,1,0:T(8,128)(2,1)S(1)} %get-tuple-element.74), channel_id=1, source_target_pairs={{0,64},{64,128},{128,192},{192,0},{1,65},{65,129},{129,193},{193,1... | collective-permute-start | bytes 110600 | tf_op jit(solution)/shard_map/ppermute | solution.py:320
  19.8 7.5 %collective-permute-start.31 = (bf16[12,16,96]{2,1,0:T(8,128)(2,1)S(1)}, bf16[12,16,96]{2,1,0:T(8,128)(2,1)S(1)}, u32[]{:S(2)}, u32[]{:S(2)}) collective-permute-start(bf16[12,16,96]{2,1,0:T(8,128)(2,1)S(1)} %get-tuple-element.75), channel_id=1, source_target_pairs={{0,192},{64,0},{128,64},{192,128},{1,193},{65,1},{129,65},{193,129... | collective-permute-start | bytes 110600 | tf_op jit(solution)/shard_map/ppermute | solution.py:320
  22.1 5.2 %collective-permute-start.32 = (bf16[12,16,96]{2,1,0:T(8,128)(2,1)S(1)}, bf16[12,16,96]{2,1,0:T(8,128)(2,1)S(1)}, u32[]{:S(2)}, u32[]{:S(2)}) collective-permute-start(bf16[12,16,96]{2,1,0:T(8,128)(2,1)S(1)} %get-tuple-element.76), channel_id=1, source_target_pairs={{0,56},{8,0},{16,8},{24,16},{32,24},{40,32},{48,40},{56,48},{1,57}... | collective-permute-start | bytes 110600 | tf_op jit(solution)/shard_map/ppermute | solution.py:320
  24.5 2.9 %collective-permute-start.33 = (bf16[12,16,96]{2,1,0:T(8,128)(2,1)S(1)}, bf16[12,16,96]{2,1,0:T(8,128)(2,1)S(1)}, u32[]{:S(2)}, u32[]{:S(2)}) collective-permute-start(bf16[12,16,96]{2,1,0:T(8,128)(2,1)S(1)} %get-tuple-element.77), channel_id=1, source_target_pairs={{0,7},{1,0},{2,1},{3,2},{4,3},{5,4},{6,5},{7,6},{8,15},{9,8},{10,9... | collective-permute-start | bytes 110600 | tf_op jit(solution)/shard_map/ppermute | solution.py:320
  24.8 3.2 %collective-permute-start.34 = (bf16[12,16,96]{2,1,0:T(8,128)(2,1)S(1)}, bf16[12,16,96]{2,1,0:T(8,128)(2,1)S(1)}, u32[]{:S(2)}, u32[]{:S(2)}) collective-permute-start(bf16[12,16,96]{2,1,0:T(8,128)(2,1)S(1)} %get-tuple-element.78), channel_id=1, source_target_pairs={{0,8},{8,16},{16,24},{24,32},{32,40},{40,48},{48,56},{56,0},{1,9},... | collective-permute-start | bytes 110600 | tf_op jit(solution)/shard_map/ppermute | solution.py:320
  24.8 4.2 %collective-permute-start.35 = (bf16[12,16,96]{2,1,0:T(8,128)(2,1)S(1)}, bf16[12,16,96]{2,1,0:T(8,128)(2,1)S(1)}, u32[]{:S(2)}, u32[]{:S(2)}) collective-permute-start(bf16[12,16,96]{2,1,0:T(8,128)(2,1)S(1)} %get-tuple-element.79), channel_id=1, source_target_pairs={{0,1},{1,2},{2,3},{3,4},{4,5},{5,6},{6,7},{7,0},{8,9},{9,10},{10,1... | collective-permute-start | bytes 110600 | tf_op jit(solution)/shard_map/ppermute | solution.py:320
  29.4 6.4 %collective-permute-start.36 = (bf16[12,16,96]{2,1,0:T(8,128)(2,1)S(1)}, bf16[12,16,96]{2,1,0:T(8,128)(2,1)S(1)}, u32[]{:S(2)}, u32[]{:S(2)}) collective-permute-start(bf16[12,16,96]{2,1,0:T(8,128)(2,1)S(1)} %get-tuple-element.83), channel_id=1, source_target_pairs={{0,64},{64,128},{128,192},{192,0},{1,65},{65,129},{129,193},{193,1... | collective-permute-start | bytes 110600 | tf_op jit(solution)/shard_map/ppermute | solution.py:320
  29.5 9.0 %collective-permute-start.37 = (bf16[12,16,96]{2,1,0:T(8,128)(2,1)S(1)}, bf16[12,16,96]{2,1,0:T(8,128)(2,1)S(1)}, u32[]{:S(2)}, u32[]{:S(2)}) collective-permute-start(bf16[12,16,96]{2,1,0:T(8,128)(2,1)S(1)} %get-tuple-element.84), channel_id=1, source_target_pairs={{0,192},{64,0},{128,64},{192,128},{1,193},{65,1},{129,65},{193,129... | collective-permute-start | bytes 110600 | tf_op jit(solution)/shard_map/ppermute | solution.py:320
  32.1 6.3 %collective-permute-start.38 = (bf16[12,16,96]{2,1,0:T(8,128)(2,1)S(1)}, bf16[12,16,96]{2,1,0:T(8,128)(2,1)S(1)}, u32[]{:S(2)}, u32[]{:S(2)}) collective-permute-start(bf16[12,16,96]{2,1,0:T(8,128)(2,1)S(1)} %get-tuple-element.85), channel_id=1, source_target_pairs={{0,56},{8,0},{16,8},{24,16},{32,24},{40,32},{48,40},{56,48},{1,57}... | collective-permute-start | bytes 110600 | tf_op jit(solution)/shard_map/ppermute | solution.py:320
  35.6 2.9 %collective-permute-start.39 = (bf16[12,16,96]{2,1,0:T(8,128)(2,1)S(1)}, bf16[12,16,96]{2,1,0:T(8,128)(2,1)S(1)}, u32[]{:S(2)}, u32[]{:S(2)}) collective-permute-start(bf16[12,16,96]{2,1,0:T(8,128)(2,1)S(1)} %get-tuple-element.86), channel_id=1, source_target_pairs={{0,7},{1,0},{2,1},{3,2},{4,3},{5,4},{6,5},{7,6},{8,15},{9,8},{10,9... | collective-permute-start | bytes 110600 | tf_op jit(solution)/shard_map/ppermute | solution.py:320
  35.8 3.3 %collective-permute-start.40 = (bf16[12,16,96]{2,1,0:T(8,128)(2,1)S(1)}, bf16[12,16,96]{2,1,0:T(8,128)(2,1)S(1)}, u32[]{:S(2)}, u32[]{:S(2)}) collective-permute-start(bf16[12,16,96]{2,1,0:T(8,128)(2,1)S(1)} %get-tuple-element.87), channel_id=1, source_target_pairs={{0,8},{8,16},{16,24},{24,32},{32,40},{40,48},{48,56},{56,0},{1,9},... | collective-permute-start | bytes 110600 | tf_op jit(solution)/shard_map/ppermute | solution.py:320
  35.8 4.2 %collective-permute-start.41 = (bf16[12,16,96]{2,1,0:T(8,128)(2,1)S(1)}, bf16[12,16,96]{2,1,0:T(8,128)(2,1)S(1)}, u32[]{:S(2)}, u32[]{:S(2)}) collective-permute-start(bf16[12,16,96]{2,1,0:T(8,128)(2,1)S(1)} %get-tuple-element.88), channel_id=1, source_target_pairs={{0,1},{1,2},{2,3},{3,4},{4,5},{5,6},{6,7},{7,0},{8,9},{9,10},{10,1... | collective-permute-start | bytes 110600 | tf_op jit(solution)/shard_map/ppermute | solution.py:320
  40.4 6.4 %collective-permute-start.42 = (bf16[12,16,96]{2,1,0:T(8,128)(2,1)S(1)}, bf16[12,16,96]{2,1,0:T(8,128)(2,1)S(1)}, u32[]{:S(2)}, u32[]{:S(2)}) collective-permute-start(bf16[12,16,96]{2,1,0:T(8,128)(2,1)S(1)} %get-tuple-element.92), channel_id=1, source_target_pairs={{0,64},{64,128},{128,192},{192,0},{1,65},{65,129},{129,193},{193,1... | collective-permute-start | bytes 110600 | tf_op jit(solution)/shard_map/ppermute | solution.py:320
  40.5 9.2 %collective-permute-start.43 = (bf16[12,16,96]{2,1,0:T(8,128)(2,1)S(1)}, bf16[12,16,96]{2,1,0:T(8,128)(2,1)S(1)}, u32[]{:S(2)}, u32[]{:S(2)}) collective-permute-start(bf16[12,16,96]{2,1,0:T(8,128)(2,1)S(1)} %get-tuple-element.93), channel_id=1, source_target_pairs={{0,192},{64,0},{128,64},{192,128},{1,193},{65,1},{129,65},{193,129... | collective-permute-start | bytes 110600 | tf_op jit(solution)/shard_map/ppermute | solution.py:320
  43.1 6.5 %collective-permute-start.44 = (bf16[12,16,96]{2,1,0:T(8,128)(2,1)S(1)}, bf16[12,16,96]{2,1,0:T(8,128)(2,1)S(1)}, u32[]{:S(2)}, u32[]{:S(2)}) collective-permute-start(bf16[12,16,96]{2,1,0:T(8,128)(2,1)S(1)} %get-tuple-element.94), channel_id=1, source_target_pairs={{0,56},{8,0},{16,8},{24,16},{32,24},{40,32},{48,40},{56,48},{1,57}... | collective-permute-start | bytes 110600 | tf_op jit(solution)/shard_map/ppermute | solution.py:320
  46.8 3.4 %collective-permute-start.46 = (bf16[12,16,96]{2,1,0:T(8,128)(2,1)S(1)}, bf16[12,16,96]{2,1,0:T(8,128)(2,1)S(1)}, u32[]{:S(2)}, u32[]{:S(2)}) collective-permute-start(bf16[12,16,96]{2,1,0:T(8,128)(2,1)S(1)} %get-tuple-element.96), channel_id=1, source_target_pairs={{0,8},{8,16},{16,24},{24,32},{32,40},{40,48},{48,56},{56,0},{1,9},... | collective-permute-start | bytes 110600 | tf_op jit(solution)/shard_map/ppermute | solution.py:320
  46.8 4.2 %collective-permute-start.47 = (bf16[12,16,96]{2,1,0:T(8,128)(2,1)S(1)}, bf16[12,16,96]{2,1,0:T(8,128)(2,1)S(1)}, u32[]{:S(2)}, u32[]{:S(2)}) collective-permute-start(bf16[12,16,96]{2,1,0:T(8,128)(2,1)S(1)} %get-tuple-element.97), channel_id=1, source_target_pairs={{0,1},{1,2},{2,3},{3,4},{4,5},{5,6},{6,7},{7,0},{8,9},{9,10},{10,1... | collective-permute-start | bytes 110600 | tf_op jit(solution)/shard_map/ppermute | solution.py:320
  63.2 12.6 %all-to-all-start.1 = ((f32[32,1,240]{2,1,0:T(1,128)}), f32[32,1,240]{2,1,0:T(1,128)S(1)}, u32[]{:S(2)}, u32[]{:S(2)}) async-start(f32[32,1,240]{2,1,0:T(1,128)} %broadcast_in_dim.5), calls=%async_computation.1 | async-start | bytes 65536 | tf_op jit(solution)/shard_map/all_to_all | solution.py:403
  (2 other events, 5.7 us)

commit v3 on v2

--- a/solution.py
+++ b/solution.py
@@ -25,8 +25,8 @@
 SECOND_GROUP = 32
 AXES = ("ta", "gz", "xy")
 ORDER = (0, 2, 1)
-KEEP_SQUARE = 1e-4
-KEEP_VECTOR = 0.1
+KEEP_SQUARE = 1e-2
+KEEP_VECTOR = 0.4
 
 LAST_SLICES = [(SITES + 16, 16)]
 LAST_SLICES += [(2 * SITES + t * 16 + 8, 8) for t in range(2)]

time: 78.6 us -> 78.6 us (level)
  no operation moved by 1% of the time
where the time goes in v3:
time: 78.6 us; the launch traced here: 78.4 us
  starting transfers between devices  37.9 us (48%)
  waiting for transfers between devices  13.9 us (18%)
  Pallas kernels  13.1 us (17%)
  blocking collectives  11 us (14%)
  between operations  1.5 us (2%)
    ppermute x24, starting transfers between devices, shifted(): lax.ppermute(shard, axis, [(i, (i + by) % length) for i in range(length)])  34 us
    pallas_call x14, Pallas kernels, call(): pl.pallas_call(kernel, name=name, out_shape=out_shape, in_specs=[pl.Block...  13.1 us
    all_to_all x1, blocking collectives, local(): sums = lax.all_to_all(jnp.broadcast_to(sums, (members, LANES)), axes, 0, 0)  11 us
    all_to_all x1, waiting for transfers between devices, local(): sums = lax.all_to_all(jnp.broadcast_to(sums, (members, LANES)), axes, 0, 0)  8.7 us
    ppermute x24, waiting for transfers between devices, shifted(): lax.ppermute(shard, axis, [(i, (i + by) % length) for i in range(length)])  5.21 us
    all_to_all x1, starting transfers between devices, local(): sums = lax.all_to_all(jnp.broadcast_to(sums, (members, LANES)), axes, 0, 0)  3.85 us
  transfers between devices with their start and end apart: 25, of which 8 were waited for; matrix products, arithmetic and copies ran while one was open for 0% of the time, Pallas kernels for 9%

profile of v3, /device:TPU:1, one launch (start us, length us, event | category | flops | bytes accessed | tf_op | source)
XLA Modules:
  0.0 78.4 jit_solution(17879526176431027789)
XLA Ops:
  0.6 2.3 %begin.1 = (f32[32,16,96]{2,1,0:T(8,128)S(1)}, bf16[32,16,96]{2,1,0:T(8,128)(2,1)S(1)}, bf16[12,16,96]{2,1,0:T(8,128)(2,1)S(1)}, bf16[12,16,96]{2,1,0:T(8,128)(2...) custom-call(f32[8,4,1152]{2,1,0:T(4,128)} %bitcast.116, ...), custom_call_target="tpu_custom_call" | custom-call | tf_op jit(solution)/shard_map/begin/pallas_call | solution.py:307
  2.9 2.2 %collective-permute-start.24 = (bf16[12,16,96]{2,1,0:T(8,128)(2,1)S(1)}, bf16[12,16,96]{2,1,0:T(8,128)(2,1)S(1)}, u32[]{:S(2)}, u32[]{:S(2)}) collective-permute-start(bf16[12,16,96]{2,1,0:T(8,128)(2,1)S(1)} %get-tuple-element.65), channel_id=1, source_target_pairs={{0,64},{64,128},{128,192},{192,0},{1,65},{65,129},{129,193},{193,1... | collective-permute-start | bytes 110600 | tf_op jit(solution)/shard_map/ppermute | solution.py:320
  5.2 1.5 %collective-permute-start.25 = (bf16[12,16,96]{2,1,0:T(8,128)(2,1)S(1)}, bf16[12,16,96]{2,1,0:T(8,128)(2,1)S(1)}, u32[]{:S(2)}, u32[]{:S(2)}) collective-permute-start(bf16[12,16,96]{2,1,0:T(8,128)(2,1)S(1)} %get-tuple-element.66), channel_id=1, source_target_pairs={{0,192},{64,0},{128,64},{192,128},{1,193},{65,1},{129,65},{193,129... | collective-permute-start | bytes 110600 | tf_op jit(solution)/shard_map/ppermute | solution.py:320
  6.7 2.8 %collective-permute-start.26 = (bf16[12,16,96]{2,1,0:T(8,128)(2,1)S(1)}, bf16[12,16,96]{2,1,0:T(8,128)(2,1)S(1)}, u32[]{:S(2)}, u32[]{:S(2)}) collective-permute-start(bf16[12,16,96]{2,1,0:T(8,128)(2,1)S(1)} %get-tuple-element.67), channel_id=1, source_target_pairs={{0,56},{8,0},{16,8},{24,16},{32,24},{40,32},{48,40},{56,48},{1,57}... | collective-permute-start | bytes 110600 | tf_op jit(solution)/shard_map/ppermute | solution.py:320
  9.5 3.8 %collective-permute-start.27 = (bf16[12,16,96]{2,1,0:T(8,128)(2,1)S(1)}, bf16[12,16,96]{2,1,0:T(8,128)(2,1)S(1)}, u32[]{:S(2)}, u32[]{:S(2)}) collective-permute-start(bf16[12,16,96]{2,1,0:T(8,128)(2,1)S(1)} %get-tuple-element.68), channel_id=1, source_target_pairs={{0,7},{1,0},{2,1},{3,2},{4,3},{5,4},{6,5},{7,6},{8,15},{9,8},{10,9... | collective-permute-start | bytes 110600 | tf_op jit(solution)/shard_map/ppermute | solution.py:320
  13.3 1.4 %collective-permute-start.28 = (bf16[12,16,96]{2,1,0:T(8,128)(2,1)S(1)}, bf16[12,16,96]{2,1,0:T(8,128)(2,1)S(1)}, u32[]{:S(2)}, u32[]{:S(2)}) collective-permute-start(bf16[12,16,96]{2,1,0:T(8,128)(2,1)S(1)} %get-tuple-element.69), channel_id=1, source_target_pairs={{0,8},{8,16},{16,24},{24,32},{32,40},{40,48},{48,56},{56,0},{1,9},... | collective-permute-start | bytes 110600 | tf_op jit(solution)/shard_map/ppermute | solution.py:320
  14.7 1.3 %inner0.1 = (f32[32,16,96]{2,1,0:T(8,128)S(1)}, f32[1,16,96]{2,1,0:T(8,128)S(1)}) custom-call(bf16[32,16,96]{2,1,0:T(8,128)(2,1)S(1)} %get-tuple-element.61.narrow_ref, bf16[160,96,96]{2,1,0:T(8,128)(2,1)S(1)} %get-tuple-element.62.links_ref, f32[32,16,96]{2,1,0:T(8,128)S(1)} %get-tuple-element.63.refs_0_.refs_2_), custom_call_target="tpu_custom_call" | custom-call | tf_op jit(solution)/shard_map/inner0/pallas_call | solution.py:307
  16.6 2.3 %collective-permute-done.29.refs_1_ = bf16[12,16,96]{2,1,0:T(8,128)(2,1)S(1)} collective-permute-done((bf16[12,16,96]{2,1,0:T(8,128)(2,1)S(1)}, bf16[12,16,96]{2,1,0:T(8,128)(2,1)S(1)}, u32[]{:S(2)}, u32[]{:S(2)}) %collective-permute-start.29) | collective-permute-done | bytes 36896 | tf_op jit(solution)/shard_map/ppermute | solution.py:320
  19.8 2.3 %collective-permute-start.31 = (bf16[12,16,96]{2,1,0:T(8,128)(2,1)S(1)}, bf16[12,16,96]{2,1,0:T(8,128)(2,1)S(1)}, u32[]{:S(2)}, u32[]{:S(2)}) collective-permute-start(bf16[12,16,96]{2,1,0:T(8,128)(2,1)S(1)} %get-tuple-element.75), channel_id=1, source_target_pairs={{0,192},{64,0},{128,64},{192,128},{1,193},{65,1},{129,65},{193,129... | collective-permute-start | bytes 110600 | tf_op jit(solution)/shard_map/ppermute | solution.py:320
  22.1 2.4 %collective-permute-start.32 = (bf16[12,16,96]{2,1,0:T(8,128)(2,1)S(1)}, bf16[12,16,96]{2,1,0:T(8,128)(2,1)S(1)}, u32[]{:S(2)}, u32[]{:S(2)}) collective-permute-start(bf16[12,16,96]{2,1,0:T(8,128)(2,1)S(1)} %get-tuple-element.76), channel_id=1, source_target_pairs={{0,56},{8,0},{16,8},{24,16},{32,24},{40,32},{48,40},{56,48},{1,57}... | collective-permute-start | bytes 110600 | tf_op jit(solution)/shard_map/ppermute | solution.py:320
  24.8 1.2 %collective-permute-start.35 = (bf16[12,16,96]{2,1,0:T(8,128)(2,1)S(1)}, bf16[12,16,96]{2,1,0:T(8,128)(2,1)S(1)}, u32[]{:S(2)}, u32[]{:S(2)}) collective-permute-start(bf16[12,16,96]{2,1,0:T(8,128)(2,1)S(1)} %get-tuple-element.79), channel_id=1, source_target_pairs={{0,1},{1,2},{2,3},{3,4},{4,5},{5,6},{6,7},{7,0},{8,9},{9,10},{10,1... | collective-permute-start | bytes 110600 | tf_op jit(solution)/shard_map/ppermute | solution.py:320
  26.0 1.3 %inner1.1 = (f32[32,16,96]{2,1,0:T(8,128)S(1)}, f32[2,16,96]{2,1,0:T(8,128)S(1)}, f32[8,4,1152]{2,1,0:T(4,128)S(1)}) custom-call(bf16[32,16,96]{2,1,0:T(8,128)(2,1)S(1)} %get-tuple-element.71.narrow_ref, bf16[160,96,96]{2,1,0:T(8,128)(2,1)S(1)} %get-tuple-element.62.links_ref, f32[32,16,96]{2,1,0:T(8,128)S(1)} %get-tuple-element.63.refs_0_.refs_2_, ...), custom_call_target="tpu_custom_call" | custom-call | tf_op jit(solution)/shard_map/inner1/pallas_call | solution.py:307
  29.5 2.7 %collective-permute-start.37 = (bf16[12,16,96]{2,1,0:T(8,128)(2,1)S(1)}, bf16[12,16,96]{2,1,0:T(8,128)(2,1)S(1)}, u32[]{:S(2)}, u32[]{:S(2)}) collective-permute-start(bf16[12,16,96]{2,1,0:T(8,128)(2,1)S(1)} %get-tuple-element.84), channel_id=1, source_target_pairs={{0,192},{64,0},{128,64},{192,128},{1,193},{65,1},{129,65},{193,129... | collective-permute-start | bytes 110600 | tf_op jit(solution)/shard_map/ppermute | solution.py:320
  32.1 3.5 %collective-permute-start.38 = (bf16[12,16,96]{2,1,0:T(8,128)(2,1)S(1)}, bf16[12,16,96]{2,1,0:T(8,128)(2,1)S(1)}, u32[]{:S(2)}, u32[]{:S(2)}) collective-permute-start(bf16[12,16,96]{2,1,0:T(8,128)(2,1)S(1)} %get-tuple-element.85), channel_id=1, source_target_pairs={{0,56},{8,0},{16,8},{24,16},{32,24},{40,32},{48,40},{56,48},{1,57}... | collective-permute-start | bytes 110600 | tf_op jit(solution)/shard_map/ppermute | solution.py:320
  35.8 1.4 %collective-permute-start.41 = (bf16[12,16,96]{2,1,0:T(8,128)(2,1)S(1)}, bf16[12,16,96]{2,1,0:T(8,128)(2,1)S(1)}, u32[]{:S(2)}, u32[]{:S(2)}) collective-permute-start(bf16[12,16,96]{2,1,0:T(8,128)(2,1)S(1)} %get-tuple-element.88), channel_id=1, source_target_pairs={{0,1},{1,2},{2,3},{3,4},{4,5},{5,6},{6,7},{7,0},{8,9},{9,10},{10,1... | collective-permute-start | bytes 110600 | tf_op jit(solution)/shard_map/ppermute | solution.py:320
  37.1 1.3 %inner2.1 = (f32[32,16,96]{2,1,0:T(8,128)S(1)}, f32[3,16,96]{2,1,0:T(8,128)S(1)}, f32[8,4,1152]{2,1,0:T(4,128)S(1)}) custom-call(bf16[32,16,96]{2,1,0:T(8,128)(2,1)S(1)} %get-tuple-element.80.narrow_ref, bf16[160,96,96]{2,1,0:T(8,128)(2,1)S(1)} %get-tuple-element.62.links_ref, f32[32,16,96]{2,1,0:T(8,128)S(1)} %get-tuple-element.63.refs_0_.refs_2_, ...), custom_call_target="tpu_custom_call" | custom-call | tf_op jit(solution)/shard_map/inner2/pallas_call | solution.py:307
  40.5 2.7 %collective-permute-start.43 = (bf16[12,16,96]{2,1,0:T(8,128)(2,1)S(1)}, bf16[12,16,96]{2,1,0:T(8,128)(2,1)S(1)}, u32[]{:S(2)}, u32[]{:S(2)}) collective-permute-start(bf16[12,16,96]{2,1,0:T(8,128)(2,1)S(1)} %get-tuple-element.93), channel_id=1, source_target_pairs={{0,192},{64,0},{128,64},{192,128},{1,193},{65,1},{129,65},{193,129... | collective-permute-start | bytes 110600 | tf_op jit(solution)/shard_map/ppermute | solution.py:320
  43.1 3.6 %collective-permute-start.44 = (bf16[12,16,96]{2,1,0:T(8,128)(2,1)S(1)}, bf16[12,16,96]{2,1,0:T(8,128)(2,1)S(1)}, u32[]{:S(2)}, u32[]{:S(2)}) collective-permute-start(bf16[12,16,96]{2,1,0:T(8,128)(2,1)S(1)} %get-tuple-element.94), channel_id=1, source_target_pairs={{0,56},{8,0},{16,8},{24,16},{32,24},{40,32},{48,40},{56,48},{1,57}... | collective-permute-start | bytes 110600 | tf_op jit(solution)/shard_map/ppermute | solution.py:320
  46.8 1.5 %collective-permute-start.47 = (bf16[12,16,96]{2,1,0:T(8,128)(2,1)S(1)}, bf16[12,16,96]{2,1,0:T(8,128)(2,1)S(1)}, u32[]{:S(2)}, u32[]{:S(2)}) collective-permute-start(bf16[12,16,96]{2,1,0:T(8,128)(2,1)S(1)} %get-tuple-element.97), channel_id=1, source_target_pairs={{0,1},{1,2},{2,3},{3,4},{4,5},{5,6},{6,7},{7,0},{8,9},{9,10},{10,1... | collective-permute-start | bytes 110600 | tf_op jit(solution)/shard_map/ppermute | solution.py:320
  48.3 1.3 %inner3.1 = (f32[32,16,96]{2,1,0:T(8,128)S(1)}, f32[4,16,96]{2,1,0:T(8,128)S(1)}, f32[8,4,1152]{2,1,0:T(4,128)S(1)}) custom-call(bf16[32,16,96]{2,1,0:T(8,128)(2,1)S(1)} %get-tuple-element.89.narrow_ref, bf16[160,96,96]{2,1,0:T(8,128)(2,1)S(1)} %get-tuple-element.62.links_ref, f32[32,16,96]{2,1,0:T(8,128)S(1)} %get-tuple-element.63.refs_0_.refs_2_, ...), custom_call_target="tpu_custom_call" | custom-call | tf_op jit(solution)/shard_map/inner3/pallas_call | solution.py:307
  51.5 11.0 %all_to_all.14 = f32[8,1,240]{2,1,0:T(1,128)S(1)} all-to-all(f32[8,1,240]{2,1,0:T(1,128)S(1)} %broadcast_in_dim.4), channel_id=1, replica_groups=mesh['ta'=4,'gz'=8,'xy'=8] {'gz'}, dimensions={0} | all-to-all | bytes 15360 | tf_op jit(solution)/shard_map/all_to_all | solution.py:403
  63.2 3.9 %all-to-all-start.1 = ((f32[32,1,240]{2,1,0:T(1,128)}), f32[32,1,240]{2,1,0:T(1,128)S(1)}, u32[]{:S(2)}, u32[]{:S(2)}) async-start(f32[32,1,240]{2,1,0:T(1,128)} %broadcast_in_dim.5), calls=%async_computation.1 | async-start | bytes 65536 | tf_op jit(solution)/shard_map/all_to_all | solution.py:403
  67.0 8.7 %all-to-all-done.1 = f32[32,1,240]{2,1,0:T(1,128)S(1)} async-done(((f32[32,1,240]{2,1,0:T(1,128)}), f32[32,1,240]{2,1,0:T(1,128)S(1)}, u32[]{:S(2)}, u32[]{:S(2)}) %all-to-all-start.1) | async-done | bytes 30752 | tf_op jit(solution)/shard_map/all_to_all | solution.py:403
  75.7 1.7 %finish.1 = (f32[8,4,1152]{2,1,0:T(4,128)}, f32[8,4,1152]{2,1,0:T(4,128)}, s32[1,1]{1,0:T(1,128)}) custom-call(f32[32,240]{1,0:T(8,128)S(1)} %bitcast.114, f32[41,4,1152]{2,1,0:T(4,128)S(1)} %last.1.held_ref), custom_call_target="tpu_custom_call" | custom-call | tf_op jit(solution)/shard_map/finish/pallas_call | solution.py:307
  (49 shorter events, 8.7 us)
Async XLA Ops:
  2.9 11.8 %collective-permute-start.24 = (bf16[12,16,96]{2,1,0:T(8,128)(2,1)S(1)}, bf16[12,16,96]{2,1,0:T(8,128)(2,1)S(1)}, u32[]{:S(2)}, u32[]{:S(2)}) collective-permute-start(bf16[12,16,96]{2,1,0:T(8,128)(2,1)S(1)} %get-tuple-element.65), channel_id=1, source_target_pairs={{0,64},{64,128},{128,192},{192,0},{1,65},{65,129},{129,193},{193,1... | collective-permute-start | bytes 110600 | tf_op jit(solution)/shard_map/ppermute | solution.py:320
  5.2 10.9 %collective-permute-start.25 = (bf16[12,16,96]{2,1,0:T(8,128)(2,1)S(1)}, bf16[12,16,96]{2,1,0:T(8,128)(2,1)S(1)}, u32[]{:S(2)}, u32[]{:S(2)}) collective-permute-start(bf16[12,16,96]{2,1,0:T(8,128)(2,1)S(1)} %get-tuple-element.66), channel_id=1, source_target_pairs={{0,192},{64,0},{128,64},{192,128},{1,193},{65,1},{129,65},{193,129... | collective-permute-start | bytes 110600 | tf_op jit(solution)/shard_map/ppermute | solution.py:320
  6.7 9.4 %collective-permute-start.26 = (bf16[12,16,96]{2,1,0:T(8,128)(2,1)S(1)}, bf16[12,16,96]{2,1,0:T(8,128)(2,1)S(1)}, u32[]{:S(2)}, u32[]{:S(2)}) collective-permute-start(bf16[12,16,96]{2,1,0:T(8,128)(2,1)S(1)} %get-tuple-element.67), channel_id=1, source_target_pairs={{0,56},{8,0},{16,8},{24,16},{32,24},{40,32},{48,40},{56,48},{1,57}... | collective-permute-start | bytes 110600 | tf_op jit(solution)/shard_map/ppermute | solution.py:320
  9.5 6.5 %collective-permute-start.27 = (bf16[12,16,96]{2,1,0:T(8,128)(2,1)S(1)}, bf16[12,16,96]{2,1,0:T(8,128)(2,1)S(1)}, u32[]{:S(2)}, u32[]{:S(2)}) collective-permute-start(bf16[12,16,96]{2,1,0:T(8,128)(2,1)S(1)} %get-tuple-element.68), channel_id=1, source_target_pairs={{0,7},{1,0},{2,1},{3,2},{4,3},{5,4},{6,5},{7,6},{8,15},{9,8},{10,9... | collective-permute-start | bytes 110600 | tf_op jit(solution)/shard_map/ppermute | solution.py:320
  13.3 3.2 %collective-permute-start.28 = (bf16[12,16,96]{2,1,0:T(8,128)(2,1)S(1)}, bf16[12,16,96]{2,1,0:T(8,128)(2,1)S(1)}, u32[]{:S(2)}, u32[]{:S(2)}) collective-permute-start(bf16[12,16,96]{2,1,0:T(8,128)(2,1)S(1)} %get-tuple-element.69), channel_id=1, source_target_pairs={{0,8},{8,16},{16,24},{24,32},{32,40},{40,48},{48,56},{56,0},{1,9},... | collective-permute-start | bytes 110600 | tf_op jit(solution)/shard_map/ppermute | solution.py:320
  14.7 4.2 %collective-permute-start.29 = (bf16[12,16,96]{2,1,0:T(8,128)(2,1)S(1)}, bf16[12,16,96]{2,1,0:T(8,128)(2,1)S(1)}, u32[]{:S(2)}, u32[]{:S(2)}) collective-permute-start(bf16[12,16,96]{2,1,0:T(8,128)(2,1)S(1)} %get-tuple-element.70), channel_id=1, source_target_pairs={{0,1},{1,2},{2,3},{3,4},{4,5},{5,6},{6,7},{7,0},{8,9},{9,10},{10,1... | collective-permute-start | bytes 110600 | tf_op jit(solution)/shard_map/ppermute | solution.py:320
  19.3 5.4 %collective-permute-start.30 = (bf16[12,16,96]{2,1,0:T(8,128)(2,1)S(1)}, bf16[12,16,96]{2,1,0:T(8,128)(2,1)S(1)}, u32[]{:S(2)}, u32[]{:S(2)}) collective-permute-start(bf16[12,16,96]{2,1,0:T(8,128)(2,1)S(1)} %get-tuple-element.74), channel_id=1, source_target_pairs={{0,64},{64,128},{128,192},{192,0},{1,65},{65,129},{129,193},{193,1... | collective-permute-start | bytes 110600 | tf_op jit(solution)/shard_map/ppermute | solution.py:320
  19.8 7.5 %collective-permute-start.31 = (bf16[12,16,96]{2,1,0:T(8,128)(2,1)S(1)}, bf16[12,16,96]{2,1,0:T(8,128)(2,1)S(1)}, u32[]{:S(2)}, u32[]{:S(2)}) collective-permute-start(bf16[12,16,96]{2,1,0:T(8,128)(2,1)S(1)} %get-tuple-element.75), channel_id=1, source_target_pairs={{0,192},{64,0},{128,64},{192,128},{1,193},{65,1},{129,65},{193,129... | collective-permute-start | bytes 110600 | tf_op jit(solution)/shard_map/ppermute | solution.py:320
  22.1 5.2 %collective-permute-start.32 = (bf16[12,16,96]{2,1,0:T(8,128)(2,1)S(1)}, bf16[12,16,96]{2,1,0:T(8,128)(2,1)S(1)}, u32[]{:S(2)}, u32[]{:S(2)}) collective-permute-start(bf16[12,16,96]{2,1,0:T(8,128)(2,1)S(1)} %get-tuple-element.76), channel_id=1, source_target_pairs={{0,56},{8,0},{16,8},{24,16},{32,24},{40,32},{48,40},{56,48},{1,57}... | collective-permute-start | bytes 110600 | tf_op jit(solution)/shard_map/ppermute | solution.py:320
  24.5 2.9 %collective-permute-start.33 = (bf16[12,16,96]{2,1,0:T(8,128)(2,1)S(1)}, bf16[12,16,96]{2,1,0:T(8,128)(2,1)S(1)}, u32[]{:S(2)}, u32[]{:S(2)}) collective-permute-start(bf16[12,16,96]{2,1,0:T(8,128)(2,1)S(1)} %get-tuple-element.77), channel_id=1, source_target_pairs={{0,7},{1,0},{2,1},{3,2},{4,3},{5,4},{6,5},{7,6},{8,15},{9,8},{10,9... | collective-permute-start | bytes 110600 | tf_op jit(solution)/shard_map/ppermute | solution.py:320
  24.8 3.2 %collective-permute-start.34 = (bf16[12,16,96]{2,1,0:T(8,128)(2,1)S(1)}, bf16[12,16,96]{2,1,0:T(8,128)(2,1)S(1)}, u32[]{:S(2)}, u32[]{:S(2)}) collective-permute-start(bf16[12,16,96]{2,1,0:T(8,128)(2,1)S(1)} %get-tuple-element.78), channel_id=1, source_target_pairs={{0,8},{8,16},{16,24},{24,32},{32,40},{40,48},{48,56},{56,0},{1,9},... | collective-permute-start | bytes 110600 | tf_op jit(solution)/shard_map/ppermute | solution.py:320
  24.8 4.2 %collective-permute-start.35 = (bf16[12,16,96]{2,1,0:T(8,128)(2,1)S(1)}, bf16[12,16,96]{2,1,0:T(8,128)(2,1)S(1)}, u32[]{:S(2)}, u32[]{:S(2)}) collective-permute-start(bf16[12,16,96]{2,1,0:T(8,128)(2,1)S(1)} %get-tuple-element.79), channel_id=1, source_target_pairs={{0,1},{1,2},{2,3},{3,4},{4,5},{5,6},{6,7},{7,0},{8,9},{9,10},{10,1... | collective-permute-start | bytes 110600 | tf_op jit(solution)/shard_map/ppermute | solution.py:320
  29.4 6.4 %collective-permute-start.36 = (bf16[12,16,96]{2,1,0:T(8,128)(2,1)S(1)}, bf16[12,16,96]{2,1,0:T(8,128)(2,1)S(1)}, u32[]{:S(2)}, u32[]{:S(2)}) collective-permute-start(bf16[12,16,96]{2,1,0:T(8,128)(2,1)S(1)} %get-tuple-element.83), channel_id=1, source_target_pairs={{0,64},{64,128},{128,192},{192,0},{1,65},{65,129},{129,193},{193,1... | collective-permute-start | bytes 110600 | tf_op jit(solution)/shard_map/ppermute | solution.py:320
  29.5 9.0 %collective-permute-start.37 = (bf16[12,16,96]{2,1,0:T(8,128)(2,1)S(1)}, bf16[12,16,96]{2,1,0:T(8,128)(2,1)S(1)}, u32[]{:S(2)}, u32[]{:S(2)}) collective-permute-start(bf16[12,16,96]{2,1,0:T(8,128)(2,1)S(1)} %get-tuple-element.84), channel_id=1, source_target_pairs={{0,192},{64,0},{128,64},{192,128},{1,193},{65,1},{129,65},{193,129... | collective-permute-start | bytes 110600 | tf_op jit(solution)/shard_map/ppermute | solution.py:320
  32.1 6.3 %collective-permute-start.38 = (bf16[12,16,96]{2,1,0:T(8,128)(2,1)S(1)}, bf16[12,16,96]{2,1,0:T(8,128)(2,1)S(1)}, u32[]{:S(2)}, u32[]{:S(2)}) collective-permute-start(bf16[12,16,96]{2,1,0:T(8,128)(2,1)S(1)} %get-tuple-element.85), channel_id=1, source_target_pairs={{0,56},{8,0},{16,8},{24,16},{32,24},{40,32},{48,40},{56,48},{1,57}... | collective-permute-start | bytes 110600 | tf_op jit(solution)/shard_map/ppermute | solution.py:320
  35.6 2.9 %collective-permute-start.39 = (bf16[12,16,96]{2,1,0:T(8,128)(2,1)S(1)}, bf16[12,16,96]{2,1,0:T(8,128)(2,1)S(1)}, u32[]{:S(2)}, u32[]{:S(2)}) collective-permute-start(bf16[12,16,96]{2,1,0:T(8,128)(2,1)S(1)} %get-tuple-element.86), channel_id=1, source_target_pairs={{0,7},{1,0},{2,1},{3,2},{4,3},{5,4},{6,5},{7,6},{8,15},{9,8},{10,9... | collective-permute-start | bytes 110600 | tf_op jit(solution)/shard_map/ppermute | solution.py:320
  35.8 3.3 %collective-permute-start.40 = (bf16[12,16,96]{2,1,0:T(8,128)(2,1)S(1)}, bf16[12,16,96]{2,1,0:T(8,128)(2,1)S(1)}, u32[]{:S(2)}, u32[]{:S(2)}) collective-permute-start(bf16[12,16,96]{2,1,0:T(8,128)(2,1)S(1)} %get-tuple-element.87), channel_id=1, source_target_pairs={{0,8},{8,16},{16,24},{24,32},{32,40},{40,48},{48,56},{56,0},{1,9},... | collective-permute-start | bytes 110600 | tf_op jit(solution)/shard_map/ppermute | solution.py:320
  35.8 4.2 %collective-permute-start.41 = (bf16[12,16,96]{2,1,0:T(8,128)(2,1)S(1)}, bf16[12,16,96]{2,1,0:T(8,128)(2,1)S(1)}, u32[]{:S(2)}, u32[]{:S(2)}) collective-permute-start(bf16[12,16,96]{2,1,0:T(8,128)(2,1)S(1)} %get-tuple-element.88), channel_id=1, source_target_pairs={{0,1},{1,2},{2,3},{3,4},{4,5},{5,6},{6,7},{7,0},{8,9},{9,10},{10,1... | collective-permute-start | bytes 110600 | tf_op jit(solution)/shard_map/ppermute | solution.py:320
  40.4 6.4 %collective-permute-start.42 = (bf16[12,16,96]{2,1,0:T(8,128)(2,1)S(1)}, bf16[12,16,96]{2,1,0:T(8,128)(2,1)S(1)}, u32[]{:S(2)}, u32[]{:S(2)}) collective-permute-start(bf16[12,16,96]{2,1,0:T(8,128)(2,1)S(1)} %get-tuple-element.92), channel_id=1, source_target_pairs={{0,64},{64,128},{128,192},{192,0},{1,65},{65,129},{129,193},{193,1... | collective-permute-start | bytes 110600 | tf_op jit(solution)/shard_map/ppermute | solution.py:320
  40.5 9.2 %collective-permute-start.43 = (bf16[12,16,96]{2,1,0:T(8,128)(2,1)S(1)}, bf16[12,16,96]{2,1,0:T(8,128)(2,1)S(1)}, u32[]{:S(2)}, u32[]{:S(2)}) collective-permute-start(bf16[12,16,96]{2,1,0:T(8,128)(2,1)S(1)} %get-tuple-element.93), channel_id=1, source_target_pairs={{0,192},{64,0},{128,64},{192,128},{1,193},{65,1},{129,65},{193,129... | collective-permute-start | bytes 110600 | tf_op jit(solution)/shard_map/ppermute | solution.py:320
  43.1 6.5 %collective-permute-start.44 = (bf16[12,16,96]{2,1,0:T(8,128)(2,1)S(1)}, bf16[12,16,96]{2,1,0:T(8,128)(2,1)S(1)}, u32[]{:S(2)}, u32[]{:S(2)}) collective-permute-start(bf16[12,16,96]{2,1,0:T(8,128)(2,1)S(1)} %get-tuple-element.94), channel_id=1, source_target_pairs={{0,56},{8,0},{16,8},{24,16},{32,24},{40,32},{48,40},{56,48},{1,57}... | collective-permute-start | bytes 110600 | tf_op jit(solution)/shard_map/ppermute | solution.py:320
  46.8 3.4 %collective-permute-start.46 = (bf16[12,16,96]{2,1,0:T(8,128)(2,1)S(1)}, bf16[12,16,96]{2,1,0:T(8,128)(2,1)S(1)}, u32[]{:S(2)}, u32[]{:S(2)}) collective-permute-start(bf16[12,16,96]{2,1,0:T(8,128)(2,1)S(1)} %get-tuple-element.96), channel_id=1, source_target_pairs={{0,8},{8,16},{16,24},{24,32},{32,40},{40,48},{48,56},{56,0},{1,9},... | collective-permute-start | bytes 110600 | tf_op jit(solution)/shard_map/ppermute | solution.py:320
  46.8 4.2 %collective-permute-start.47 = (bf16[12,16,96]{2,1,0:T(8,128)(2,1)S(1)}, bf16[12,16,96]{2,1,0:T(8,128)(2,1)S(1)}, u32[]{:S(2)}, u32[]{:S(2)}) collective-permute-start(bf16[12,16,96]{2,1,0:T(8,128)(2,1)S(1)} %get-tuple-element.97), channel_id=1, source_target_pairs={{0,1},{1,2},{2,3},{3,4},{4,5},{5,6},{6,7},{7,0},{8,9},{9,10},{10,1... | collective-permute-start | bytes 110600 | tf_op jit(solution)/shard_map/ppermute | solution.py:320
  63.2 12.6 %all-to-all-start.1 = ((f32[32,1,240]{2,1,0:T(1,128)}), f32[32,1,240]{2,1,0:T(1,128)S(1)}, u32[]{:S(2)}, u32[]{:S(2)}) async-start(f32[32,1,240]{2,1,0:T(1,128)} %broadcast_in_dim.5), calls=%async_computation.1 | async-start | bytes 65536 | tf_op jit(solution)/shard_map/all_to_all | solution.py:403
  (2 other events, 5.7 us)

commit v4 on v3

--- a/solution.py
+++ b/solution.py
@@ -225,10 +225,12 @@
 
 def combine(left, right):
     terms = [a * b for a, b in zip(left, right)]
-    return sum(terms[1:], terms[0])
-
-
-def finish_kernel(gathered_ref, held_ref, solution_ref, residual_ref, unsound_ref):
+    while len(terms) > 1:
+        terms = [sum(terms[i + 1 : i + 2], terms[i]) for i in range(0, len(terms), 2)]
+    return terms[0]
+
+
+def finish_kernel(gathered_ref, held_ref, solution_ref, residual_ref, unsound_ref, made_ref, sems):
     summed = lax.dot_general(
         gathered_ref[...], jnp.ones((SECOND_GROUP, 128), jnp.float32), TN,
         precision=lax.Precision.HIGHEST, preferred_element_type=jnp.float32,
@@ -284,10 +286,19 @@
     factors = lax.dot_general(
         packed[:, 0:ROWS], spread, TN, precision=lax.Precision.HIGHEST, preferred_element_type=jnp.float32
     )
-    for group in range(GROUPS):
-        held = [held_ref[j * GROUPS + group] for j in range(BASIS)]
-        solution_ref[group] = combine([factors[i : i + 1] for i in range(ITERS)], held)
-        residual_ref[group] = combine([factors[ITERS + i : ITERS + i + 1] for i in range(BASIS)], held)
+    copies = []
+    for half in (0, 4):
+        for side, ref in enumerate((solution_ref, residual_ref)):
+            count, at = (ITERS, 0) if side == 0 else (BASIS, ITERS)
+            weights = [factors[at + i : at + i + 1] for i in range(count)]
+            for group in range(half, half + 4):
+                made_ref[side, group] = combine(weights, [held_ref[j * GROUPS + group] for j in range(count)])
+            here = pl.ds(half, 4)
+            copy = pltpu.make_async_copy(made_ref.at[side, here], ref.at[here], sems.at[len(copies)])
+            copy.start()
+            copies.append(copy)
+    for copy in copies:
+        copy.wait()
 
 
 def shape(dims, dtype=jnp.float32):
@@ -301,15 +312,18 @@
 NARROW = shape((SITES, ROWS, COMP), jnp.bfloat16)
 
 
-def call(kernel, name, out_shape, operands, scratch=(), apart=()):
+def call(kernel, name, out_shape, operands, scratch=(), apart=(), out_apart=()):
     whole = pl.BlockSpec(memory_space=pltpu.VMEM)
     scalar = pl.BlockSpec(memory_space=pltpu.SMEM)
+    far = pl.BlockSpec(memory_space=pl.ANY)
     return pl.pallas_call(
         kernel,
         name=name,
         out_shape=out_shape,
         in_specs=[pl.BlockSpec(memory_space=pl.ANY) if i in apart else whole for i in range(len(operands))],
-        out_specs=[scalar if o.shape == (1, 1) else whole for o in out_shape],
+        out_specs=[
+            far if i in out_apart else scalar if o.shape == (1, 1) else whole for i, o in enumerate(out_shape)
+        ],
         scratch_shapes=scratch,
         compiler_params=pltpu.CompilerParams(vmem_limit_bytes=24 * 2**20),
     )(*operands)
@@ -404,7 +418,8 @@
         if members == 8:
             sums = jnp.sum(sums, 0)
     out, residual, unsound = call(
-        finish_kernel, "finish", [ROW, ROW, shape((1, 1), jnp.int32)], (sums, held)
+        finish_kernel, "finish", [ROW, ROW, shape((1, 1), jnp.int32)], (sums, held),
+        [pltpu.VMEM((2, GROUPS, 4, RHS * COMP), jnp.float32), pltpu.SemaphoreType.DMA((4,))], out_apart=(0, 1),
     )
     return lax.cond(
         unsound[0, 0] > 0,

time: 78.6 us -> 79.1 us (level)
  no operation moved by 1% of the time
where the time goes in v4:
time: 79.1 us; the launch traced here: 78.9 us
  starting transfers between devices  37.9 us (48%)
  waiting for transfers between devices  13.9 us (18%)
  Pallas kernels  13.7 us (17%)
  blocking collectives  11 us (14%)
  between operations  1.5 us (2%)
    ppermute x24, starting transfers between devices, shifted(): lax.ppermute(shard, axis, [(i, (i + by) % length) for i in range(length)])  34 us
    pallas_call x14, Pallas kernels, call(): pl.pallas_call(kernel, name=name, out_shape=out_shape, in_specs=[pl.Block...  13.7 us
    all_to_all x1, blocking collectives, local(): sums = lax.all_to_all(jnp.broadcast_to(sums, (members, LANES)), axes, 0, 0)  11 us
    all_to_all x1, waiting for transfers between devices, local(): sums = lax.all_to_all(jnp.broadcast_to(sums, (members, LANES)), axes, 0, 0)  8.7 us
    ppermute x24, waiting for transfers between devices, shifted(): lax.ppermute(shard, axis, [(i, (i + by) % length) for i in range(length)])  5.21 us
    all_to_all x1, starting transfers between devices, local(): sums = lax.all_to_all(jnp.broadcast_to(sums, (members, LANES)), axes, 0, 0)  3.85 us
  transfers between devices with their start and end apart: 25, of which 8 were waited for; matrix products, arithmetic and copies ran while one was open for 0% of the time, Pallas kernels for 9%

profile of v4, /device:TPU:1, one launch (start us, length us, event | category | flops | bytes accessed | tf_op | source)
XLA Modules:
  0.0 78.9 jit_solution(2120699140042604385)
XLA Ops:
  0.6 2.3 %begin.1 = (f32[32,16,96]{2,1,0:T(8,128)S(1)}, bf16[32,16,96]{2,1,0:T(8,128)(2,1)S(1)}, bf16[12,16,96]{2,1,0:T(8,128)(2,1)S(1)}, bf16[12,16,96]{2,1,0:T(8,128)(2...) custom-call(f32[8,4,1152]{2,1,0:T(4,128)} %bitcast.116, ...), custom_call_target="tpu_custom_call" | custom-call | tf_op jit(solution)/shard_map/begin/pallas_call | solution.py:319
  2.9 2.2 %collective-permute-start.24 = (bf16[12,16,96]{2,1,0:T(8,128)(2,1)S(1)}, bf16[12,16,96]{2,1,0:T(8,128)(2,1)S(1)}, u32[]{:S(2)}, u32[]{:S(2)}) collective-permute-start(bf16[12,16,96]{2,1,0:T(8,128)(2,1)S(1)} %get-tuple-element.65), channel_id=1, source_target_pairs={{0,64},{64,128},{128,192},{192,0},{1,65},{65,129},{129,193},{193,1... | collective-permute-start | bytes 110600 | tf_op jit(solution)/shard_map/ppermute | solution.py:334
  5.2 1.5 %collective-permute-start.25 = (bf16[12,16,96]{2,1,0:T(8,128)(2,1)S(1)}, bf16[12,16,96]{2,1,0:T(8,128)(2,1)S(1)}, u32[]{:S(2)}, u32[]{:S(2)}) collective-permute-start(bf16[12,16,96]{2,1,0:T(8,128)(2,1)S(1)} %get-tuple-element.66), channel_id=1, source_target_pairs={{0,192},{64,0},{128,64},{192,128},{1,193},{65,1},{129,65},{193,129... | collective-permute-start | bytes 110600 | tf_op jit(solution)/shard_map/ppermute | solution.py:334
  6.7 2.8 %collective-permute-start.26 = (bf16[12,16,96]{2,1,0:T(8,128)(2,1)S(1)}, bf16[12,16,96]{2,1,0:T(8,128)(2,1)S(1)}, u32[]{:S(2)}, u32[]{:S(2)}) collective-permute-start(bf16[12,16,96]{2,1,0:T(8,128)(2,1)S(1)} %get-tuple-element.67), channel_id=1, source_target_pairs={{0,56},{8,0},{16,8},{24,16},{32,24},{40,32},{48,40},{56,48},{1,57}... | collective-permute-start | bytes 110600 | tf_op jit(solution)/shard_map/ppermute | solution.py:334
  9.5 3.8 %collective-permute-start.27 = (bf16[12,16,96]{2,1,0:T(8,128)(2,1)S(1)}, bf16[12,16,96]{2,1,0:T(8,128)(2,1)S(1)}, u32[]{:S(2)}, u32[]{:S(2)}) collective-permute-start(bf16[12,16,96]{2,1,0:T(8,128)(2,1)S(1)} %get-tuple-element.68), channel_id=1, source_target_pairs={{0,7},{1,0},{2,1},{3,2},{4,3},{5,4},{6,5},{7,6},{8,15},{9,8},{10,9... | collective-permute-start | bytes 110600 | tf_op jit(solution)/shard_map/ppermute | solution.py:334
  13.3 1.4 %collective-permute-start.28 = (bf16[12,16,96]{2,1,0:T(8,128)(2,1)S(1)}, bf16[12,16,96]{2,1,0:T(8,128)(2,1)S(1)}, u32[]{:S(2)}, u32[]{:S(2)}) collective-permute-start(bf16[12,16,96]{2,1,0:T(8,128)(2,1)S(1)} %get-tuple-element.69), channel_id=1, source_target_pairs={{0,8},{8,16},{16,24},{24,32},{32,40},{40,48},{48,56},{56,0},{1,9},... | collective-permute-start | bytes 110600 | tf_op jit(solution)/shard_map/ppermute | solution.py:334
  14.7 1.3 %inner0.1 = (f32[32,16,96]{2,1,0:T(8,128)S(1)}, f32[1,16,96]{2,1,0:T(8,128)S(1)}) custom-call(bf16[32,16,96]{2,1,0:T(8,128)(2,1)S(1)} %get-tuple-element.61.narrow_ref, bf16[160,96,96]{2,1,0:T(8,128)(2,1)S(1)} %get-tuple-element.62.links_ref, f32[32,16,96]{2,1,0:T(8,128)S(1)} %get-tuple-element.63.refs_0_.refs_2_), custom_call_target="tpu_custom_call" | custom-call | tf_op jit(solution)/shard_map/inner0/pallas_call | solution.py:319
  16.6 2.3 %collective-permute-done.29.refs_1_ = bf16[12,16,96]{2,1,0:T(8,128)(2,1)S(1)} collective-permute-done((bf16[12,16,96]{2,1,0:T(8,128)(2,1)S(1)}, bf16[12,16,96]{2,1,0:T(8,128)(2,1)S(1)}, u32[]{:S(2)}, u32[]{:S(2)}) %collective-permute-start.29) | collective-permute-done | bytes 36896 | tf_op jit(solution)/shard_map/ppermute | solution.py:334
  19.8 2.3 %collective-permute-start.31 = (bf16[12,16,96]{2,1,0:T(8,128)(2,1)S(1)}, bf16[12,16,96]{2,1,0:T(8,128)(2,1)S(1)}, u32[]{:S(2)}, u32[]{:S(2)}) collective-permute-start(bf16[12,16,96]{2,1,0:T(8,128)(2,1)S(1)} %get-tuple-element.75), channel_id=1, source_target_pairs={{0,192},{64,0},{128,64},{192,128},{1,193},{65,1},{129,65},{193,129... | collective-permute-start | bytes 110600 | tf_op jit(solution)/shard_map/ppermute | solution.py:334
  22.1 2.4 %collective-permute-start.32 = (bf16[12,16,96]{2,1,0:T(8,128)(2,1)S(1)}, bf16[12,16,96]{2,1,0:T(8,128)(2,1)S(1)}, u32[]{:S(2)}, u32[]{:S(2)}) collective-permute-start(bf16[12,16,96]{2,1,0:T(8,128)(2,1)S(1)} %get-tuple-element.76), channel_id=1, source_target_pairs={{0,56},{8,0},{16,8},{24,16},{32,24},{40,32},{48,40},{56,48},{1,57}... | collective-permute-start | bytes 110600 | tf_op jit(solution)/shard_map/ppermute | solution.py:334
  24.8 1.2 %collective-permute-start.35 = (bf16[12,16,96]{2,1,0:T(8,128)(2,1)S(1)}, bf16[12,16,96]{2,1,0:T(8,128)(2,1)S(1)}, u32[]{:S(2)}, u32[]{:S(2)}) collective-permute-start(bf16[12,16,96]{2,1,0:T(8,128)(2,1)S(1)} %get-tuple-element.79), channel_id=1, source_target_pairs={{0,1},{1,2},{2,3},{3,4},{4,5},{5,6},{6,7},{7,0},{8,9},{9,10},{10,1... | collective-permute-start | bytes 110600 | tf_op jit(solution)/shard_map/ppermute | solution.py:334
  26.0 1.3 %inner1.1 = (f32[32,16,96]{2,1,0:T(8,128)S(1)}, f32[2,16,96]{2,1,0:T(8,128)S(1)}, f32[8,4,1152]{2,1,0:T(4,128)S(1)}) custom-call(bf16[32,16,96]{2,1,0:T(8,128)(2,1)S(1)} %get-tuple-element.71.narrow_ref, bf16[160,96,96]{2,1,0:T(8,128)(2,1)S(1)} %get-tuple-element.62.links_ref, f32[32,16,96]{2,1,0:T(8,128)S(1)} %get-tuple-element.63.refs_0_.refs_2_, ...), custom_call_target="tpu_custom_call" | custom-call | tf_op jit(solution)/shard_map/inner1/pallas_call | solution.py:319
  29.5 2.7 %collective-permute-start.37 = (bf16[12,16,96]{2,1,0:T(8,128)(2,1)S(1)}, bf16[12,16,96]{2,1,0:T(8,128)(2,1)S(1)}, u32[]{:S(2)}, u32[]{:S(2)}) collective-permute-start(bf16[12,16,96]{2,1,0:T(8,128)(2,1)S(1)} %get-tuple-element.84), channel_id=1, source_target_pairs={{0,192},{64,0},{128,64},{192,128},{1,193},{65,1},{129,65},{193,129... | collective-permute-start | bytes 110600 | tf_op jit(solution)/shard_map/ppermute | solution.py:334
  32.1 3.5 %collective-permute-start.38 = (bf16[12,16,96]{2,1,0:T(8,128)(2,1)S(1)}, bf16[12,16,96]{2,1,0:T(8,128)(2,1)S(1)}, u32[]{:S(2)}, u32[]{:S(2)}) collective-permute-start(bf16[12,16,96]{2,1,0:T(8,128)(2,1)S(1)} %get-tuple-element.85), channel_id=1, source_target_pairs={{0,56},{8,0},{16,8},{24,16},{32,24},{40,32},{48,40},{56,48},{1,57}... | collective-permute-start | bytes 110600 | tf_op jit(solution)/shard_map/ppermute | solution.py:334
  35.8 1.4 %collective-permute-start.41 = (bf16[12,16,96]{2,1,0:T(8,128)(2,1)S(1)}, bf16[12,16,96]{2,1,0:T(8,128)(2,1)S(1)}, u32[]{:S(2)}, u32[]{:S(2)}) collective-permute-start(bf16[12,16,96]{2,1,0:T(8,128)(2,1)S(1)} %get-tuple-element.88), channel_id=1, source_target_pairs={{0,1},{1,2},{2,3},{3,4},{4,5},{5,6},{6,7},{7,0},{8,9},{9,10},{10,1... | collective-permute-start | bytes 110600 | tf_op jit(solution)/shard_map/ppermute | solution.py:334
  37.1 1.3 %inner2.1 = (f32[32,16,96]{2,1,0:T(8,128)S(1)}, f32[3,16,96]{2,1,0:T(8,128)S(1)}, f32[8,4,1152]{2,1,0:T(4,128)S(1)}) custom-call(bf16[32,16,96]{2,1,0:T(8,128)(2,1)S(1)} %get-tuple-element.80.narrow_ref, bf16[160,96,96]{2,1,0:T(8,128)(2,1)S(1)} %get-tuple-element.62.links_ref, f32[32,16,96]{2,1,0:T(8,128)S(1)} %get-tuple-element.63.refs_0_.refs_2_, ...), custom_call_target="tpu_custom_call" | custom-call | tf_op jit(solution)/shard_map/inner2/pallas_call | solution.py:319
  40.5 2.7 %collective-permute-start.43 = (bf16[12,16,96]{2,1,0:T(8,128)(2,1)S(1)}, bf16[12,16,96]{2,1,0:T(8,128)(2,1)S(1)}, u32[]{:S(2)}, u32[]{:S(2)}) collective-permute-start(bf16[12,16,96]{2,1,0:T(8,128)(2,1)S(1)} %get-tuple-element.93), channel_id=1, source_target_pairs={{0,192},{64,0},{128,64},{192,128},{1,193},{65,1},{129,65},{193,129... | collective-permute-start | bytes 110600 | tf_op jit(solution)/shard_map/ppermute | solution.py:334
  43.1 3.6 %collective-permute-start.44 = (bf16[12,16,96]{2,1,0:T(8,128)(2,1)S(1)}, bf16[12,16,96]{2,1,0:T(8,128)(2,1)S(1)}, u32[]{:S(2)}, u32[]{:S(2)}) collective-permute-start(bf16[12,16,96]{2,1,0:T(8,128)(2,1)S(1)} %get-tuple-element.94), channel_id=1, source_target_pairs={{0,56},{8,0},{16,8},{24,16},{32,24},{40,32},{48,40},{56,48},{1,57}... | collective-permute-start | bytes 110600 | tf_op jit(solution)/shard_map/ppermute | solution.py:334
  46.8 1.5 %collective-permute-start.47 = (bf16[12,16,96]{2,1,0:T(8,128)(2,1)S(1)}, bf16[12,16,96]{2,1,0:T(8,128)(2,1)S(1)}, u32[]{:S(2)}, u32[]{:S(2)}) collective-permute-start(bf16[12,16,96]{2,1,0:T(8,128)(2,1)S(1)} %get-tuple-element.97), channel_id=1, source_target_pairs={{0,1},{1,2},{2,3},{3,4},{4,5},{5,6},{6,7},{7,0},{8,9},{9,10},{10,1... | collective-permute-start | bytes 110600 | tf_op jit(solution)/shard_map/ppermute | solution.py:334
  48.3 1.3 %inner3.1 = (f32[32,16,96]{2,1,0:T(8,128)S(1)}, f32[4,16,96]{2,1,0:T(8,128)S(1)}, f32[8,4,1152]{2,1,0:T(4,128)S(1)}) custom-call(bf16[32,16,96]{2,1,0:T(8,128)(2,1)S(1)} %get-tuple-element.89.narrow_ref, bf16[160,96,96]{2,1,0:T(8,128)(2,1)S(1)} %get-tuple-element.62.links_ref, f32[32,16,96]{2,1,0:T(8,128)S(1)} %get-tuple-element.63.refs_0_.refs_2_, ...), custom_call_target="tpu_custom_call" | custom-call | tf_op jit(solution)/shard_map/inner3/pallas_call | solution.py:319
  51.5 11.0 %all_to_all.14 = f32[8,1,240]{2,1,0:T(1,128)S(1)} all-to-all(f32[8,1,240]{2,1,0:T(1,128)S(1)} %broadcast_in_dim.4), channel_id=1, replica_groups=mesh['ta'=4,'gz'=8,'xy'=8] {'gz'}, dimensions={0} | all-to-all | bytes 15360 | tf_op jit(solution)/shard_map/all_to_all | solution.py:417
  63.2 3.9 %all-to-all-start.1 = ((f32[32,1,240]{2,1,0:T(1,128)}), f32[32,1,240]{2,1,0:T(1,128)S(1)}, u32[]{:S(2)}, u32[]{:S(2)}) async-start(f32[32,1,240]{2,1,0:T(1,128)} %broadcast_in_dim.5), calls=%async_computation.1 | async-start | bytes 65536 | tf_op jit(solution)/shard_map/all_to_all | solution.py:417
  67.0 8.7 %all-to-all-done.1 = f32[32,1,240]{2,1,0:T(1,128)S(1)} async-done(((f32[32,1,240]{2,1,0:T(1,128)}), f32[32,1,240]{2,1,0:T(1,128)S(1)}, u32[]{:S(2)}, u32[]{:S(2)}) %all-to-all-start.1) | async-done | bytes 30752 | tf_op jit(solution)/shard_map/all_to_all | solution.py:417
  75.7 2.2 %finish.1 = (f32[8,4,1152]{2,1,0:T(4,128)}, f32[8,4,1152]{2,1,0:T(4,128)}, s32[1,1]{1,0:T(1,128)}) custom-call(f32[32,240]{1,0:T(8,128)S(1)} %bitcast.114, f32[41,4,1152]{2,1,0:T(4,128)S(1)} %last.1.held_ref), custom_call_target="tpu_custom_call" | custom-call | tf_op jit(solution)/shard_map/finish/pallas_call | solution.py:319
  (49 shorter events, 8.7 us)
Async XLA Ops:
  2.9 11.8 %collective-permute-start.24 = (bf16[12,16,96]{2,1,0:T(8,128)(2,1)S(1)}, bf16[12,16,96]{2,1,0:T(8,128)(2,1)S(1)}, u32[]{:S(2)}, u32[]{:S(2)}) collective-permute-start(bf16[12,16,96]{2,1,0:T(8,128)(2,1)S(1)} %get-tuple-element.65), channel_id=1, source_target_pairs={{0,64},{64,128},{128,192},{192,0},{1,65},{65,129},{129,193},{193,1... | collective-permute-start | bytes 110600 | tf_op jit(solution)/shard_map/ppermute | solution.py:334
  5.2 10.9 %collective-permute-start.25 = (bf16[12,16,96]{2,1,0:T(8,128)(2,1)S(1)}, bf16[12,16,96]{2,1,0:T(8,128)(2,1)S(1)}, u32[]{:S(2)}, u32[]{:S(2)}) collective-permute-start(bf16[12,16,96]{2,1,0:T(8,128)(2,1)S(1)} %get-tuple-element.66), channel_id=1, source_target_pairs={{0,192},{64,0},{128,64},{192,128},{1,193},{65,1},{129,65},{193,129... | collective-permute-start | bytes 110600 | tf_op jit(solution)/shard_map/ppermute | solution.py:334
  6.7 9.4 %collective-permute-start.26 = (bf16[12,16,96]{2,1,0:T(8,128)(2,1)S(1)}, bf16[12,16,96]{2,1,0:T(8,128)(2,1)S(1)}, u32[]{:S(2)}, u32[]{:S(2)}) collective-permute-start(bf16[12,16,96]{2,1,0:T(8,128)(2,1)S(1)} %get-tuple-element.67), channel_id=1, source_target_pairs={{0,56},{8,0},{16,8},{24,16},{32,24},{40,32},{48,40},{56,48},{1,57}... | collective-permute-start | bytes 110600 | tf_op jit(solution)/shard_map/ppermute | solution.py:334
  9.5 6.5 %collective-permute-start.27 = (bf16[12,16,96]{2,1,0:T(8,128)(2,1)S(1)}, bf16[12,16,96]{2,1,0:T(8,128)(2,1)S(1)}, u32[]{:S(2)}, u32[]{:S(2)}) collective-permute-start(bf16[12,16,96]{2,1,0:T(8,128)(2,1)S(1)} %get-tuple-element.68), channel_id=1, source_target_pairs={{0,7},{1,0},{2,1},{3,2},{4,3},{5,4},{6,5},{7,6},{8,15},{9,8},{10,9... | collective-permute-start | bytes 110600 | tf_op jit(solution)/shard_map/ppermute | solution.py:334
  13.3 3.2 %collective-permute-start.28 = (bf16[12,16,96]{2,1,0:T(8,128)(2,1)S(1)}, bf16[12,16,96]{2,1,0:T(8,128)(2,1)S(1)}, u32[]{:S(2)}, u32[]{:S(2)}) collective-permute-start(bf16[12,16,96]{2,1,0:T(8,128)(2,1)S(1)} %get-tuple-element.69), channel_id=1, source_target_pairs={{0,8},{8,16},{16,24},{24,32},{32,40},{40,48},{48,56},{56,0},{1,9},... | collective-permute-start | bytes 110600 | tf_op jit(solution)/shard_map/ppermute | solution.py:334
  14.7 4.2 %collective-permute-start.29 = (bf16[12,16,96]{2,1,0:T(8,128)(2,1)S(1)}, bf16[12,16,96]{2,1,0:T(8,128)(2,1)S(1)}, u32[]{:S(2)}, u32[]{:S(2)}) collective-permute-start(bf16[12,16,96]{2,1,0:T(8,128)(2,1)S(1)} %get-tuple-element.70), channel_id=1, source_target_pairs={{0,1},{1,2},{2,3},{3,4},{4,5},{5,6},{6,7},{7,0},{8,9},{9,10},{10,1... | collective-permute-start | bytes 110600 | tf_op jit(solution)/shard_map/ppermute | solution.py:334
  19.3 5.4 %collective-permute-start.30 = (bf16[12,16,96]{2,1,0:T(8,128)(2,1)S(1)}, bf16[12,16,96]{2,1,0:T(8,128)(2,1)S(1)}, u32[]{:S(2)}, u32[]{:S(2)}) collective-permute-start(bf16[12,16,96]{2,1,0:T(8,128)(2,1)S(1)} %get-tuple-element.74), channel_id=1, source_target_pairs={{0,64},{64,128},{128,192},{192,0},{1,65},{65,129},{129,193},{193,1... | collective-permute-start | bytes 110600 | tf_op jit(solution)/shard_map/ppermute | solution.py:334
  19.8 7.5 %collective-permute-start.31 = (bf16[12,16,96]{2,1,0:T(8,128)(2,1)S(1)}, bf16[12,16,96]{2,1,0:T(8,128)(2,1)S(1)}, u32[]{:S(2)}, u32[]{:S(2)}) collective-permute-start(bf16[12,16,96]{2,1,0:T(8,128)(2,1)S(1)} %get-tuple-element.75), channel_id=1, source_target_pairs={{0,192},{64,0},{128,64},{192,128},{1,193},{65,1},{129,65},{193,129... | collective-permute-start | bytes 110600 | tf_op jit(solution)/shard_map/ppermute | solution.py:334
  22.1 5.2 %collective-permute-start.32 = (bf16[12,16,96]{2,1,0:T(8,128)(2,1)S(1)}, bf16[12,16,96]{2,1,0:T(8,128)(2,1)S(1)}, u32[]{:S(2)}, u32[]{:S(2)}) collective-permute-start(bf16[12,16,96]{2,1,0:T(8,128)(2,1)S(1)} %get-tuple-element.76), channel_id=1, source_target_pairs={{0,56},{8,0},{16,8},{24,16},{32,24},{40,32},{48,40},{56,48},{1,57}... | collective-permute-start | bytes 110600 | tf_op jit(solution)/shard_map/ppermute | solution.py:334
  24.5 2.9 %collective-permute-start.33 = (bf16[12,16,96]{2,1,0:T(8,128)(2,1)S(1)}, bf16[12,16,96]{2,1,0:T(8,128)(2,1)S(1)}, u32[]{:S(2)}, u32[]{:S(2)}) collective-permute-start(bf16[12,16,96]{2,1,0:T(8,128)(2,1)S(1)} %get-tuple-element.77), channel_id=1, source_target_pairs={{0,7},{1,0},{2,1},{3,2},{4,3},{5,4},{6,5},{7,6},{8,15},{9,8},{10,9... | collective-permute-start | bytes 110600 | tf_op jit(solution)/shard_map/ppermute | solution.py:334
  24.8 3.2 %collective-permute-start.34 = (bf16[12,16,96]{2,1,0:T(8,128)(2,1)S(1)}, bf16[12,16,96]{2,1,0:T(8,128)(2,1)S(1)}, u32[]{:S(2)}, u32[]{:S(2)}) collective-permute-start(bf16[12,16,96]{2,1,0:T(8,128)(2,1)S(1)} %get-tuple-element.78), channel_id=1, source_target_pairs={{0,8},{8,16},{16,24},{24,32},{32,40},{40,48},{48,56},{56,0},{1,9},... | collective-permute-start | bytes 110600 | tf_op jit(solution)/shard_map/ppermute | solution.py:334
  24.8 4.2 %collective-permute-start.35 = (bf16[12,16,96]{2,1,0:T(8,128)(2,1)S(1)}, bf16[12,16,96]{2,1,0:T(8,128)(2,1)S(1)}, u32[]{:S(2)}, u32[]{:S(2)}) collective-permute-start(bf16[12,16,96]{2,1,0:T(8,128)(2,1)S(1)} %get-tuple-element.79), channel_id=1, source_target_pairs={{0,1},{1,2},{2,3},{3,4},{4,5},{5,6},{6,7},{7,0},{8,9},{9,10},{10,1... | collective-permute-start | bytes 110600 | tf_op jit(solution)/shard_map/ppermute | solution.py:334
  29.4 6.4 %collective-permute-start.36 = (bf16[12,16,96]{2,1,0:T(8,128)(2,1)S(1)}, bf16[12,16,96]{2,1,0:T(8,128)(2,1)S(1)}, u32[]{:S(2)}, u32[]{:S(2)}) collective-permute-start(bf16[12,16,96]{2,1,0:T(8,128)(2,1)S(1)} %get-tuple-element.83), channel_id=1, source_target_pairs={{0,64},{64,128},{128,192},{192,0},{1,65},{65,129},{129,193},{193,1... | collective-permute-start | bytes 110600 | tf_op jit(solution)/shard_map/ppermute | solution.py:334
  29.5 9.0 %collective-permute-start.37 = (bf16[12,16,96]{2,1,0:T(8,128)(2,1)S(1)}, bf16[12,16,96]{2,1,0:T(8,128)(2,1)S(1)}, u32[]{:S(2)}, u32[]{:S(2)}) collective-permute-start(bf16[12,16,96]{2,1,0:T(8,128)(2,1)S(1)} %get-tuple-element.84), channel_id=1, source_target_pairs={{0,192},{64,0},{128,64},{192,128},{1,193},{65,1},{129,65},{193,129... | collective-permute-start | bytes 110600 | tf_op jit(solution)/shard_map/ppermute | solution.py:334
  32.1 6.3 %collective-permute-start.38 = (bf16[12,16,96]{2,1,0:T(8,128)(2,1)S(1)}, bf16[12,16,96]{2,1,0:T(8,128)(2,1)S(1)}, u32[]{:S(2)}, u32[]{:S(2)}) collective-permute-start(bf16[12,16,96]{2,1,0:T(8,128)(2,1)S(1)} %get-tuple-element.85), channel_id=1, source_target_pairs={{0,56},{8,0},{16,8},{24,16},{32,24},{40,32},{48,40},{56,48},{1,57}... | collective-permute-start | bytes 110600 | tf_op jit(solution)/shard_map/ppermute | solution.py:334
  35.6 2.9 %collective-permute-start.39 = (bf16[12,16,96]{2,1,0:T(8,128)(2,1)S(1)}, bf16[12,16,96]{2,1,0:T(8,128)(2,1)S(1)}, u32[]{:S(2)}, u32[]{:S(2)}) collective-permute-start(bf16[12,16,96]{2,1,0:T(8,128)(2,1)S(1)} %get-tuple-element.86), channel_id=1, source_target_pairs={{0,7},{1,0},{2,1},{3,2},{4,3},{5,4},{6,5},{7,6},{8,15},{9,8},{10,9... | collective-permute-start | bytes 110600 | tf_op jit(solution)/shard_map/ppermute | solution.py:334
  35.8 3.3 %collective-permute-start.40 = (bf16[12,16,96]{2,1,0:T(8,128)(2,1)S(1)}, bf16[12,16,96]{2,1,0:T(8,128)(2,1)S(1)}, u32[]{:S(2)}, u32[]{:S(2)}) collective-permute-start(bf16[12,16,96]{2,1,0:T(8,128)(2,1)S(1)} %get-tuple-element.87), channel_id=1, source_target_pairs={{0,8},{8,16},{16,24},{24,32},{32,40},{40,48},{48,56},{56,0},{1,9},... | collective-permute-start | bytes 110600 | tf_op jit(solution)/shard_map/ppermute | solution.py:334
  35.8 4.2 %collective-permute-start.41 = (bf16[12,16,96]{2,1,0:T(8,128)(2,1)S(1)}, bf16[12,16,96]{2,1,0:T(8,128)(2,1)S(1)}, u32[]{:S(2)}, u32[]{:S(2)}) collective-permute-start(bf16[12,16,96]{2,1,0:T(8,128)(2,1)S(1)} %get-tuple-element.88), channel_id=1, source_target_pairs={{0,1},{1,2},{2,3},{3,4},{4,5},{5,6},{6,7},{7,0},{8,9},{9,10},{10,1... | collective-permute-start | bytes 110600 | tf_op jit(solution)/shard_map/ppermute | solution.py:334
  40.4 6.4 %collective-permute-start.42 = (bf16[12,16,96]{2,1,0:T(8,128)(2,1)S(1)}, bf16[12,16,96]{2,1,0:T(8,128)(2,1)S(1)}, u32[]{:S(2)}, u32[]{:S(2)}) collective-permute-start(bf16[12,16,96]{2,1,0:T(8,128)(2,1)S(1)} %get-tuple-element.92), channel_id=1, source_target_pairs={{0,64},{64,128},{128,192},{192,0},{1,65},{65,129},{129,193},{193,1... | collective-permute-start | bytes 110600 | tf_op jit(solution)/shard_map/ppermute | solution.py:334
  40.5 9.2 %collective-permute-start.43 = (bf16[12,16,96]{2,1,0:T(8,128)(2,1)S(1)}, bf16[12,16,96]{2,1,0:T(8,128)(2,1)S(1)}, u32[]{:S(2)}, u32[]{:S(2)}) collective-permute-start(bf16[12,16,96]{2,1,0:T(8,128)(2,1)S(1)} %get-tuple-element.93), channel_id=1, source_target_pairs={{0,192},{64,0},{128,64},{192,128},{1,193},{65,1},{129,65},{193,129... | collective-permute-start | bytes 110600 | tf_op jit(solution)/shard_map/ppermute | solution.py:334
  43.1 6.5 %collective-permute-start.44 = (bf16[12,16,96]{2,1,0:T(8,128)(2,1)S(1)}, bf16[12,16,96]{2,1,0:T(8,128)(2,1)S(1)}, u32[]{:S(2)}, u32[]{:S(2)}) collective-permute-start(bf16[12,16,96]{2,1,0:T(8,128)(2,1)S(1)} %get-tuple-element.94), channel_id=1, source_target_pairs={{0,56},{8,0},{16,8},{24,16},{32,24},{40,32},{48,40},{56,48},{1,57}... | collective-permute-start | bytes 110600 | tf_op jit(solution)/shard_map/ppermute | solution.py:334
  46.8 3.4 %collective-permute-start.46 = (bf16[12,16,96]{2,1,0:T(8,128)(2,1)S(1)}, bf16[12,16,96]{2,1,0:T(8,128)(2,1)S(1)}, u32[]{:S(2)}, u32[]{:S(2)}) collective-permute-start(bf16[12,16,96]{2,1,0:T(8,128)(2,1)S(1)} %get-tuple-element.96), channel_id=1, source_target_pairs={{0,8},{8,16},{16,24},{24,32},{32,40},{40,48},{48,56},{56,0},{1,9},... | collective-permute-start | bytes 110600 | tf_op jit(solution)/shard_map/ppermute | solution.py:334
  46.8 4.2 %collective-permute-start.47 = (bf16[12,16,96]{2,1,0:T(8,128)(2,1)S(1)}, bf16[12,16,96]{2,1,0:T(8,128)(2,1)S(1)}, u32[]{:S(2)}, u32[]{:S(2)}) collective-permute-start(bf16[12,16,96]{2,1,0:T(8,128)(2,1)S(1)} %get-tuple-element.97), channel_id=1, source_target_pairs={{0,1},{1,2},{2,3},{3,4},{4,5},{5,6},{6,7},{7,0},{8,9},{9,10},{10,1... | collective-permute-start | bytes 110600 | tf_op jit(solution)/shard_map/ppermute | solution.py:334
  63.2 12.6 %all-to-all-start.1 = ((f32[32,1,240]{2,1,0:T(1,128)}), f32[32,1,240]{2,1,0:T(1,128)S(1)}, u32[]{:S(2)}, u32[]{:S(2)}) async-start(f32[32,1,240]{2,1,0:T(1,128)} %broadcast_in_dim.5), calls=%async_computation.1 | async-start | bytes 65536 | tf_op jit(solution)/shard_map/all_to_all | solution.py:417
  (2 other events, 5.7 us)
